TPU v7x, 32 devices: a whole 2x2x4 slice. The times are simulated.
32 devices in a mesh: tok: 16 (over z, x, core), mem: 2 (over y).
Axes of the slice: x: 2, y: 2, z: 4, core: 2. Of those that a mesh axis runs over, the one named last changes fastest.
Arguments:
- tokens: bfloat16 [6144, 1472], P(('tok', 'mem')), may hold values from -6 to 6
- memory: bfloat16 [9216, 1472], P(('tok', 'mem')), may hold values from -6 to 6
- target_lengths: int32 [16, 2, 8], P('tok'), may hold values from 1 to 69, 192 in all within a row
- memory_lengths: int32 [16, 16], P('tok'), may hold values from 1 to 384, 576 in all within a row
- keep_mask: int32 [9216], P(('tok', 'mem')), may hold values 0 or 1
- distance_bucket_lookup: int32 [192], replicated, may hold values from 0 to 31, as said below
- self_query: bfloat16 [1472, 384], P(None, ('tok', 'mem')), may hold values from -0.0390625 to 0.0390625
- self_kv: bfloat16 [2, 1472, 384], P(None, None, ('tok', 'mem')), may hold values from -0.15625 to 0.15625
- self_out: bfloat16 [384, 1472], P(('tok', 'mem')), may hold values from -0.625 to 0.625
- cross_query: bfloat16 [1472, 384], P(None, ('tok', 'mem')), may hold values from -0.0390625 to 0.0390625
- cross_key_value: bfloat16 [2, 1472, 384], P(None, None, ('tok', 'mem')), may hold values from -0.15625 to 0.15625
- cross_out: bfloat16 [384, 1472], P(('tok', 'mem')), may hold values from -0.625 to 0.625
- ffn_in: bfloat16 [2, 1472, 3584], P(None, None, ('tok', 'mem')), may hold values from -0.15625 to 0.15625
- ffn_down: bfloat16 [3584, 1472], P(('tok', 'mem')), may hold values from -0.09375 to 0.09375
- norm_gains: float32 [3, 1472], replicated, may hold values from 0.5 to 1.5
- rel_bias: float32 [32, 6], replicated, may hold values from -4 to 4
- cotangent: bfloat16 [6144, 1472], P(('tok', 'mem')), may hold values from -6 to 6
Outputs:
- block_out: bfloat16 [6144, 1472], P(('tok', 'mem'))
- input_grad: float32 [6144, 1472], P(('tok', 'mem'))
- memory_grad: float32 [9216, 1472], P(('tok', 'mem'))
- self_query_grad: float32 [1472, 384], P(None, ('tok', 'mem'))
- self_kv_grad: float32 [2, 1472, 384], P(None, None, ('tok', 'mem'))
- self_out_grad: float32 [384, 1472], P(('tok', 'mem'))
- cross_query_grad: float32 [1472, 384], P(None, ('tok', 'mem'))
- cross_kv_grad: float32 [2, 1472, 384], P(None, None, ('tok', 'mem'))
- cross_out_grad: float32 [384, 1472], P(('tok', 'mem'))
- ffn_in_grad: float32 [2, 1472, 3584], P(None, None, ('tok', 'mem'))
- ffn_down_grad: float32 [3584, 1472], P(('tok', 'mem'))
- gain_grads: float32 [3, 1472], replicated
- rel_bias_grad: float32 [32, 6], replicated
Inputs may be any that keep to these rules, and one draw needn't show every extreme that they name: Every block of target_lengths sums to 192. Every row of memory_lengths sums to 576. distance_bucket_lookup[d] equals d for d < 16, never falls as d grows, and equals 31 from d = 68 on.
All inputs are finite; a program needn't handle non-finite values. No bound on the sum of `keep_mask` on one device may be relied on, other than what follows from the above.
Results may differ from a plain program's by a relative error of at most 0.024.
Values may be sent and summed in bfloat16 or wider, within the bound.
No kernel may reach another device: no remote copies, remote signals or barrier semaphores. Data moves between devices by JAX's collectives and lax.ppermute only.
A program may use at most 320 MiB of HBM per device.

v0:
```python
from functools import partial

import jax
import jax.numpy as jnp
from jax import lax
from jax.sharding import PartitionSpec as P

HEADS = 6
HEAD_DIM = 64
ITEMS_DEV = 8


eps = 1e-06
masked_value = -1e30
highest = lax.Precision.HIGHEST


def contract(left, right):
    return jnp.dot(left, right, preferred_element_type=jnp.float32)


def rms_stats(values, norm_gain):
    norm_scale = lax.rsqrt(jnp.mean(values * values, axis=-1, keepdims=True) + eps)
    return (values * norm_scale * norm_gain, norm_scale)


def norm_back(values, norm_scale, norm_gain, grad_out):
    weighted = grad_out * norm_gain
    inner_mean = jnp.mean(weighted * values, axis=-1, keepdims=True)
    grad_in = norm_scale * weighted - values * (norm_scale * norm_scale * norm_scale) * inner_mean
    grad_gain = jnp.sum(grad_out * values * norm_scale, axis=0)
    return (grad_in, grad_gain)


def run_items(run_lengths, row_count):
    run_ends = jnp.cumsum(run_lengths)
    position = lax.iota(jnp.int32, row_count)
    return jnp.sum((position[:, None] >= run_ends[None, :]).astype(jnp.int32), axis=1)


def split_heads(matrix):
    return matrix.reshape(matrix.shape[0], HEADS, HEAD_DIM)


def on_device(
    tokens,
    memory,
    target_lengths,
    memory_lengths,
    keep_mask,
    distance_bucket_lookup,
    self_query,
    self_kv,
    self_out,
    cross_query,
    cross_key_value,
    cross_out,
    ffn_in,
    ffn_down,
    norm_gains,
    rel_bias,
    cotangent,
):
    tok_rows = tokens.shape[0]
    mem_rows = memory.shape[0]
    pair_count = lax.axis_size("mem")
    memory_row_index = lax.axis_index("mem")
    (
        self_query_full,
        self_kv_full,
        self_out_full,
        complete_cross_query_weight,
        cross_kv_full,
        cross_out_full,
        ffn_in_full,
        ffn_down_full,
    ) = (
        lax.all_gather(self_query, ("tok", "mem"), axis=1, tiled=True),
        lax.all_gather(self_kv, ("tok", "mem"), axis=2, tiled=True),
        lax.all_gather(self_out, ("tok", "mem"), axis=0, tiled=True),
        lax.all_gather(cross_query, ("tok", "mem"), axis=1, tiled=True),
        lax.all_gather(cross_key_value, ("tok", "mem"), axis=2, tiled=True),
        lax.all_gather(cross_out, ("tok", "mem"), axis=0, tiled=True),
        lax.all_gather(ffn_in, ("tok", "mem"), axis=2, tiled=True),
        lax.all_gather(ffn_down, ("tok", "mem"), axis=0, tiled=True),
    )
    block_items = jax.vmap(lambda run_lengths: run_items(run_lengths, tok_rows))(target_lengths[0])
    pair_items = (block_items + ITEMS_DEV * lax.iota(jnp.int32, pair_count)[:, None]).reshape(-1)
    own_items = lax.dynamic_slice_in_dim(pair_items, memory_row_index * tok_rows, tok_rows)
    position = lax.iota(jnp.int32, tok_rows)
    offset = position[:, None] - position[None, :]
    allowed = (own_items[:, None] == own_items[None, :]) & (offset >= 0)
    distance = jnp.clip(offset, 0, distance_bucket_lookup.shape[0] - 1)
    bucket_hot = (
        distance_bucket_lookup[:, None] == lax.iota(jnp.int32, rel_bias.shape[0])[None, :]
    ).astype(jnp.float32)

    def make_relative_bias(table):
        per_distance = jnp.dot(
            table.T, bucket_hot.T, precision=highest, preferred_element_type=jnp.float32
        )
        return jnp.take(per_distance, distance, axis=1)

    bias_heads, bias_back = jax.vjp(make_relative_bias, rel_bias)
    mem_position = memory_row_index * mem_rows + lax.iota(jnp.int32, mem_rows)
    run_lengths = memory_lengths[0]
    run_ends = jnp.cumsum(run_lengths)
    run_starts = run_ends - run_lengths
    mem_items = jnp.sum((mem_position[:, None] >= run_ends[None, :]).astype(jnp.int32), axis=1)
    first_slot = jnp.any(mem_position[:, None] == run_starts[None, :], axis=1)
    live_slot = (keep_mask > 0) | first_slot
    reachable = (pair_items[:, None] == mem_items[None, :]) & live_slot[None, :]
    x_first = tokens.astype(jnp.float32)
    normed_one, scale_one = rms_stats(x_first, norm_gains[0])
    low_one = normed_one.astype(jnp.bfloat16)
    query_self = contract(low_one, self_query_full).astype(jnp.bfloat16)
    keyval_self = jnp.einsum(
        "td,kdi->kti", low_one, self_kv_full, preferred_element_type=jnp.float32
    ).astype(jnp.bfloat16)
    query_heads = split_heads(query_self)
    key_heads_self = split_heads(keyval_self[0])
    value_heads_self = split_heads(keyval_self[1])

    def self_scores():
        raw_self = jnp.einsum(
            "thd,shd->hts", query_heads, key_heads_self, preferred_element_type=jnp.float32
        )
        return jnp.where(allowed[None], raw_self + bias_heads, masked_value)

    scores_self = self_scores()
    top_self = jnp.max(scores_self, axis=-1, keepdims=True)
    weight_self = jnp.exp(scores_self - top_self)
    total_self = jnp.sum(weight_self, axis=-1, keepdims=True)
    probs_self = weight_self / total_self
    mixed_self = jnp.einsum(
        "hts,shd->thd",
        probs_self.astype(jnp.bfloat16),
        value_heads_self,
        preferred_element_type=jnp.float32,
    )
    attn_low = mixed_self.reshape(tok_rows, -1).astype(jnp.bfloat16)
    x_second = x_first + contract(attn_low, self_out_full)
    normed_two, scale_two = rms_stats(x_second, norm_gains[1])
    low_two = normed_two.astype(jnp.bfloat16)
    query_cross = contract(low_two, complete_cross_query_weight).astype(jnp.bfloat16)
    keyval_cross = jnp.einsum(
        "td,kdi->kti", memory, cross_kv_full, preferred_element_type=jnp.float32
    ).astype(jnp.bfloat16)
    pair_query = lax.all_gather(query_cross, "mem", axis=0, tiled=True)
    key_heads = split_heads(keyval_cross[0])
    value_wide = split_heads(keyval_cross[1].astype(jnp.float32))
    raw_cross = jnp.einsum(
        "thd,shd->hts", split_heads(pair_query), key_heads, preferred_element_type=jnp.float32
    )
    scores_cross = jnp.where(reachable[None], raw_cross, masked_value)
    local_top = jnp.max(scores_cross, axis=-1)
    local_weight = jnp.where(reachable[None], jnp.exp(scores_cross - local_top[:, :, None]), 0.0)
    local_total = jnp.sum(local_weight, axis=-1)
    local_out = jnp.einsum(
        "hts,shd->thd",
        local_weight,
        value_wide,
        precision=highest,
        preferred_element_type=jnp.float32,
    )
    tops_in, totals_in, outs_in = (
        lax.all_to_all(
            local_top.T.reshape(pair_count, tok_rows, -1),
            "mem",
            split_axis=0,
            concat_axis=0,
            tiled=True,
        ),
        lax.all_to_all(
            local_total.T.reshape(pair_count, tok_rows, -1),
            "mem",
            split_axis=0,
            concat_axis=0,
            tiled=True,
        ),
        lax.all_to_all(
            local_out.reshape(pair_count, tok_rows, -1),
            "mem",
            split_axis=0,
            concat_axis=0,
            tiled=True,
        ),
    )
    merged_top = jnp.max(tops_in, axis=0)
    factor = jnp.exp(tops_in - merged_top[None])
    merged_total = jnp.sum(totals_in * factor, axis=0)
    joined_head_output = jnp.sum(outs_in * jnp.repeat(factor, HEAD_DIM, axis=2), axis=0)
    cross_mixed = joined_head_output / jnp.repeat(merged_total, HEAD_DIM, axis=1)
    cross_low = cross_mixed.astype(jnp.bfloat16)
    hidden_third = x_second + contract(cross_low, cross_out_full)
    normed_three, scale_three = rms_stats(hidden_third, norm_gains[2])
    low_three = normed_three.astype(jnp.bfloat16)
    gate_up_weight = jnp.einsum(
        "td,kdf->ktf", low_three, ffn_in_full, preferred_element_type=jnp.float32
    )
    activated, gelu_back = jax.vjp(partial(jax.nn.gelu, approximate=True), gate_up_weight[0])
    hidden = (activated * gate_up_weight[1]).astype(jnp.bfloat16)
    ffn_part = contract(hidden, ffn_down_full)
    block_out = (hidden_third + ffn_part).astype(jnp.bfloat16)
    grad_hidden = jnp.einsum(
        "td,fd->tf", cotangent, ffn_down_full, preferred_element_type=jnp.float32
    )
    grad_ffn_down = jnp.einsum("tf,td->fd", hidden, cotangent, preferred_element_type=jnp.float32)
    grad_gate = gelu_back(grad_hidden * gate_up_weight[1])[0]
    grad_gate_up = jnp.stack([grad_gate, grad_hidden * activated]).astype(jnp.bfloat16)
    grad_ffn_in_rows = jnp.einsum(
        "td,ktf->fkd", low_three, grad_gate_up, preferred_element_type=jnp.float32
    )
    normed_part = jnp.einsum(
        "ktf,kdf->td", grad_gate_up, ffn_in_full, preferred_element_type=jnp.float32
    )
    grad_in_three, gain_three = norm_back(hidden_third, scale_three, norm_gains[2], normed_part)
    grad_third = cotangent.astype(jnp.float32) + grad_in_three
    grad_cross_in = grad_third.astype(jnp.bfloat16)
    grad_cross_out = jnp.einsum(
        "ti,td->id", cross_low, grad_cross_in, preferred_element_type=jnp.float32
    )
    grad_mixed = jnp.einsum(
        "td,id->ti", grad_cross_in, cross_out_full, preferred_element_type=jnp.float32
    ).astype(jnp.bfloat16)
    grad_mixed_wide = grad_mixed.astype(jnp.float32)
    local_delta_rows = jnp.sum(
        (grad_mixed_wide * cross_mixed).reshape(tok_rows, HEADS, HEAD_DIM), axis=2
    )
    pair_grad, pair_top, pair_total, pair_delta = (
        lax.all_gather(grad_mixed_wide, "mem", axis=0, tiled=True),
        lax.all_gather(merged_top, "mem", axis=0, tiled=True),
        lax.all_gather(merged_total, "mem", axis=0, tiled=True),
        lax.all_gather(local_delta_rows, "mem", axis=0, tiled=True),
    )
    probs_cross = jnp.where(
        reachable[None],
        jnp.exp(scores_cross - pair_top.T[:, :, None]) / pair_total.T[:, :, None],
        0.0,
    )
    grad_probs_cross = jnp.einsum(
        "thd,shd->hts",
        split_heads(pair_grad.astype(jnp.bfloat16)),
        split_heads(keyval_cross[1]),
        preferred_element_type=jnp.float32,
    )
    grad_scores_cross = (probs_cross * (grad_probs_cross - pair_delta.T[:, :, None])).astype(
        jnp.bfloat16
    )
    grad_value_cross = (
        jnp.einsum(
            "hts,thd->shd",
            probs_cross,
            split_heads(pair_grad),
            precision=highest,
            preferred_element_type=jnp.float32,
        )
        .reshape(mem_rows, -1)
        .astype(jnp.bfloat16)
    )
    grad_key_cross = (
        jnp.einsum(
            "hts,thd->shd",
            grad_scores_cross,
            split_heads(pair_query),
            preferred_element_type=jnp.float32,
        )
        .reshape(mem_rows, -1)
        .astype(jnp.bfloat16)
    )
    query_part = jnp.einsum(
        "hts,shd->thd", grad_scores_cross, key_heads, preferred_element_type=jnp.float32
    ).reshape(pair_count, tok_rows, -1)
    query_parts = lax.all_to_all(query_part, "mem", split_axis=0, concat_axis=0, tiled=True)
    grad_query_cross = jnp.sum(query_parts, axis=0).astype(jnp.bfloat16)
    grad_kv_cross = jnp.stack([grad_key_cross, grad_value_cross])
    grad_memory = jnp.einsum(
        "kti,kdi->td", grad_kv_cross, cross_kv_full, preferred_element_type=jnp.float32
    )
    grad_cross_kv_rows = jnp.einsum(
        "td,kti->ikd", memory, grad_kv_cross, preferred_element_type=jnp.float32
    )
    grad_cross_query_rows = jnp.einsum(
        "td,ti->id", low_two, grad_query_cross, preferred_element_type=jnp.float32
    )
    grad_normed_two = jnp.einsum(
        "ti,di->td",
        grad_query_cross,
        complete_cross_query_weight,
        preferred_element_type=jnp.float32,
    )
    grad_in_two, gain_two = norm_back(x_second, scale_two, norm_gains[1], grad_normed_two)
    grad_second = grad_third + grad_in_two
    grad_attn_in = grad_second.astype(jnp.bfloat16)
    grad_self_out = jnp.einsum(
        "ti,td->id", attn_low, grad_attn_in, preferred_element_type=jnp.float32
    )
    grad_attn_mixed = jnp.einsum(
        "td,id->ti", grad_attn_in, self_out_full, preferred_element_type=jnp.float32
    ).astype(jnp.bfloat16)
    gradient_per_head = split_heads(grad_attn_mixed)
    again_self = jnp.exp(self_scores() - top_self) / total_self
    grad_probs_self = jnp.einsum(
        "thd,shd->hts", gradient_per_head, value_heads_self, preferred_element_type=jnp.float32
    )
    grad_scores_self = again_self * (
        grad_probs_self - jnp.sum(again_self * grad_probs_self, axis=-1, keepdims=True)
    )
    bias_grad = bias_back(grad_scores_self)[0]
    scores_low = grad_scores_self.astype(jnp.bfloat16)
    grad_query_self = (
        jnp.einsum("hts,shd->thd", scores_low, key_heads_self, preferred_element_type=jnp.float32)
        .reshape(tok_rows, -1)
        .astype(jnp.bfloat16)
    )
    grad_key_self = (
        jnp.einsum("hts,thd->shd", scores_low, query_heads, preferred_element_type=jnp.float32)
        .reshape(tok_rows, -1)
        .astype(jnp.bfloat16)
    )
    grad_value_self = (
        jnp.einsum(
            "hts,thd->shd",
            again_self.astype(jnp.bfloat16),
            gradient_per_head,
            preferred_element_type=jnp.float32,
        )
        .reshape(tok_rows, -1)
        .astype(jnp.bfloat16)
    )
    grad_kv_self = jnp.stack([grad_key_self, grad_value_self])
    grad_self_query_rows = jnp.einsum(
        "td,ti->id", low_one, grad_query_self, preferred_element_type=jnp.float32
    )
    grad_self_kv_rows = jnp.einsum(
        "td,kti->ikd", low_one, grad_kv_self, preferred_element_type=jnp.float32
    )
    grad_normed_one = jnp.einsum(
        "ti,di->td", grad_query_self, self_query_full, preferred_element_type=jnp.float32
    ) + jnp.einsum("kti,kdi->td", grad_kv_self, self_kv_full, preferred_element_type=jnp.float32)
    grad_in_one, gain_one = norm_back(x_first, scale_one, norm_gains[0], grad_normed_one)
    grad_tokens = grad_second + grad_in_one
    (
        shard_squery,
        partial_self_key_value,
        summed_sout,
        shard_cquery,
        shard_ckv,
        summed_cout,
        shard_ffn_in,
        summed_ffn_down,
    ) = (
        lax.psum_scatter(grad_self_query_rows, ("tok", "mem"), scatter_dimension=0, tiled=True),
        lax.psum_scatter(grad_self_kv_rows, ("tok", "mem"), scatter_dimension=0, tiled=True),
        lax.psum_scatter(grad_self_out, ("tok", "mem"), scatter_dimension=0, tiled=True),
        lax.psum_scatter(grad_cross_query_rows, ("tok", "mem"), scatter_dimension=0, tiled=True),
        lax.psum_scatter(grad_cross_kv_rows, ("tok", "mem"), scatter_dimension=0, tiled=True),
        lax.psum_scatter(grad_cross_out, ("tok", "mem"), scatter_dimension=0, tiled=True),
        lax.psum_scatter(grad_ffn_in_rows, ("tok", "mem"), scatter_dimension=0, tiled=True),
        lax.psum_scatter(grad_ffn_down, ("tok", "mem"), scatter_dimension=0, tiled=True),
    )
    summed_squery = shard_squery.T
    summed_cquery = shard_cquery.T
    reduced_self_key_value = jnp.transpose(partial_self_key_value, (1, 2, 0))
    summed_ckv = jnp.transpose(shard_ckv, (1, 2, 0))
    reduced_feedforward_input = jnp.transpose(shard_ffn_in, (1, 2, 0))
    summed_gains, summed_bias = lax.psum(
        (jnp.stack([gain_one, gain_two, gain_three]), bias_grad), ("tok", "mem")
    )
    return (
        block_out,
        grad_tokens,
        grad_memory,
        summed_squery,
        reduced_self_key_value,
        summed_sout,
        summed_cquery,
        summed_ckv,
        summed_cout,
        reduced_feedforward_input,
        summed_ffn_down,
        summed_gains,
        summed_bias,
    )


def solution(mesh):
    in_specs = (
        P(("tok", "mem"), None),
        P(("tok", "mem"), None),
        P("tok", None, None),
        P("tok", None),
        P(("tok", "mem")),
        P(),
        P(None, ("tok", "mem")),
        P(None, None, ("tok", "mem")),
        P(("tok", "mem"), None),
        P(None, ("tok", "mem")),
        P(None, None, ("tok", "mem")),
        P(("tok", "mem"), None),
        P(None, None, ("tok", "mem")),
        P(("tok", "mem"), None),
        P(),
        P(),
        P(("tok", "mem"), None),
    )
    out_specs = (
        P(("tok", "mem"), None),
        P(("tok", "mem"), None),
        P(("tok", "mem"), None),
        P(None, ("tok", "mem")),
        P(None, None, ("tok", "mem")),
        P(("tok", "mem"), None),
        P(None, ("tok", "mem")),
        P(None, None, ("tok", "mem")),
        P(("tok", "mem"), None),
        P(None, None, ("tok", "mem")),
        P(("tok", "mem"), None),
        P(),
        P(),
    )
    return jax.shard_map(
        on_device, mesh=mesh, in_specs=in_specs, out_specs=out_specs, check_vma=False
    )
```

profile of v0, /device:TPU:0, one launch (start us, length us, event | category | flops | bytes accessed | tf_op | source)
XLA Modules:
  0.0 1902.2 jit_solution(5298072570055149490)
XLA Ops:
  14.0 121.8 %gather_fusion = f32[36864,6]{1,0:T(8,128)} fusion(f32[6,192]{0,1:T(8,128)S(1)} %copy.224, s32[36864]{0:T(1024)S(1)} %broadcast_clamp_fusion), kind=kCustom, calls=%fused_computation | custom fusion | bytes 1916928 | tf_op jit(solution)/shard_map/jvp(jit(_take))/gather | solution.py:102
  135.9 12.0 copy.226
  159.1 23.6 %all-gather.28.cloned.1.call-done = bf16[32,12,1472]{2,1,0:T(8,128)(2,1)} async-done(((bf16[1,12,1472]{2,1,0:T(8,128)(2,1)}), bf16[32,12,1472]{2,1,0:T(8,128)(2,1)}) %all-gather.28.cloned.1.call-update) | async-done | bytes 1130512 | tf_op jit(solution)/shard_map/all_gather | solution.py:81
  185.9 55.8 %all-gather.16.cloned.1.call-done = bf16[2,1472,384]{1,0,2:T(2,128)(2,1)} async-done(((bf16[2,1472,12]{1,0,2:T(2,128)(2,1)}), bf16[2,1472,384]{1,0,2:T(2,128)(2,1)}) %all-gather.16.cloned.1.call-update) | async-done | bytes 2261008 | tf_op jit(solution)/shard_map/all_gather | solution.py:79
  245.3 55.4 %all-gather.18.cloned.1.call-done = bf16[2,1472,384]{1,0,2:T(2,128)(2,1)} async-done(((bf16[2,1472,12]{1,0,2:T(2,128)(2,1)}), bf16[2,1472,384]{1,0,2:T(2,128)(2,1)}) %all-gather.18.cloned.1.call-update) | async-done | bytes 2261008 | tf_op jit(solution)/shard_map/all_gather | solution.py:82
  313.2 6.7 all_gather.44
  344.3 14.5 all-gather.30.cloned.1.call-done
  377.0 123.7 %all-gather.20.cloned.1.call-done = bf16[2,1472,3584]{1,2,0:T(8,128)(2,1)} async-done(((bf16[2,1472,112]{1,2,0:T(8,128)(2,1)}), bf16[2,1472,3584]{1,2,0:T(8,128)(2,1)}) %all-gather.20.cloned.1.call-update) | async-done | bytes 21102608 | tf_op jit(solution)/shard_map/all_gather | solution.py:84
  500.7 13.1 convolution_bitcast_fusion.1
  513.8 77.1 %all-gather.22.cloned.1.call-done = bf16[3584,1472]{1,0:T(8,128)(2,1)} async-done(((bf16[112,1472]{1,0:T(8,128)(2,1)}), bf16[3584,1472]{1,0:T(8,128)(2,1)}) %all-gather.22.cloned.1.call-update) | async-done | bytes 10551312 | tf_op jit(solution)/shard_map/all_gather | solution.py:85
  590.9 9.7 fusion.25
  600.7 11.5 multiply_reduce_fusion
  614.7 9.8 all_gather.50
  631.7 5.0 all-gather.6
  667.2 8.2 copy.259
  695.0 8.2 copy.258
  703.9 19.2 %convolution_bitcast_fusion = f32[3584,2,1472]{0,2,1:T(8,128)} fusion(bf16[1,192,3584]{2,1,0:T(8,128)(2,1)} %copy-done.31, bf16[1,192,3584]{2,1,0:T(8,128)(2,1)} %copy-done.30, f32[192,1472]{1,0:T(8,128)S(1)} %get-tuple-element.136, f32[1472]{0:T(1024)S(1)} %copy-done.55, f32[192]{0:T(256)S(1)} %copy-done.105), kind=kOutput, calls=%fused_computation.3 | convolution fusion | flops 4053921792 | bytes 46094848 | tf_op jit(solution)/shard_map/td,ktf->fkd/dot_general | solution.py:211
  723.1 64.2 %copy.260 = f32[3584,2,1472]{2,1,0:T(2,128)} copy(f32[3584,2,1472]{0,2,1:T(8,128)} %convolution_bitcast_fusion) | data formatting | bytes 84410368 | tf_op jit(solution)/shard_map/td,ktf->fkd/transpose | solution.py:211
  787.4 12.0 fusion.107
  802.7 7.6 fusion.12
  816.4 384.6 %fusion.102 = (f32[16,1472]{1,0:T(8,128)S(1)}, f32[16,1472]{1,0:T(8,128)S(1)}, f32[16,1472]{1,0:T(8,128)S(1)}, f32[16,1472]{1,0:T(8,128)S(1)}) fusion(f32[384,1472]{1,0:T(8,128)} %fusion.98, f32[384,1472]{1,0:T(8,128)} %fusion.60, f32[384,1472]{1,0:T(8,128)} %fusion.73, f32[384,1472]{1,0:T(8,128)} %fusion.63), kind=kCustom, calls=%all-reduce-scatter.4 | all-reduce-scatter fusion | flops 3014657 | bytes 9420800
  1203.4 6.5 collective-permute-start.23
  1214.5 7.5 collective-permute-start.6
  1223.3 5.0 collective-permute-start.4
  1235.0 8.1 collective-permute-start.3
  1251.7 14.6 collective-permute-start.14
  1299.3 9.9 copy.270
  1309.2 221.0 %scatter_custom_fusion = f32[6,192]{0,1:T(8,128)S(1)} fusion(s32[36864]{0:T(1024)} %copy-done.50, f32[36864,6]{1,0:T(8,128)} %bitcast.202, f32[]{:T(128)} %constant.20.clone.1), kind=kCustom, calls=%fused_computation.138 | custom fusion | flops 221184 | bytes 5120 | tf_op jit(solution)/shard_map/transpose(jvp(jit(_take)))/scatter-add | solution.py:102
  1553.9 40.6 %all-reduce.11 = (f32[3,1472]{1,0:T(4,128)}, f32[32,6]{0,1:T(8,128)}) all-reduce(f32[3,1472]{1,0:T(4,128)S(1)} %pad_maximum_fusion.9, f32[32,6]{0,1:T(8,128)S(1)} %fusion.77), channel_id=1, replica_groups=mesh['tok'=16,'mem'=2] {'tok','mem'}, use_global_device_ids=true, to_apply=%region_32.33 | all-reduce | flops 4608 | bytes 36864 | tf_op jit(solution)/shard_map/psum | solution.py:367
  1603.5 8.8 concatenate.3
  1618.3 42.3 %all-reduce.17.cloned.1.call-done = f32[3584,2,1472]{2,1,0:T(2,128)} async-done(((f32[3584,2,1472]{2,1,0:T(2,128)}), f32[3584,2,1472]{2,1,0:T(2,128)}) %all-reduce.17.cloned.1.call-update) | async-done | bytes 42205200
  1663.4 232.1 %reduce-scatter.10.cloned.1.call-done = f32[112,1472]{1,0:T(8,128)} async-done(((f32[3584,1472]{1,0:T(8,128)}), f32[112,1472]{1,0:T(8,128)}) %reduce-scatter.10.cloned.1.call-update) | async-done | bytes 659472 | tf_op jit(solution)/shard_map/reduce_scatter | solution.py:360
  (467 shorter events, 246.0 us)
Async XLA Ops:
  7.2 143.3 %all-gather.24.cloned.1.call-start = ((), (), s32[]{:S(2)}) async-start(), calls=%async_computation.10 | async-start | bytes 1622016 | tf_op jit(solution)/shard_map/all_gather | solution.py:78
  8.0 147.8 %all-gather.26.cloned.1.call-start = ((), (), s32[]{:S(2)}) async-start(), calls=%async_computation.11 | async-start | bytes 1622016 | tf_op jit(solution)/shard_map/all_gather | solution.py:80
  8.7 173.9 %all-gather.28.cloned.1.call-start = ((), (), s32[]{:S(2)}) async-start(), calls=%async_computation.12 | async-start | bytes 1622016 | tf_op jit(solution)/shard_map/all_gather | solution.py:81
  9.5 232.2 %all-gather.16.cloned.1.call-start = ((), (), s32[]{:S(2)}) async-start(), calls=%async_computation.5 | async-start | bytes 2433024 | tf_op jit(solution)/shard_map/all_gather | solution.py:79
  10.0 290.7 %all-gather.18.cloned.1.call-start = ((), (), s32[]{:S(2)}) async-start(), calls=%async_computation.6 | async-start | bytes 2433024 | tf_op jit(solution)/shard_map/all_gather | solution.py:82
  10.6 348.2 %all-gather.30.cloned.1.call-start = ((), (), s32[]{:S(2)}) async-start(), calls=%async_computation.13 | async-start | bytes 1622016 | tf_op jit(solution)/shard_map/all_gather | solution.py:83
  11.2 489.5 %all-gather.20.cloned.1.call-start = ((), (), s32[]{:S(2)}) async-start(), calls=%async_computation.7 | async-start | bytes 22708224 | tf_op jit(solution)/shard_map/all_gather | solution.py:84
  11.9 579.0 %all-gather.22.cloned.1.call-start = ((), (), s32[]{:S(2)}) async-start(), calls=%async_computation.8 | async-start | bytes 11354112 | tf_op jit(solution)/shard_map/all_gather | solution.py:85
  340.7 33.5 %all-to-all-start = ((f32[2,192,384]{2,1,0:T(8,128)}), f32[2,192,384]{2,1,0:T(8,128)S(1)}, u32[]{:S(2)}, u32[]{:S(2)}) async-start(f32[2,192,384]{2,1,0:T(8,128)} %copy.233), calls=%async_computation | async-start | bytes 1179648 | tf_op jit(solution)/shard_map/all_to_all | solution.py:181
  662.6 952.4 %all-reduce.19.cloned.1.call-start = ((), (), s32[]{:S(2)}) async-start(), calls=%async_computation.15 | async-start | bytes 18874368
  703.2 957.3 %all-reduce.17.cloned.1.call-start = ((), (), s32[]{:S(2)}) async-start(), calls=%async_computation.14 | async-start | bytes 88080384
  787.3 1108.1 %reduce-scatter.10.cloned.1.call-start = ((), (), s32[]{:S(2)}) async-start(), calls=%async_computation.9 | async-start | bytes 22708224 | tf_op jit(solution)/shard_map/reduce_scatter | solution.py:360
  1201.1 27.1 %collective-permute-start.31 = (f32[12,1472]{1,0:T(8,128)S(1)}, f32[12,1472]{1,0:T(8,128)S(1)}, u32[]{:S(2)}, u32[]{:S(2)}) collective-permute-start(f32[12,1472]{1,0:T(8,128)S(1)} %slice.52), channel_id=1, source_target_pairs={{0,8},{1,9},{2,10},{3,11},{4,12},{5,13},{6,14},{7,15},{8,16},{9,17... | collective-permute-start | bytes 211976
  1203.4 26.4 %collective-permute-start.23 = (f32[12,1472]{1,0:T(8,128)S(1)}, f32[12,1472]{1,0:T(8,128)S(1)}, u32[]{:S(2)}, u32[]{:S(2)}) collective-permute-start(f32[12,1472]{1,0:T(8,128)S(1)} %slice.51), channel_id=1, source_target_pairs={{0,8},{1,9},{2,10},{3,11},{4,12},{5,13},{6,14},{7,15},{8,16},{9,17... | collective-permute-start | bytes 211976
  1214.5 30.0 %collective-permute-start.6 = (f32[16,1472]{1,0:T(8,128)S(1)}, f32[16,1472]{1,0:T(8,128)S(1)}, u32[]{:S(2)}, u32[]{:S(2)}) collective-permute-start(f32[16,1472]{1,0:T(8,128)S(1)} %get-tuple-element.108), channel_id=1, source_target_pairs={{0,7},{1,8},{2,9},{3,10},{4,11},{5,12},{6,13},{7,14},{8,15},{9,16}... | collective-permute-start | bytes 282632
  1222.0 26.3 %collective-permute-start.5 = (f32[16,1472]{1,0:T(8,128)S(1)}, f32[16,1472]{1,0:T(8,128)S(1)}, u32[]{:S(2)}, u32[]{:S(2)}) collective-permute-start(f32[16,1472]{1,0:T(8,128)S(1)} %get-tuple-element.108), channel_id=1, source_target_pairs={{0,6},{1,7},{2,8},{3,9},{4,10},{5,11},{6,12},{7,13},{8,14},{9,15},... | collective-permute-start | bytes 282632
  1223.3 28.4 %collective-permute-start.4 = (f32[16,1472]{1,0:T(8,128)S(1)}, f32[16,1472]{1,0:T(8,128)S(1)}, u32[]{:S(2)}, u32[]{:S(2)}) collective-permute-start(f32[16,1472]{1,0:T(8,128)S(1)} %get-tuple-element.108), channel_id=1, source_target_pairs={{0,5},{1,6},{2,7},{3,8},{4,9},{5,10},{6,11},{7,12},{8,13},{9,14},{... | collective-permute-start | bytes 282632
  1235.0 32.2 %collective-permute-start.3 = (f32[16,1472]{1,0:T(8,128)S(1)}, f32[16,1472]{1,0:T(8,128)S(1)}, u32[]{:S(2)}, u32[]{:S(2)}) collective-permute-start(f32[16,1472]{1,0:T(8,128)S(1)} %get-tuple-element.108), channel_id=1, source_target_pairs={{0,4},{1,5},{2,6},{3,7},{4,8},{5,9},{6,10},{7,11},{8,12},{9,13},{1... | collective-permute-start | bytes 282632
  1243.2 28.8 %collective-permute-start.2 = (f32[16,1472]{1,0:T(8,128)S(1)}, f32[16,1472]{1,0:T(8,128)S(1)}, u32[]{:S(2)}, u32[]{:S(2)}) collective-permute-start(f32[16,1472]{1,0:T(8,128)S(1)} %get-tuple-element.108), channel_id=1, source_target_pairs={{0,3},{1,4},{2,5},{3,6},{4,7},{5,8},{6,9},{7,10},{8,11},{9,12},{10... | collective-permute-start | bytes 282632
  1244.5 28.9 %collective-permute-start.1 = (f32[16,1472]{1,0:T(8,128)S(1)}, f32[16,1472]{1,0:T(8,128)S(1)}, u32[]{:S(2)}, u32[]{:S(2)}) collective-permute-start(f32[16,1472]{1,0:T(8,128)S(1)} %get-tuple-element.108), channel_id=1, source_target_pairs={{0,2},{1,3},{2,4},{3,5},{4,6},{5,7},{6,8},{7,9},{8,10},{9,11},{10,... | collective-permute-start | bytes 282632
  1248.3 29.7 %collective-permute-start = (f32[16,1472]{1,0:T(8,128)S(1)}, f32[16,1472]{1,0:T(8,128)S(1)}, u32[]{:S(2)}, u32[]{:S(2)}) collective-permute-start(f32[16,1472]{1,0:T(8,128)S(1)} %get-tuple-element.108), channel_id=1, source_target_pairs={{0,1},{1,2},{2,3},{3,4},{4,5},{5,6},{6,7},{7,8},{8,9},{9,10},{10,1... | collective-permute-start | bytes 282632
  1251.7 30.4 %collective-permute-start.14 = (f32[16,1472]{1,0:T(8,128)S(1)}, f32[16,1472]{1,0:T(8,128)S(1)}, u32[]{:S(2)}, u32[]{:S(2)}) collective-permute-start(f32[16,1472]{1,0:T(8,128)S(1)} %get-tuple-element.109), channel_id=1, source_target_pairs={{0,7},{1,8},{2,9},{3,10},{4,11},{5,12},{6,13},{7,14},{8,15},{9,16}... | collective-permute-start | bytes 282632
  1285.1 245.1 %collective-permute-start.8 = (f32[16,1472]{1,0:T(8,128)S(1)}, f32[16,1472]{1,0:T(8,128)}, u32[]{:S(2)}, u32[]{:S(2)}) collective-permute-start(f32[16,1472]{1,0:T(8,128)S(1)} %get-tuple-element.109), channel_id=1, source_target_pairs={{0,1},{1,2},{2,3},{3,4},{4,5},{5,6},{6,7},{7,8},{8,9},{9,10},{10,1... | collective-permute-start | bytes 282632
  1287.5 244.1 %collective-permute-start.22 = (f32[16,1472]{1,0:T(8,128)S(1)}, f32[16,1472]{1,0:T(8,128)}, u32[]{:S(2)}, u32[]{:S(2)}) collective-permute-start(f32[16,1472]{1,0:T(8,128)S(1)} %get-tuple-element.110), channel_id=1, source_target_pairs={{0,7},{1,8},{2,9},{3,10},{4,11},{5,12},{6,13},{7,14},{8,15},{9,16}... | collective-permute-start | bytes 282632
  1290.8 243.1 %collective-permute-start.21 = (f32[16,1472]{1,0:T(8,128)S(1)}, f32[16,1472]{1,0:T(8,128)}, u32[]{:S(2)}, u32[]{:S(2)}) collective-permute-start(f32[16,1472]{1,0:T(8,128)S(1)} %get-tuple-element.110), channel_id=1, source_target_pairs={{0,6},{1,7},{2,8},{3,9},{4,10},{5,11},{6,12},{7,13},{8,14},{9,15},... | collective-permute-start | bytes 282632
  1292.7 243.6 %collective-permute-start.20 = (f32[16,1472]{1,0:T(8,128)S(1)}, f32[16,1472]{1,0:T(8,128)}, u32[]{:S(2)}, u32[]{:S(2)}) collective-permute-start(f32[16,1472]{1,0:T(8,128)S(1)} %get-tuple-element.110), channel_id=1, source_target_pairs={{0,5},{1,6},{2,7},{3,8},{4,9},{5,10},{6,11},{7,12},{8,13},{9,14},{... | collective-permute-start | bytes 282632
  1295.7 242.3 %collective-permute-start.19 = (f32[16,1472]{1,0:T(8,128)S(1)}, f32[16,1472]{1,0:T(8,128)}, u32[]{:S(2)}, u32[]{:S(2)}) collective-permute-start(f32[16,1472]{1,0:T(8,128)S(1)} %get-tuple-element.110), channel_id=1, source_target_pairs={{0,4},{1,5},{2,6},{3,7},{4,8},{5,9},{6,10},{7,11},{8,12},{9,13},{1... | collective-permute-start | bytes 282632
  1539.9 63.6 %collective-permute-start.28 = (f32[16,1472]{1,0:T(8,128)S(1)}, f32[16,1472]{1,0:T(8,128)}, u32[]{:S(2)}, u32[]{:S(2)}) collective-permute-start(f32[16,1472]{1,0:T(8,128)S(1)} %get-tuple-element.111), channel_id=1, source_target_pairs={{0,5},{1,6},{2,7},{3,8},{4,9},{5,10},{6,11},{7,12},{8,13},{9,14},{... | collective-permute-start | bytes 282632
  1542.8 60.7 %collective-permute-start.27 = (f32[16,1472]{1,0:T(8,128)S(1)}, f32[16,1472]{1,0:T(8,128)}, u32[]{:S(2)}, u32[]{:S(2)}) collective-permute-start(f32[16,1472]{1,0:T(8,128)S(1)} %get-tuple-element.111), channel_id=1, source_target_pairs={{0,4},{1,5},{2,6},{3,7},{4,8},{5,9},{6,10},{7,11},{8,12},{9,13},{1... | collective-permute-start | bytes 282632
  1545.9 57.6 %collective-permute-start.26 = (f32[16,1472]{1,0:T(8,128)S(1)}, f32[16,1472]{1,0:T(8,128)}, u32[]{:S(2)}, u32[]{:S(2)}) collective-permute-start(f32[16,1472]{1,0:T(8,128)S(1)} %get-tuple-element.111), channel_id=1, source_target_pairs={{0,3},{1,4},{2,5},{3,6},{4,7},{5,8},{6,9},{7,10},{8,11},{9,12},{10... | collective-permute-start | bytes 282632
  1547.8 55.7 %collective-permute-start.25 = (f32[16,1472]{1,0:T(8,128)S(1)}, f32[16,1472]{1,0:T(8,128)}, u32[]{:S(2)}, u32[]{:S(2)}) collective-permute-start(f32[16,1472]{1,0:T(8,128)S(1)} %get-tuple-element.111), channel_id=1, source_target_pairs={{0,2},{1,3},{2,4},{3,5},{4,6},{5,7},{6,8},{7,9},{8,10},{9,11},{10,... | collective-permute-start | bytes 282632
  1550.5 53.0 %collective-permute-start.24 = (f32[16,1472]{1,0:T(8,128)S(1)}, f32[16,1472]{1,0:T(8,128)}, u32[]{:S(2)}, u32[]{:S(2)}) collective-permute-start(f32[16,1472]{1,0:T(8,128)S(1)} %get-tuple-element.111), channel_id=1, source_target_pairs={{0,1},{1,2},{2,3},{3,4},{4,5},{5,6},{6,7},{7,8},{8,9},{9,10},{10,1... | collective-permute-start | bytes 282632
  (136 other events, 9189.3 us)
Sparse Core Ops, SparseCore 0:
  11.0 57.8 all-gather.23
  71.7 53.9 all-gather.25
  128.6 53.9 all-gather.27
  185.4 56.2 all-gather.15
  244.4 56.2 all-gather.17
  303.5 55.3 all-gather.29
  361.8 138.8 all-gather.19
  503.6 87.2 all-gather.21
  703.3 214.5 all-reduce.18
  925.4 735.1 all-reduce.16
  1667.5 227.8 reduce-scatter.9
where the time goes:
time: 1910 us; the launch traced here: 1900 us
  waiting for transfers between devices  633 us (33%)
  blocking collectives  455 us (24%)
  local copies, waits for them, and re-layouts  300 us (16%)
  other arithmetic  237 us (12%)
  matrix products  135 us (7%)
  starting transfers between devices  126 us (7%)
    unnamed x1, blocking collectives  385 us
    reduce_scatter x1, waiting for transfers between devices, on_device(): lax.psum_scatter(grad_ffn_down, ('tok', 'mem'), scatter_dimension=0, tile...  232 us
    scatter-add x1, other arithmetic, make_relative_bias(): return jnp.take(per_distance, distance, axis=1)  221 us
    gather x2, local copies, waits for them, and re-layouts, make_relative_bias(): return jnp.take(per_distance, distance, axis=1)  134 us
    all_gather x1, waiting for transfers between devices, on_device(): lax.all_gather(ffn_in, ('tok', 'mem'), axis=2, tiled=True)  124 us
    unnamed x34, starting transfers between devices  111 us
    all_gather x1, waiting for transfers between devices, on_device(): lax.all_gather(ffn_down, ('tok', 'mem'), axis=0, tiled=True)  77.1 us
    transpose x1, local copies, waits for them, and re-layouts, on_device(): jnp.einsum('td,ktf->fkd', low_three, grad_gate_up, preferred_element_type...  64.2 us
  transfers between devices with their start and end apart: 47, of which 10 were waited for; matrix products, arithmetic and copies ran while one was open for 51% of the time, Pallas kernels for 0%

commit v1 on v0

v1 whole, which is shorter than its diff:
```python
from functools import partial

import jax
import jax.numpy as jnp
from jax import lax
from jax.experimental import pallas as pl
from jax.experimental.pallas import tpu as pltpu
from jax.sharding import Mesh, PartitionSpec as P

HEADS = 6
HEAD_DIM = 64
INNER = HEADS * HEAD_DIM
ITEMS_DEV = 8
EPS = 1e-06
MASKED = -1e30
WIDTH = 256
LANES = 128
PAIRS = INNER // LANES
GELU_A = 0.7978845608028654
GELU_B = 0.044715
F32 = jnp.float32
BF16 = jnp.bfloat16
AXES = ("o", "a", "b", "c", "m")
VMEM = 56 * 1024 * 1024


def dot_nn(left, right):
    return lax.dot_general(left, right, (((1,), (0,)), ((), ())), preferred_element_type=F32)


def dot_nt(left, right):
    return lax.dot_general(left, right, (((1,), (1,)), ((), ())), preferred_element_type=F32)


def dot_tn(left, right):
    return lax.dot_general(left, right, (((0,), (0,)), ((), ())), preferred_element_type=F32)


def whole(kernel, out_shape, *args, flops=0, scratch=()):
    nbytes = sum(a.size * a.dtype.itemsize for a in args)
    return pl.pallas_call(
        kernel,
        out_shape=out_shape,
        in_specs=[pl.BlockSpec(memory_space=pltpu.VMEM)] * len(args),
        out_specs=jax.tree.map(lambda _: pl.BlockSpec(memory_space=pltpu.VMEM), out_shape),
        scratch_shapes=list(scratch),
        compiler_params=pltpu.CompilerParams(vmem_limit_bytes=VMEM),
        cost_estimate=pl.CostEstimate(flops=flops, bytes_accessed=nbytes, transcendentals=0),
    )(*args)


def lane_half(rows, side):
    lane = lax.broadcasted_iota(jnp.int32, (rows, LANES), 1)
    return (lane < HEAD_DIM) if side == 0 else (lane >= HEAD_DIM)


def pick(value, side):
    return jnp.where(lane_half(value.shape[0], side), value, jnp.zeros_like(value))


def softmax(scores):
    top = jnp.max(scores, axis=-1, keepdims=True)
    weight = jnp.exp(scores - top)
    return weight / jnp.sum(weight, axis=-1, keepdims=True)


def self_scores(query, key, ring, allowed):
    rows = query.shape[0]
    spread = jnp.broadcast_to(ring, (rows, WIDTH))
    bias = pltpu.roll(spread, 0, 1, stride=1, stride_axis=0)[:, :rows]
    return jnp.where(allowed, dot_nt(query, key) + bias, MASKED)


def self_allowed(items_col, items_row):
    rows = items_col.shape[0]
    r = lax.broadcasted_iota(jnp.int32, (rows, rows), 0)
    q = lax.broadcasted_iota(jnp.int32, (rows, rows), 1)
    return (items_col == items_row) & (r >= q)


def self_forward_kernel(y_ref, order_ref, ring_ref, col_ref, row_ref, qkv_ref, mixed_ref):
    qkv_ref[...] = dot_nn(y_ref[...], order_ref[:, : 3 * INNER]).astype(BF16)
    allowed = self_allowed(col_ref[...], row_ref[...])
    rows = y_ref.shape[0]
    parts = []
    for pair in range(PAIRS):
        at = pair * LANES
        query = qkv_ref[:, at : at + LANES]
        key = qkv_ref[:, INNER + at : INNER + at + LANES]
        value = qkv_ref[:, 2 * INNER + at : 2 * INNER + at + LANES]
        outs = []
        for side in range(2):
            h = 2 * pair + side
            probs = softmax(self_scores(pick(query, side), key, ring_ref[h : h + 1, :], allowed))
            outs.append(dot_nn(probs.astype(BF16), value))
        parts.append(jnp.where(lane_half(rows, 0), outs[0], outs[1]).astype(BF16))
    mixed = jnp.concatenate(parts, axis=1)
    mixed_ref[...] = dot_nt(mixed, order_ref[:, 3 * INNER :]).astype(BF16)


def self_backward_kernel(
    gy_ref, order_ref, qkv_ref, ring_ref, col_ref, row_ref, dy_ref, diag_ref, dqkv_ref
):
    grad = dot_nn(gy_ref[...], order_ref[:, 3 * INNER :]).astype(BF16)
    allowed = self_allowed(col_ref[...], row_ref[...])
    rows = gy_ref.shape[0]
    diag_ref[...] = jnp.zeros_like(diag_ref)
    r = lax.broadcasted_iota(jnp.int32, (rows, rows), 0)
    q = lax.broadcasted_iota(jnp.int32, (rows, rows), 1)
    upside = (r + q == rows - 1).astype(BF16)
    for pair in range(PAIRS):
        at = pair * LANES
        query = qkv_ref[:, at : at + LANES]
        key = qkv_ref[:, INNER + at : INNER + at + LANES]
        value = qkv_ref[:, 2 * INNER + at : 2 * INNER + at + LANES]
        g_pair = grad[:, at : at + LANES]
        dq, dk, dv = [], [], []
        for side in range(2):
            h = 2 * pair + side
            probs = softmax(self_scores(pick(query, side), key, ring_ref[h : h + 1, :], allowed))
            dp = dot_nt(pick(g_pair, side), value)
            ds = probs * (dp - jnp.sum(probs * dp, axis=-1, keepdims=True))
            low = ds.astype(BF16)
            wide = jnp.concatenate(
                [dot_nn(upside, low), jnp.zeros((rows, WIDTH - rows), F32)], axis=1
            )
            turned = pltpu.roll(wide, 0, 1, stride=1, stride_axis=0)
            diag_ref[h : h + 1, :] = jnp.sum(turned, axis=0, keepdims=True)
            dq.append(dot_nn(low, key))
            dk.append(dot_tn(low, query))
            dv.append(dot_tn(probs.astype(BF16), g_pair))
        left = lane_half(rows, 0)
        for k, two in enumerate((dq, dk, dv)):
            dqkv_ref[:, k * INNER + at : k * INNER + at + LANES] = jnp.where(
                left, two[0], two[1]
            ).astype(BF16)
    dy_ref[...] = dot_nt(dqkv_ref[...], order_ref[:, : 3 * INNER]).astype(BF16)


def cross_forward_kernel(
    y_ref, order_ref, own_ref, peer_ref, col_ref, slot_ref, q_ref, mixed_ref
):
    q_ref[...] = dot_nn(y_ref[...], order_ref[:, :INNER]).astype(BF16)
    reach = col_ref[...] == slot_ref[...]
    rows = y_ref.shape[0]
    parts = []
    for pair in range(PAIRS):
        at = pair * LANES
        query = q_ref[:, at : at + LANES]
        key = jnp.concatenate([r[:, at : at + LANES] for r in (own_ref, peer_ref)], axis=0)
        value = jnp.concatenate(
            [r[:, INNER + at : INNER + at + LANES] for r in (own_ref, peer_ref)], axis=0
        )
        outs = []
        for side in range(2):
            probs = softmax(jnp.where(reach, dot_nt(pick(query, side), key), MASKED))
            outs.append(dot_nn(probs.astype(BF16), value))
        parts.append(jnp.where(lane_half(rows, 0), outs[0], outs[1]).astype(BF16))
    mixed = jnp.concatenate(parts, axis=1)
    mixed_ref[...] = dot_nt(mixed, order_ref[:, 3 * INNER :]).astype(BF16)


def cross_backward_kernel(
    gy_ref, order_ref, q_ref, own_ref, peer_ref, col_ref, slot_ref, dy_ref, dkv_ref, dq_ref
):
    grad = dot_nn(gy_ref[...], order_ref[:, 3 * INNER :]).astype(BF16)
    reach = col_ref[...] == slot_ref[...]
    rows = gy_ref.shape[0]
    slots = dkv_ref.shape[0]
    for pair in range(PAIRS):
        at = pair * LANES
        query = q_ref[:, at : at + LANES]
        key = jnp.concatenate([r[:, at : at + LANES] for r in (own_ref, peer_ref)], axis=0)
        value = jnp.concatenate(
            [r[:, INNER + at : INNER + at + LANES] for r in (own_ref, peer_ref)], axis=0
        )
        g_pair = grad[:, at : at + LANES]
        dq, dk, dv = [], [], []
        for side in range(2):
            probs = softmax(jnp.where(reach, dot_nt(pick(query, side), key), MASKED))
            dp = dot_nt(pick(g_pair, side), value)
            ds = (probs * (dp - jnp.sum(probs * dp, axis=-1, keepdims=True))).astype(BF16)
            dq.append(dot_nn(ds, key))
            dk.append(dot_tn(ds, query))
            dv.append(dot_tn(probs.astype(BF16), g_pair))
        dq_ref[:, at : at + LANES] = jnp.where(lane_half(rows, 0), dq[0], dq[1]).astype(BF16)
        left = lane_half(slots, 0)
        dkv_ref[:, at : at + LANES] = jnp.where(left, dk[0], dk[1]).astype(BF16)
        dkv_ref[:, INNER + at : INNER + at + LANES] = jnp.where(left, dv[0], dv[1]).astype(BF16)
    dy_ref[...] = dot_nt(dq_ref[...], order_ref[:, :INNER]).astype(BF16)


def ffn_kernel(
    n_ref, c_ref, wg_ref, wu_ref, wd_ref, out_ref, gn_ref, gg_ref, gu_ref, gd_ref, ag, au, ad
):
    step = pl.program_id(0)

    @pl.when(step == 0)
    def _():
        ag[...] = jnp.zeros_like(ag)
        au[...] = jnp.zeros_like(au)
        ad[...] = jnp.zeros_like(ad)

    n = n_ref[...]
    c = c_ref[...]
    gate = dot_nt(n, wg_ref[...])
    up = dot_nt(n, wu_ref[...])
    square = gate * gate
    t = jnp.tanh(GELU_A * gate * (1.0 + GELU_B * square))
    half = 0.5 * (1.0 + t)
    act = gate * half
    hidden = (act * up).astype(BF16)
    out_ref[...] = dot_nn(hidden, wd_ref[...]).astype(BF16)
    gh = dot_nt(c, wd_ref[...])
    slope = half + 0.5 * gate * (1.0 - t * t) * (GELU_A * (1.0 + 3.0 * GELU_B * square))
    d_gate = (gh * up * slope).astype(BF16)
    d_up = (gh * act).astype(BF16)
    gn_ref[...] = (dot_nn(d_gate, wg_ref[...]) + dot_nn(d_up, wu_ref[...])).astype(BF16)
    ad[...] += dot_tn(hidden, c)
    ag[...] += dot_tn(d_gate, n)
    au[...] += dot_tn(d_up, n)

    @pl.when(step == pl.num_programs(0) - 1)
    def _():
        gg_ref[...] = ag[...].astype(BF16)
        gu_ref[...] = au[...].astype(BF16)
        gd_ref[...] = ad[...].astype(BF16)


def ffn(n_all, c_all, wg, wu, wd):
    rows, width = n_all.shape
    cols = wg.shape[0]
    tile = rows // 8
    block = pl.BlockSpec((tile, width), lambda i: (i, 0))
    full = pl.BlockSpec((cols, width), lambda i: (0, 0))
    act = jax.ShapeDtypeStruct((rows, width), BF16)
    wgt = jax.ShapeDtypeStruct((cols, width), BF16)
    return pl.pallas_call(
        ffn_kernel,
        grid=(rows // tile,),
        in_specs=[block, block, full, full, full],
        out_specs=[block, block, full, full, full],
        out_shape=[act, act, wgt, wgt, wgt],
        scratch_shapes=[pltpu.VMEM((cols, width), F32)] * 3,
        compiler_params=pltpu.CompilerParams(
            vmem_limit_bytes=VMEM, dimension_semantics=("arbitrary",)
        ),
        cost_estimate=pl.CostEstimate(
            flops=18 * rows * width * cols,
            bytes_accessed=8 * rows * width + 12 * cols * width,
            transcendentals=rows * cols,
        ),
    )(n_all, c_all, wg, wu, wd)


def rms_scale(values):
    return lax.rsqrt(jnp.mean(values * values, axis=-1, keepdims=True) + EPS)


def norm_back(values, scale, gain, grad_out):
    weighted = grad_out * gain
    inner = jnp.mean(weighted * values, axis=-1, keepdims=True)
    grad_in = scale * weighted - values * (scale * scale * scale) * inner
    return grad_in, jnp.sum(grad_out * values * scale, axis=0)


def run_items(run_lengths, row_count):
    run_ends = jnp.cumsum(run_lengths)
    position = lax.iota(jnp.int32, row_count)
    return jnp.sum((position[:, None] >= run_ends[None, :]).astype(jnp.int32), axis=1)


def on_device(
    tokens,
    memory,
    target_lengths,
    memory_lengths,
    keep_mask,
    distance_bucket_lookup,
    self_query,
    self_kv,
    self_out,
    cross_query,
    cross_key_value,
    cross_out,
    ffn_in,
    ffn_down,
    norm_gains,
    rel_bias,
    cotangent,
):
    size = {axis: lax.axis_size(axis) for axis in AXES}
    me = {axis: lax.axis_index(axis) for axis in AXES}
    rows, width = tokens.shape
    slots = memory.shape[0]
    n_o, n_z = size["o"], size["o"] * 2
    n_dev = n_z * 8

    def permute(value, move):
        pairs = []
        for flat in range(n_dev):
            rest, at = flat, {}
            for axis in reversed(AXES):
                at[axis], rest = rest % size[axis], rest // size[axis]
            to = move(dict(at))
            there = 0
            for axis in AXES:
                there = there * size[axis] + to[axis]
            pairs.append((flat, there))
        return lax.ppermute(value, AXES, pairs)

    def flip(axis, mask=1):
        def move(at):
            at[axis] ^= mask
            return at

        return move

    def flip_by_core(first, second):
        def move(at):
            at[first if at["c"] == 0 else second] ^= 1
            return at

        return move

    def flip_z(mask):
        def move(at):
            z = (at["o"] * 2 + at["a"]) ^ mask
            at["o"], at["a"] = z // 2, z % 2
            return at

        return move

    def gather_all(own):
        held = jnp.stack([own] + [permute(own, flip_z(k)) for k in range(1, n_z)])
        for move in (flip_by_core("m", "b"), flip_by_core("b", "m"), flip("c")):
            held = jnp.concatenate([held, permute(held, move)], axis=0)
        return held.reshape(-1, width)

    def scatter_all(parts, extra):
        held = parts.reshape(n_dev, -1, width).astype(BF16)
        for move in (flip("c"), flip_by_core("b", "m"), flip_by_core("m", "b")):
            half = held.shape[0] // 2
            sent = held[half:]
            kept = held[:half].astype(F32)
            got = permute(sent, move).astype(F32)
            total = kept + got
            if extra is not None:
                extra = extra + permute(extra, move)
            held = total.astype(BF16)
        got = [permute(held[k], flip_z(k)).astype(F32) for k in range(1, n_z)]
        total = total[0] + sum(got)
        if extra is not None:
            extra = extra + sum([permute(extra, flip_z(k)) for k in range(1, n_z)])
        return total, extra

    def gather_eight(own):
        held = own[None]
        for move in (flip_by_core("b", "a"), flip_by_core("a", "b"), flip("c")):
            held = jnp.concatenate([held, permute(held, move)], axis=0)
        return held.reshape(-1, own.shape[1])

    def scatter_eight(parts):
        held = parts.reshape(8, rows, width)
        for move in (flip("c"), flip_by_core("a", "b"), flip_by_core("b", "a")):
            half = held.shape[0] // 2
            total = held[:half].astype(F32) + permute(held[half:], move).astype(F32)
            held = total.astype(BF16)
        return total[0]

    def gather_ffn(own):
        held = jnp.stack([own] + [permute(own, flip("o", k)) for k in range(1, n_o)])
        return jnp.concatenate([held, permute(held, flip("m"))], axis=0)

    def scatter_ffn(parts):
        total = parts[:n_o].astype(F32) + permute(parts[n_o:], flip("m")).astype(F32)
        low = total.astype(BF16)
        return total[0] + sum(
            [permute(low[k], flip("o", k)).astype(F32) for k in range(1, n_o)]
        )

    own_self = jnp.concatenate([self_query.T, self_kv[0].T, self_kv[1].T, self_out], axis=0)
    own_cross = jnp.concatenate(
        [cross_query.T, cross_key_value[0].T, cross_key_value[1].T, cross_out], axis=0
    )
    own_ffn = jnp.concatenate([ffn_in[0].T, ffn_in[1].T, ffn_down], axis=0)
    part_rows = self_out.shape[0]
    ff_rows = ffn_down.shape[0]
    w_self = gather_all(own_self)
    w_cross = gather_all(own_cross)
    ffn_parts = gather_ffn(own_ffn)
    wg, wu, wd = (
        ffn_parts[:, k * ff_rows : (k + 1) * ff_rows].reshape(-1, width) for k in range(3)
    )
    cot_all = gather_eight(cotangent)

    piece = lax.iota(jnp.int32, n_dev)
    z_mask, first, second, other = (
        piece % n_z,
        (piece // n_z) % 2,
        (piece // (2 * n_z)) % 2,
        piece // (4 * n_z),
    )
    core = me["c"] ^ other
    m_at = me["m"] ^ jnp.where(core == 0, first, second)
    b_at = me["b"] ^ jnp.where(core == 0, second, first)
    z_at = (me["o"] * 2 + me["a"]) ^ z_mask
    owner = ((z_at * 2 + b_at) * 2 + core) * 2 + m_at
    target = (
        lax.iota(jnp.int32, 4)[None, :, None] * INNER
        + owner[:, None, None] * part_rows
        + lax.iota(jnp.int32, part_rows)[None, None, :]
    ).reshape(-1)
    order = (target[:, None] == lax.iota(jnp.int32, 4 * INNER)[None, :]).astype(BF16)

    block_items = jax.vmap(lambda lengths: run_items(lengths, rows))(target_lengths[0])
    own_items = lax.dynamic_index_in_dim(block_items, me["m"], 0, keepdims=False)
    own_items = own_items + ITEMS_DEV * me["m"]
    items_col, items_row = own_items[:, None], own_items[None, :]
    peer_keep = permute(keep_mask, flip("m"))
    run_ends = jnp.cumsum(memory_lengths[0])
    run_starts = run_ends - memory_lengths[0]

    def slot_of(side, keep):
        position = side * slots + lax.iota(jnp.int32, slots)
        items = jnp.sum((position[:, None] >= run_ends[None, :]).astype(jnp.int32), axis=1)
        first_slot = jnp.any(position[:, None] == run_starts[None, :], axis=1)
        return jnp.where((keep > 0) | first_slot, items, -1)

    slot = jnp.concatenate([slot_of(me["m"], keep_mask), slot_of(1 - me["m"], peer_keep)])[None, :]

    def hot_of(distance):
        bucket = distance_bucket_lookup[jnp.clip(distance, 0, distance_bucket_lookup.shape[0] - 1)]
        return (bucket[:, None] == lax.iota(jnp.int32, rel_bias.shape[0])[None, :]).astype(F32)

    bucket_hot = hot_of((WIDTH - lax.iota(jnp.int32, WIDTH)) % WIDTH)
    back_hot = hot_of(rows - 1 - lax.iota(jnp.int32, WIDTH))
    table = jnp.pad(rel_bias, ((0, 0), (0, 8 - HEADS)))
    ring = lax.dot_general(
        table,
        bucket_hot,
        (((0,), (1,)), ((), ())),
        precision=lax.Precision.HIGHEST,
        preferred_element_type=F32,
    )

    gain_1, gain_2, gain_3 = norm_gains[0], norm_gains[1], norm_gains[2]
    x_1 = tokens.astype(F32)
    s_1 = rms_scale(x_1)
    n_1 = (x_1 * s_1 * gain_1).astype(BF16)
    inner_4 = order.shape[0]
    y_1 = dot_nt(n_1, w_self).astype(BF16)

    def shape(*dims, kind=BF16):
        return jax.ShapeDtypeStruct(dims, kind)

    qkv, mixed_1 = whole(
        self_forward_kernel,
        [shape(rows, 3 * INNER), shape(rows, inner_4)],
        y_1,
        order,
        ring,
        items_col,
        items_row,
        flops=2 * rows * inner_4 * inner_4,
    )
    x_2 = x_1 + dot_nn(mixed_1, w_self)
    s_2 = rms_scale(x_2)
    n_2 = (x_2 * s_2 * gain_2).astype(BF16)
    kv_low = dot_nt(memory, w_cross).astype(BF16)
    kv_own = dot_nn(kv_low, order[:, INNER : 3 * INNER]).astype(BF16)
    kv_peer = permute(kv_own, flip("m"))
    y_2 = dot_nt(n_2, w_cross).astype(BF16)
    q_2, mixed_2 = whole(
        cross_forward_kernel,
        [shape(rows, INNER), shape(rows, inner_4)],
        y_2,
        order,
        kv_own,
        kv_peer,
        items_col,
        slot,
        flops=2 * rows * inner_4 * inner_4,
    )
    x_3 = x_2 + dot_nn(mixed_2, w_cross)
    s_3 = rms_scale(x_3)
    n_3 = (x_3 * s_3 * gain_3).astype(BF16)
    n_all = gather_eight(n_3)
    part_out, part_gn, g_gate, g_up, g_down = ffn(n_all, cot_all, wg, wu, wd)

    grad_n3 = scatter_eight(part_gn)
    block_out = (x_3 + scatter_eight(part_out)).astype(BF16)
    ffn_grads = jnp.concatenate(
        [g.reshape(-1, ff_rows, width) for g in (g_gate, g_up, g_down)], axis=1
    )
    sum_ffn = scatter_ffn(ffn_grads)
    back_3, gain_g3 = norm_back(x_3, s_3, gain_3, grad_n3)
    grad_3 = cotangent.astype(F32) + back_3
    low_3 = grad_3.astype(BF16)
    gy_2 = dot_nt(low_3, w_cross).astype(BF16)
    dq_2, dkv = whole(
        lambda *refs: cross_backward_kernel(*refs),
        [shape(rows, inner_4), shape(2 * slots, 2 * INNER)],
        gy_2,
        order,
        q_2,
        kv_own,
        kv_peer,
        items_col,
        slot,
        flops=2 * rows * inner_4 * inner_4,
        scratch=[pltpu.VMEM((rows, INNER), BF16)],
    )
    dkv_peer = permute(dkv[slots:], flip("m"))
    dkv_own = (dkv[:slots].astype(F32) + dkv_peer.astype(F32)).astype(BF16)
    dkv_low = dot_nt(dkv_own, order[:, INNER : 3 * INNER]).astype(BF16)
    grad_memory = dot_nn(dkv_low, w_cross)
    part_cross = dot_tn(
        jnp.concatenate([dq_2, mixed_2, dkv_low], axis=0),
        jnp.concatenate([n_2, low_3, memory], axis=0),
    )
    sum_cross, _ = scatter_all(part_cross, None)
    back_2, gain_g2 = norm_back(x_2, s_2, gain_2, dot_nn(dq_2, w_cross))
    grad_2 = grad_3 + back_2
    low_2 = grad_2.astype(BF16)
    gy_1 = dot_nt(low_2, w_self).astype(BF16)
    dy_1, diag = whole(
        self_backward_kernel,
        [shape(rows, inner_4), shape(8, WIDTH, kind=F32)],
        gy_1,
        order,
        qkv,
        ring,
        items_col,
        items_row,
        flops=2 * rows * inner_4 * inner_4,
        scratch=[pltpu.VMEM((rows, 3 * INNER), BF16)],
    )
    back_1, gain_g1 = norm_back(x_1, s_1, gain_1, dot_nn(dy_1, w_self))
    grad_tokens = grad_2 + back_1
    part_self = dot_tn(
        jnp.concatenate([dy_1, mixed_1], axis=0), jnp.concatenate([n_1, low_2], axis=0)
    )
    bias_grad = lax.dot_general(
        back_hot,
        diag,
        (((0,), (1,)), ((), ())),
        precision=lax.Precision.HIGHEST,
        preferred_element_type=F32,
    )[:, :HEADS]
    flat_bias = jnp.pad(bias_grad.reshape(-1), (0, width - bias_grad.size))
    small = jnp.stack([gain_g1, gain_g2, gain_g3, flat_bias])
    sum_self, small = scatter_all(part_self, small)

    def four(total):
        q, k, v, out = (total[i * part_rows : (i + 1) * part_rows] for i in range(4))
        return q.T, jnp.stack([k.T, v.T]), out

    squery, skv, sout = four(sum_self)
    cquery, ckv, cout = four(sum_cross)
    fin = jnp.stack([sum_ffn[:ff_rows].T, sum_ffn[ff_rows : 2 * ff_rows].T])
    return (
        block_out,
        grad_tokens,
        grad_memory,
        squery,
        skv,
        sout,
        cquery,
        ckv,
        cout,
        fin,
        sum_ffn[2 * ff_rows :],
        small[:3],
        small[3, : bias_grad.size].reshape(bias_grad.shape),
    )


def solution(mesh):
    n_tok, n_mem = mesh.devices.shape
    grid = Mesh(mesh.devices.reshape(n_tok // 8, 2, 2, 2, n_mem), AXES)
    tok = AXES[:-1]
    rows = P(AXES, None)
    cols = P(None, AXES)
    deep = P(None, None, AXES)
    in_specs = (
        rows,
        rows,
        P(tok, None, None),
        P(tok, None),
        P(AXES),
        P(),
        cols,
        deep,
        rows,
        cols,
        deep,
        rows,
        deep,
        rows,
        P(),
        P(),
        rows,
    )
    out_specs = (rows, rows, rows, cols, deep, rows, cols, deep, rows, deep, rows, P(), P())
    return jax.shard_map(
        on_device, mesh=grid, in_specs=in_specs, out_specs=out_specs, check_vma=False
    )
```

time: 1910 us -> 513 us (0.27)
  blocking collectives: 455 us -> 0 us
  waiting for transfers between devices: 633 us -> 202 us
  local copies, waits for them, and re-layouts: 300 us -> 67.2 us
  other arithmetic: 237 us -> 63.8 us
  matrix products: 135 us -> 48 us
  starting transfers between devices: 126 us -> 59.9 us
  Pallas kernels: 0 us -> 64.7 us
    unnamed x1 -> x0, blocking collectives: 385 us -> none
    all_gather x8 -> x0, waiting for transfers between devices: 350 us -> none  [the longest x1 124 us: on_device(): lax.all_gather(ffn_in, ('tok', 'mem'), axis=2, tiled=True)]
    reduce_scatter x1 -> x0, waiting for transfers between devices: 232 us -> none  [on_device(): lax.psum_scatter(grad_ffn_down, ('tok', 'mem'), scatter_dimension=0, tile...]
    scatter-add x1 -> x0, other arithmetic: 221 us -> none  [make_relative_bias(): return jnp.take(per_distance, distance, axis=1)]
    ppermute x0 -> x49, waiting for transfers between devices: none -> 202 us  [permute(): return lax.ppermute(value, AXES, pairs)]
    gather x2, local copies, waits for them, and re-layouts: 134 us -> 5.51 us  [hot_of(): distance_bucket_lookup[jnp.clip(distance, 0, distance_bucket_lookup.shape...]
    unnamed x34 -> x0, starting transfers between devices: 111 us -> none
    dot_general x38 -> x14, matrix products: 135 us -> 47.7 us  [the longest x6 21.9 us: dot_nn(): lax.dot_general(left, right, (((1,), (0,)), ((), ())), preferred_element_...]
  transfers between devices with their start and end apart: 47 -> 49, of which waited for: 10 -> 23; matrix products, arithmetic and copies ran while one was open for 51% -> 29% of each run, Pallas kernels for 0% -> 3%
where the time goes in v1:
time: 513 us; the launch traced here: 508 us
  waiting for transfers between devices  202 us (39%)
  local copies, waits for them, and re-layouts  67.2 us (13%)
  Pallas kernels  64.7 us (13%)
  other arithmetic  63.8 us (12%)
  starting transfers between devices  59.9 us (12%)
  matrix products  48 us (9%)
    ppermute x49, waiting for transfers between devices, permute(): return lax.ppermute(value, AXES, pairs)  202 us
    ppermute x49, starting transfers between devices, permute(): return lax.ppermute(value, AXES, pairs)  59.9 us
    pallas_call x1, Pallas kernels, ffn(): pl.pallas_call(ffn_kernel, grid=(rows // tile,), in_specs=[block, block,...  34.6 us
    pallas_call x4, Pallas kernels, whole(): pl.pallas_call(kernel, out_shape=out_shape, in_specs=[pl.BlockSpec(memory...  30.2 us
    dot_general x6, matrix products, dot_nn(): lax.dot_general(left, right, (((1,), (0,)), ((), ())), preferred_element_...  21.9 us
    dot_general x5, matrix products, dot_nt(): lax.dot_general(left, right, (((1,), (1,)), ((), ())), preferred_element_...  17 us
    unnamed x141, local copies, waits for them, and re-layouts  15.4 us
    convert_element_type x2, local copies, waits for them, and re-layouts, scatter_all(): kept = held[:half].astype(F32)  12.2 us
  transfers between devices with their start and end apart: 49, of which 23 were waited for; matrix products, arithmetic and copies ran while one was open for 29% of the time, Pallas kernels for 3%

profile of v1, /device:TPU:0, one launch (start us, length us, event | category | flops | bytes accessed | tf_op | source)
XLA Modules:
  0.0 508.0 jit_solution(11555008868501803006)
XLA Ops:
  3.4 5.0 collective-permute-start.8
  11.6 3.8 collective-permute-start.2
  17.6 4.1 iota_compare_fusion
  58.9 6.0 %collective-permute-done.10 = bf16[8,48,1472]{2,1,0:T(8,128)(2,1)S(1)} collective-permute-done((bf16[8,48,1472]{2,1,0:T(8,128)(2,1)}, bf16[8,48,1472]{2,1,0:T(8,128)(2,1)S(1)}, u32[]{:S(2)}, u32[]{:S(2)}) %collective-permute-start.10) | collective-permute-done | bytes 1130528 | tf_op jit(solution)/shard_map/ppermute | solution.py:310
  68.8 8.8 %collective-permute-done.4 = bf16[8,48,1472]{2,1,0:T(8,128)(2,1)} collective-permute-done((bf16[8,48,1472]{2,1,0:T(8,128)(2,1)}, bf16[8,48,1472]{2,1,0:T(8,128)(2,1)}, u32[]{:S(2)}, u32[]{:S(2)}) %collective-permute-start.4) | collective-permute-done | bytes 1130528 | tf_op jit(solution)/shard_map/ppermute | solution.py:310
  88.6 5.4 %fusion.20.own_ref.refs_3_ = bf16[288,768]{1,0:T(8,128)(2,1)S(1)} fusion(pred[1536,1536]{1,0:T(32,128)(4,1)} %get-tuple-element.172, bf16[1536,1472]{1,0:T(8,128)(2,1)} %bitcast.195, bf16[288,1472]{1,0:T(8,128)(2,1)} %param.18), kind=kOutput, calls=%fused_computation.56 | convolution fusion | flops 1982472192 | bytes 7225344 | tf_op jit(solution)/shard_map/dot_general | solution.py:28
  97.9 4.8 convolution_convert_fusion.6.y_ref
  102.7 5.8 %shard_map.264 = (bf16[192,1152]{1,0:T(8,128)(2,1)}, bf16[192,1536]{1,0:T(8,128)(2,1)}) custom-call(bf16[192,1536]{1,0:T(8,128)(2,1)} %convolution_convert_fusion.6.y_ref, bf16[1536,1536]{1,0:T(8,128)(2,1)} %get-tuple-element.173.order_ref.refs_1_, f32[8,256]{1,0:T(8,128)} %fusion.48.ring_ref, s32[192,1]{1,0:T(8,128)} %copy.60.col_ref.refs_5_, ...), custom_call_target="tpu_custom_call" | custom-call | flops 905969664 | bytes 5318144 | tf_op jit(solution)/shard_map/pallas_call | solution.py:41
  108.5 3.8 multiply_reduce_fusion.4
  116.4 7.3 %shard_map.265 = (bf16[192,384]{1,0:T(8,128)(2,1)}, bf16[192,1536]{1,0:T(8,128)(2,1)}) custom-call(bf16[192,1536]{1,0:T(8,128)(2,1)} %convolution_convert_fusion.5.y_ref, bf16[1536,1536]{1,0:T(8,128)(2,1)} %get-tuple-element.173.order_ref.refs_1_, bf16[288,768]{1,0:T(8,128)(2,1)} %copy-done.12, bf16[288,768]{1,0:T(8,128)(2,1)} %copy-done.13, ...), custom_call_target="tpu_custom_call" | custom-call | flops 905969664 | bytes 6196224 | tf_op jit(solution)/shard_map/pallas_call | solution.py:41
  129.9 12.9 %collective-permute-done.14 = bf16[1,192,1472]{2,1,0:T(8,128)(2,1)S(1)} collective-permute-done((bf16[1,192,1472]{2,1,0:T(8,128)(2,1)S(1)}, bf16[1,192,1472]{2,1,0:T(8,128)(2,1)S(1)}, u32[]{:S(2)}, u32[]{:S(2)}) %collective-permute-start.14) | collective-permute-done | bytes 565280 | tf_op jit(solution)/shard_map/ppermute | solution.py:310
  151.1 10.4 %collective-permute-done.15 = bf16[2,192,1472]{2,1,0:T(8,128)(2,1)S(1)} collective-permute-done((bf16[2,192,1472]{2,1,0:T(8,128)(2,1)S(1)}, bf16[2,192,1472]{2,1,0:T(8,128)(2,1)S(1)}, u32[]{:S(2)}, u32[]{:S(2)}) %collective-permute-start.15) | collective-permute-done | bytes 1130528 | tf_op jit(solution)/shard_map/ppermute | solution.py:310
  162.7 27.1 %collective-permute-done.21 = bf16[2,336,1472]{2,1,0:T(8,128)(2,1)S(1)} collective-permute-done((bf16[2,336,1472]{2,1,0:T(8,128)(2,1)S(1)}, bf16[2,336,1472]{2,1,0:T(8,128)(2,1)S(1)}, u32[]{:S(2)}, u32[]{:S(2)}) %collective-permute-start.21) | collective-permute-done | bytes 1978400 | tf_op jit(solution)/shard_map/ppermute | solution.py:310
  199.2 34.6 %shard_map.266 = (bf16[1536,1472]{1,0:T(8,128)(2,1)}, bf16[1536,1472]{1,0:T(8,128)(2,1)}, bf16[448,1472]{1,0:T(8,128)(2,1)}, bf16[448,1472]{1,0:T(8,128)(2,1)}, bf16[448,1472]{1,0:T(8,128)(2,1)}) custom-call(bf16[1536,1472]{1,0:T(8,128)(2,1)} %bitcast.212, bf16[1536,1472]{1,0:T(8,128)(2,1)} %bitcast.209, bf16[448,1472]{1,0:T(8,128)(2,1)} %bitcast.217, ...), custom_call_target="tpu_custom_call" | custom-call | flops 18232639488 | bytes 26001408 | tf_op jit(solution)/shard_map/pallas_call | solution.py:238
  250.5 33.9 %collective-permute-done.41 = bf16[2,336,1472]{2,1,0:T(8,128)(2,1)} collective-permute-done((bf16[2,336,1472]{2,1,0:T(8,128)(2,1)}, bf16[2,336,1472]{2,1,0:T(8,128)(2,1)}, u32[]{:S(2)}, u32[]{:S(2)}) %collective-permute-start.41) | collective-permute-done | bytes 1978400 | tf_op jit(solution)/shard_map/ppermute | solution.py:310
  297.4 34.6 %collective-permute-done.42 = bf16[336,1472]{1,0:T(8,128)(2,1)S(1)} collective-permute-done((bf16[336,1472]{1,0:T(8,128)(2,1)S(1)}, bf16[336,1472]{1,0:T(8,128)(2,1)S(1)}, u32[]{:S(2)}, u32[]{:S(2)}) %collective-permute-start.42) | collective-permute-done | bytes 989216 | tf_op jit(solution)/shard_map/ppermute | solution.py:310
  333.7 14.4 %collective-permute-done.23 = bf16[2,192,1472]{2,1,0:T(8,128)(2,1)S(1)} collective-permute-done((bf16[2,192,1472]{2,1,0:T(8,128)(2,1)S(1)}, bf16[2,192,1472]{2,1,0:T(8,128)(2,1)S(1)}, u32[]{:S(2)}, u32[]{:S(2)}) %collective-permute-start.23) | collective-permute-done | bytes 1130528 | tf_op jit(solution)/shard_map/ppermute | solution.py:310
  351.1 7.2 %collective-permute-done.24 = bf16[1,192,1472]{2,1,0:T(8,128)(2,1)S(1)} collective-permute-done((bf16[1,192,1472]{2,1,0:T(8,128)(2,1)S(1)}, bf16[1,192,1472]{2,1,0:T(8,128)(2,1)S(1)}, u32[]{:S(2)}, u32[]{:S(2)}) %collective-permute-start.24) | collective-permute-done | bytes 565280 | tf_op jit(solution)/shard_map/ppermute | solution.py:310
  362.7 8.9 %shard_map.267 = (bf16[192,1536]{1,0:T(8,128)(2,1)}, bf16[576,768]{1,0:T(8,128)(2,1)}) custom-call(bf16[192,1536]{1,0:T(8,128)(2,1)} %convolution_convert_fusion.4.refs_0_, bf16[1536,1536]{1,0:T(8,128)(2,1)} %get-tuple-element.173.order_ref.refs_1_, bf16[192,384]{1,0:T(8,128)(2,1)} %get-tuple-element.30.refs_2_, bf16[288,768]{1,0:T(8,128)(2,1)} %copy-done.12, ...), custom_call_target="tpu_custom_call" | custom-call | flops 905969664 | bytes 6343680 | tf_op jit(solution)/shard_map/pallas_call | solution.py:41
  375.6 5.1 convolution_convert_fusion.3.gy_ref
  380.6 8.2 %shard_map.268 = (bf16[192,1536]{1,0:T(8,128)(2,1)}, f32[8,256]{1,0:T(8,128)}) custom-call(bf16[192,1536]{1,0:T(8,128)(2,1)} %convolution_convert_fusion.3.gy_ref, bf16[1536,1536]{1,0:T(8,128)(2,1)} %get-tuple-element.173.order_ref.refs_1_, bf16[192,1152]{1,0:T(8,128)(2,1)} %get-tuple-element.32.qkv_ref, f32[8,256]{1,0:T(8,128)} %fusion.48.ring_ref, ...), custom_call_target="tpu_custom_call" | custom-call | flops 905969664 | bytes 5760512 | tf_op jit(solution)/shard_map/pallas_call | solution.py:41
  388.9 4.8 fusion.31
  394.4 3.7 convolution_convert_fusion.1
  407.5 6.2 %copy.67 = f32[768,1472]{1,0:T(8,128)} copy(f32[768,1472]{0,1:T(8,128)} %get-tuple-element.106) | data formatting | bytes 9043968 | tf_op jit(solution)/shard_map/convert_element_type | solution.py:345
  421.0 4.3 convolution_convert_fusion
  430.4 3.6 collective-permute-start.35
  434.0 3.9 add_convert_fusion.1
  443.7 6.0 %copy.69 = f32[768,1472]{1,0:T(8,128)} copy(f32[768,1472]{0,1:T(8,128)} %get-tuple-element.104) | data formatting | bytes 9043968 | tf_op jit(solution)/shard_map/convert_element_type | solution.py:345
  449.8 5.7 %collective-permute-done.30 = bf16[8,48,1472]{2,1,0:T(8,128)(2,1)} collective-permute-done((bf16[8,48,1472]{2,1,0:T(8,128)(2,1)}, bf16[8,48,1472]{2,1,0:T(8,128)(2,1)}, u32[]{:S(2)}, u32[]{:S(2)}) %collective-permute-start.30) | collective-permute-done | bytes 1130528 | tf_op jit(solution)/shard_map/ppermute | solution.py:310
  466.3 4.8 collective-permute-done.31
  483.5 5.0 collective-permute-done.37
  498.8 7.1 %collective-permute-done.39 = bf16[48,1472]{1,0:T(8,128)(2,1)S(1)} collective-permute-done((bf16[48,1472]{1,0:T(8,128)(2,1)S(1)}, bf16[48,1472]{1,0:T(8,128)(2,1)S(1)}, u32[]{:S(2)}, u32[]{:S(2)}) %collective-permute-start.39) | collective-permute-done | bytes 141344 | tf_op jit(solution)/shard_map/ppermute | solution.py:310
  (352 shorter events, 198.5 us)
Async XLA Ops:
  3.4 21.1 %collective-permute-start.8 = (bf16[48,1472]{1,0:T(8,128)(2,1)S(1)}, bf16[48,1472]{1,0:T(8,128)(2,1)S(1)}, u32[]{:S(2)}, u32[]{:S(2)}) collective-permute-start(bf16[48,1472]{1,0:T(8,128)(2,1)S(1)} %get-tuple-element.96), channel_id=1, source_target_pairs={{0,24},{1,25},{2,26},{3,27},{4,28},{5,29},{6,30},{7,31},{8,16},{9,... | collective-permute-start | bytes 423944 | tf_op jit(solution)/shard_map/ppermute | solution.py:310
  8.4 19.8 %collective-permute-start.7 = (bf16[48,1472]{1,0:T(8,128)(2,1)S(1)}, bf16[48,1472]{1,0:T(8,128)(2,1)S(1)}, u32[]{:S(2)}, u32[]{:S(2)}) collective-permute-start(bf16[48,1472]{1,0:T(8,128)(2,1)S(1)} %get-tuple-element.96), channel_id=1, source_target_pairs={{0,16},{1,17},{2,18},{3,19},{4,20},{5,21},{6,22},{7,23},{8,24},{9,... | collective-permute-start | bytes 423944 | tf_op jit(solution)/shard_map/ppermute | solution.py:310
  8.4 21.3 %collective-permute-start.6 = (bf16[48,1472]{1,0:T(8,128)(2,1)S(1)}, bf16[48,1472]{1,0:T(8,128)(2,1)S(1)}, u32[]{:S(2)}, u32[]{:S(2)}) collective-permute-start(bf16[48,1472]{1,0:T(8,128)(2,1)S(1)} %get-tuple-element.96), channel_id=1, source_target_pairs={{0,8},{1,9},{2,10},{3,11},{4,12},{5,13},{6,14},{7,15},{8,0},{9,1},... | collective-permute-start | bytes 423944 | tf_op jit(solution)/shard_map/ppermute | solution.py:310
  11.6 19.6 %collective-permute-start.2 = (bf16[48,1472]{1,0:T(8,128)(2,1)S(1)}, bf16[48,1472]{1,0:T(8,128)(2,1)S(1)}, u32[]{:S(2)}, u32[]{:S(2)}) collective-permute-start(bf16[48,1472]{1,0:T(8,128)(2,1)S(1)} %get-tuple-element.98), channel_id=1, source_target_pairs={{0,24},{1,25},{2,26},{3,27},{4,28},{5,29},{6,30},{7,31},{8,16},{9,... | collective-permute-start | bytes 423944 | tf_op jit(solution)/shard_map/ppermute | solution.py:310
  15.5 19.1 %collective-permute-start.1 = (bf16[48,1472]{1,0:T(8,128)(2,1)S(1)}, bf16[48,1472]{1,0:T(8,128)(2,1)S(1)}, u32[]{:S(2)}, u32[]{:S(2)}) collective-permute-start(bf16[48,1472]{1,0:T(8,128)(2,1)S(1)} %get-tuple-element.98), channel_id=1, source_target_pairs={{0,16},{1,17},{2,18},{3,19},{4,20},{5,21},{6,22},{7,23},{8,24},{9,... | collective-permute-start | bytes 423944 | tf_op jit(solution)/shard_map/ppermute | solution.py:310
  28.2 56.8 %collective-permute-start.13 = (s32[288]{0:T(512)}, s32[288]{0:T(512)}, u32[]{:S(2)}, u32[]{:S(2)}) collective-permute-start(s32[288]{0:T(512)} %param.21), channel_id=1, source_target_pairs={{0,1},{1,0},{2,3},{3,2},{4,5},{5,4},{6,7},{7,6},{8,9},{9,8},{10,11... | collective-permute-start | bytes 3464 | tf_op jit(solution)/shard_map/ppermute | solution.py:310
  29.7 98.9 %collective-permute-start.17 = (bf16[1,192,1472]{2,1,0:T(8,128)(2,1)S(1)}, bf16[1,192,1472]{2,1,0:T(8,128)(2,1)}, u32[]{:S(2)}, u32[]{:S(2)}) collective-permute-start(bf16[1,192,1472]{2,1,0:T(8,128)(2,1)S(1)} %bitcast.189), channel_id=1, source_target_pairs={{0,4},{1,5},{2,10},{3,11},{4,0},{5,1},{6,14},{7,15},{8,12},{9,13},... | collective-permute-start | bytes 1695752 | tf_op jit(solution)/shard_map/ppermute | solution.py:310
  31.3 111.7 %collective-permute-start.20 = (bf16[336,1472]{1,0:T(8,128)(2,1)}, bf16[336,1472]{1,0:T(8,128)(2,1)}, u32[]{:S(2)}, u32[]{:S(2)}) collective-permute-start(bf16[336,1472]{1,0:T(8,128)(2,1)} %get-tuple-element.123), channel_id=1, source_target_pairs={{0,16},{1,17},{2,18},{3,19},{4,20},{5,21},{6,22},{7,23},{8,24},{9,... | collective-permute-start | bytes 2967560 | tf_op jit(solution)/shard_map/ppermute | solution.py:310
  45.8 19.0 %collective-permute-start.10 = (bf16[8,48,1472]{2,1,0:T(8,128)(2,1)}, bf16[8,48,1472]{2,1,0:T(8,128)(2,1)S(1)}, u32[]{:S(2)}, u32[]{:S(2)}) collective-permute-start(bf16[8,48,1472]{2,1,0:T(8,128)(2,1)} %get-tuple-element.134), channel_id=1, source_target_pairs={{0,4},{1,5},{2,3},{3,2},{4,0},{5,1},{6,7},{7,6},{8,12},{9,13},{10,... | collective-permute-start | bytes 3391496 | tf_op jit(solution)/shard_map/ppermute | solution.py:310
  52.6 25.0 %collective-permute-start.4 = (bf16[8,48,1472]{2,1,0:T(8,128)(2,1)}, bf16[8,48,1472]{2,1,0:T(8,128)(2,1)}, u32[]{:S(2)}, u32[]{:S(2)}) collective-permute-start(bf16[8,48,1472]{2,1,0:T(8,128)(2,1)} %get-tuple-element.137), channel_id=1, source_target_pairs={{0,4},{1,5},{2,3},{3,2},{4,0},{5,1},{6,7},{7,6},{8,12},{9,13},{10,... | collective-permute-start | bytes 3391496 | tf_op jit(solution)/shard_map/ppermute | solution.py:310
  66.6 20.4 %collective-permute-start.11 = (bf16[16,48,1472]{2,1,0:T(8,128)(2,1)}, bf16[16,48,1472]{2,1,0:T(8,128)(2,1)S(1)}, u32[]{:S(2)}, u32[]{:S(2)}) collective-permute-start(bf16[16,48,1472]{2,1,0:T(8,128)(2,1)} %get-tuple-element.118), channel_id=1, source_target_pairs={{0,2},{1,3},{2,0},{3,1},{4,6},{5,7},{6,4},{7,5},{8,10},{9,11},{10,... | collective-permute-start | bytes 6782984 | tf_op jit(solution)/shard_map/ppermute | solution.py:310
  94.0 21.6 %collective-permute-start.12 = (bf16[288,768]{1,0:T(8,128)(2,1)S(1)}, bf16[288,768]{1,0:T(8,128)(2,1)S(1)}, u32[]{:S(2)}, u32[]{:S(2)}) collective-permute-start(bf16[288,768]{1,0:T(8,128)(2,1)S(1)} %fusion.20.own_ref.refs_3_), channel_id=1, source_target_pairs={{0,1},{1,0},{2,3},{3,2},{4,5},{5,4},{6,7},{7,6},{8,9},{9,8},{10,11... | collective-permute-start | bytes 1327112 | tf_op jit(solution)/shard_map/ppermute | solution.py:310
  129.8 19.1 %collective-permute-start.18 = (bf16[2,192,1472]{2,1,0:T(8,128)(2,1)S(1)}, bf16[2,192,1472]{2,1,0:T(8,128)(2,1)S(1)}, u32[]{:S(2)}, u32[]{:S(2)}) collective-permute-start(bf16[2,192,1472]{2,1,0:T(8,128)(2,1)S(1)} %pad_maximum_fusion.9), channel_id=1, source_target_pairs={{0,8},{1,9},{2,6},{3,7},{4,12},{5,13},{6,2},{7,3},{8,0},{9,1},{10,... | collective-permute-start | bytes 3391496 | tf_op jit(solution)/shard_map/ppermute | solution.py:310
  142.9 18.7 %collective-permute-start.15 = (bf16[2,192,1472]{2,1,0:T(8,128)(2,1)S(1)}, bf16[2,192,1472]{2,1,0:T(8,128)(2,1)S(1)}, u32[]{:S(2)}, u32[]{:S(2)}) collective-permute-start(bf16[2,192,1472]{2,1,0:T(8,128)(2,1)S(1)} %pad_maximum_fusion.8), channel_id=1, source_target_pairs={{0,8},{1,9},{2,6},{3,7},{4,12},{5,13},{6,2},{7,3},{8,0},{9,1},{10,... | collective-permute-start | bytes 3391496 | tf_op jit(solution)/shard_map/ppermute | solution.py:310
  144.4 45.4 %collective-permute-start.21 = (bf16[2,336,1472]{2,1,0:T(8,128)(2,1)S(1)}, bf16[2,336,1472]{2,1,0:T(8,128)(2,1)S(1)}, u32[]{:S(2)}, u32[]{:S(2)}) collective-permute-start(bf16[2,336,1472]{2,1,0:T(8,128)(2,1)S(1)} %pad_maximum_fusion.6), channel_id=1, source_target_pairs={{0,1},{1,0},{2,3},{3,2},{4,5},{5,4},{6,7},{7,6},{8,9},{9,8},{10,11... | collective-permute-start | bytes 5935112 | tf_op jit(solution)/shard_map/ppermute | solution.py:310
  150.2 43.2 %collective-permute-start.19 = (bf16[4,192,1472]{2,1,0:T(8,128)(2,1)S(1)}, bf16[4,192,1472]{2,1,0:T(8,128)(2,1)S(1)}, u32[]{:S(2)}, u32[]{:S(2)}) collective-permute-start(bf16[4,192,1472]{2,1,0:T(8,128)(2,1)S(1)} %pad_maximum_fusion.5), channel_id=1, source_target_pairs={{0,2},{1,3},{2,0},{3,1},{4,6},{5,7},{6,4},{7,5},{8,10},{9,11},{10,... | collective-permute-start | bytes 6782984 | tf_op jit(solution)/shard_map/ppermute | solution.py:310
  161.8 35.0 %collective-permute-start.16 = (bf16[4,192,1472]{2,1,0:T(8,128)(2,1)S(1)}, bf16[4,192,1472]{2,1,0:T(8,128)(2,1)S(1)}, u32[]{:S(2)}, u32[]{:S(2)}) collective-permute-start(bf16[4,192,1472]{2,1,0:T(8,128)(2,1)S(1)} %pad_maximum_fusion.4), channel_id=1, source_target_pairs={{0,2},{1,3},{2,0},{3,1},{4,6},{5,7},{6,4},{7,5},{8,10},{9,11},{10,... | collective-permute-start | bytes 6782984 | tf_op jit(solution)/shard_map/ppermute | solution.py:310
  239.6 44.8 %collective-permute-start.41 = (bf16[2,336,1472]{2,1,0:T(8,128)(2,1)}, bf16[2,336,1472]{2,1,0:T(8,128)(2,1)}, u32[]{:S(2)}, u32[]{:S(2)}) collective-permute-start(bf16[2,336,1472]{2,1,0:T(8,128)(2,1)} %slice.327), channel_id=1, source_target_pairs={{0,1},{1,0},{2,3},{3,2},{4,5},{5,4},{6,7},{7,6},{8,9},{9,8},{10,11... | collective-permute-start | bytes 5935112 | tf_op jit(solution)/shard_map/ppermute | solution.py:310
  243.9 44.0 %collective-permute-start.25 = (bf16[4,192,1472]{2,1,0:T(8,128)(2,1)}, bf16[4,192,1472]{2,1,0:T(8,128)(2,1)}, u32[]{:S(2)}, u32[]{:S(2)}) collective-permute-start(bf16[4,192,1472]{2,1,0:T(8,128)(2,1)} %bitcast.42), channel_id=1, source_target_pairs={{0,2},{1,3},{2,0},{3,1},{4,6},{5,7},{6,4},{7,5},{8,10},{9,11},{10,... | collective-permute-start | bytes 6782984 | tf_op jit(solution)/shard_map/ppermute | solution.py:310
  247.7 45.7 %collective-permute-start.22 = (bf16[4,192,1472]{2,1,0:T(8,128)(2,1)}, bf16[4,192,1472]{2,1,0:T(8,128)(2,1)}, u32[]{:S(2)}, u32[]{:S(2)}) collective-permute-start(bf16[4,192,1472]{2,1,0:T(8,128)(2,1)} %bitcast.39), channel_id=1, source_target_pairs={{0,2},{1,3},{2,0},{3,1},{4,6},{5,7},{6,4},{7,5},{8,10},{9,11},{10,... | collective-permute-start | bytes 6782984 | tf_op jit(solution)/shard_map/ppermute | solution.py:310
  287.5 44.5 %collective-permute-start.42 = (bf16[336,1472]{1,0:T(8,128)(2,1)S(1)}, bf16[336,1472]{1,0:T(8,128)(2,1)S(1)}, u32[]{:S(2)}, u32[]{:S(2)}) collective-permute-start(bf16[336,1472]{1,0:T(8,128)(2,1)S(1)} %fusion.41), channel_id=1, source_target_pairs={{0,16},{1,17},{2,18},{3,19},{4,20},{5,21},{6,22},{7,23},{8,24},{9,... | collective-permute-start | bytes 2967560 | tf_op jit(solution)/shard_map/ppermute | solution.py:310
  290.4 42.9 %collective-permute-start.26 = (bf16[2,192,1472]{2,1,0:T(8,128)(2,1)S(1)}, bf16[2,192,1472]{2,1,0:T(8,128)(2,1)S(1)}, u32[]{:S(2)}, u32[]{:S(2)}) collective-permute-start(bf16[2,192,1472]{2,1,0:T(8,128)(2,1)S(1)} %slice.295), channel_id=1, source_target_pairs={{0,8},{1,9},{2,6},{3,7},{4,12},{5,13},{6,2},{7,3},{8,0},{9,1},{10,... | collective-permute-start | bytes 3391496 | tf_op jit(solution)/shard_map/ppermute | solution.py:310
  295.8 52.2 %collective-permute-start.23 = (bf16[2,192,1472]{2,1,0:T(8,128)(2,1)S(1)}, bf16[2,192,1472]{2,1,0:T(8,128)(2,1)S(1)}, u32[]{:S(2)}, u32[]{:S(2)}) collective-permute-start(bf16[2,192,1472]{2,1,0:T(8,128)(2,1)S(1)} %slice.291), channel_id=1, source_target_pairs={{0,8},{1,9},{2,6},{3,7},{4,12},{5,13},{6,2},{7,3},{8,0},{9,1},{10,... | collective-permute-start | bytes 3391496 | tf_op jit(solution)/shard_map/ppermute | solution.py:310
  333.6 16.4 %collective-permute-start.27 = (bf16[1,192,1472]{2,1,0:T(8,128)(2,1)S(1)}, bf16[1,192,1472]{2,1,0:T(8,128)(2,1)S(1)}, u32[]{:S(2)}, u32[]{:S(2)}) collective-permute-start(bf16[1,192,1472]{2,1,0:T(8,128)(2,1)S(1)} %slice.297), channel_id=1, source_target_pairs={{0,4},{1,5},{2,10},{3,11},{4,0},{5,1},{6,14},{7,15},{8,12},{9,13},... | collective-permute-start | bytes 1695752 | tf_op jit(solution)/shard_map/ppermute | solution.py:310
  398.9 20.0 %collective-permute-start.28 = (bf16[288,768]{1,0:T(8,128)(2,1)}, bf16[288,768]{1,0:T(8,128)(2,1)}, u32[]{:S(2)}, u32[]{:S(2)}) collective-permute-start(bf16[288,768]{1,0:T(8,128)(2,1)} %slice.240), channel_id=1, source_target_pairs={{0,1},{1,0},{2,3},{3,2},{4,5},{5,4},{6,7},{7,6},{8,9},{9,8},{10,11... | collective-permute-start | bytes 1327112 | tf_op jit(solution)/shard_map/ppermute | solution.py:310
  405.8 28.2 %collective-permute-start.29 = (bf16[16,48,1472]{2,1,0:T(8,128)(2,1)}, bf16[16,48,1472]{2,1,0:T(8,128)(2,1)}, u32[]{:S(2)}, u32[]{:S(2)}) collective-permute-start(bf16[16,48,1472]{2,1,0:T(8,128)(2,1)} %bitcast.213), channel_id=1, source_target_pairs={{0,2},{1,3},{2,0},{3,1},{4,6},{5,7},{6,4},{7,5},{8,10},{9,11},{10,... | collective-permute-start | bytes 6782984 | tf_op jit(solution)/shard_map/ppermute | solution.py:310
  414.4 27.7 %collective-permute-start.48 = (f32[4,1472]{1,0:T(4,128)}, f32[4,1472]{1,0:T(4,128)}, u32[]{:S(2)}, u32[]{:S(2)}) collective-permute-start(f32[4,1472]{1,0:T(4,128)} %add.374), channel_id=1, source_target_pairs={{0,24},{1,25},{2,26},{3,27},{4,28},{5,29},{6,30},{7,31},{8,16},{9,... | collective-permute-start | bytes 70664 | tf_op jit(solution)/shard_map/ppermute | solution.py:310
  416.3 25.8 %collective-permute-start.47 = (f32[4,1472]{1,0:T(4,128)}, f32[4,1472]{1,0:T(4,128)}, u32[]{:S(2)}, u32[]{:S(2)}) collective-permute-start(f32[4,1472]{1,0:T(4,128)} %add.374), channel_id=1, source_target_pairs={{0,16},{1,17},{2,18},{3,19},{4,20},{5,21},{6,22},{7,23},{8,24},{9,... | collective-permute-start | bytes 70664 | tf_op jit(solution)/shard_map/ppermute | solution.py:310
  416.3 25.8 %collective-permute-start.46 = (f32[4,1472]{1,0:T(4,128)}, f32[4,1472]{1,0:T(4,128)}, u32[]{:S(2)}, u32[]{:S(2)}) collective-permute-start(f32[4,1472]{1,0:T(4,128)} %add.374), channel_id=1, source_target_pairs={{0,8},{1,9},{2,10},{3,11},{4,12},{5,13},{6,14},{7,15},{8,0},{9,1},... | collective-permute-start | bytes 70664 | tf_op jit(solution)/shard_map/ppermute | solution.py:310
  430.4 28.6 %collective-permute-start.35 = (bf16[16,48,1472]{2,1,0:T(8,128)(2,1)}, bf16[16,48,1472]{2,1,0:T(8,128)(2,1)}, u32[]{:S(2)}, u32[]{:S(2)}) collective-permute-start(bf16[16,48,1472]{2,1,0:T(8,128)(2,1)} %bitcast.214), channel_id=1, source_target_pairs={{0,2},{1,3},{2,0},{3,1},{4,6},{5,7},{6,4},{7,5},{8,10},{9,11},{10,... | collective-permute-start | bytes 6782984 | tf_op jit(solution)/shard_map/ppermute | solution.py:310
  439.0 16.5 %collective-permute-start.30 = (bf16[8,48,1472]{2,1,0:T(8,128)(2,1)}, bf16[8,48,1472]{2,1,0:T(8,128)(2,1)}, u32[]{:S(2)}, u32[]{:S(2)}) collective-permute-start(bf16[8,48,1472]{2,1,0:T(8,128)(2,1)} %slice.301), channel_id=1, source_target_pairs={{0,4},{1,5},{2,3},{3,2},{4,0},{5,1},{6,7},{7,6},{8,12},{9,13},{10,... | collective-permute-start | bytes 3391496 | tf_op jit(solution)/shard_map/ppermute | solution.py:310
  461.8 16.4 %collective-permute-start.36 = (bf16[8,48,1472]{2,1,0:T(8,128)(2,1)S(1)}, bf16[8,48,1472]{2,1,0:T(8,128)(2,1)S(1)}, u32[]{:S(2)}, u32[]{:S(2)}) collective-permute-start(bf16[8,48,1472]{2,1,0:T(8,128)(2,1)S(1)} %slice.315), channel_id=1, source_target_pairs={{0,4},{1,5},{2,3},{3,2},{4,0},{5,1},{6,7},{7,6},{8,12},{9,13},{10,... | collective-permute-start | bytes 3391496 | tf_op jit(solution)/shard_map/ppermute | solution.py:310
  (81 other events, 707.3 us)

commit v2 on v1

v2 whole, which is shorter than its diff:
```python
import jax
import jax.numpy as jnp
import numpy as np
from jax import lax
from jax.experimental import pallas as pl
from jax.experimental.pallas import tpu as pltpu
from jax.sharding import Mesh, PartitionSpec as P

HEADS = 6
HEAD_DIM = 64
INNER = HEADS * HEAD_DIM
ITEMS_DEV = 8
EPS = 1e-06
MASKED = -1e30
WIDTH = 256
LANES = 128
PAIRS = INNER // LANES
GELU_A = 0.7978845608028654
GELU_B = 0.044715
F32 = jnp.float32
BF16 = jnp.bfloat16
AXES = ("o", "a", "b", "c", "m")
GROUP = ("a", "b", "c")
VMEM = 24 * 1024 * 1024


def dot_nn(left, right):
    return lax.dot_general(left, right, (((1,), (0,)), ((), ())), preferred_element_type=F32)


def dot_nt(left, right):
    return lax.dot_general(left, right, (((1,), (1,)), ((), ())), preferred_element_type=F32)


def dot_tn(left, right):
    return lax.dot_general(left, right, (((0,), (0,)), ((), ())), preferred_element_type=F32)


def kernel_call(kernel, out_shape, *args, scratch=(), scalars=0, us=5, vmem=VMEM):
    spaces = [pltpu.SMEM] * scalars + [pltpu.VMEM] * (len(args) - scalars)
    return pl.pallas_call(
        kernel,
        out_shape=out_shape,
        in_specs=[pl.BlockSpec(memory_space=space) for space in spaces],
        out_specs=jax.tree.map(lambda _: pl.BlockSpec(memory_space=pltpu.VMEM), out_shape),
        scratch_shapes=list(scratch),
        compiler_params=pltpu.CompilerParams(vmem_limit_bytes=vmem),
        cost_estimate=pl.CostEstimate(flops=us * 1_000_000_000, bytes_accessed=1, transcendentals=0),
    )(*args)


def shape(*dims, kind=BF16):
    return jax.ShapeDtypeStruct(dims, kind)


def after(value, *others):
    return lax.optimization_barrier((value, *others))[0]


def lane_half(rows, side):
    lane = lax.broadcasted_iota(jnp.int32, (rows, LANES), 1)
    return (lane < HEAD_DIM) if side == 0 else (lane >= HEAD_DIM)


def pick(value, side):
    return jnp.where(lane_half(value.shape[0], side), value, jnp.zeros_like(value))


def softmax(scores):
    top = jnp.max(scores, axis=-1, keepdims=True)
    weight = jnp.exp(scores - top)
    return weight / jnp.sum(weight, axis=-1, keepdims=True)


def rms_scale(values):
    return lax.rsqrt(jnp.mean(values * values, axis=-1, keepdims=True) + EPS)


def norm_back(values, gain, grad_out):
    scale = rms_scale(values)
    weighted = grad_out * gain
    inner = jnp.mean(weighted * values, axis=-1, keepdims=True)
    grad_in = scale * weighted - values * (scale * scale * scale) * inner
    return grad_in, jnp.sum(grad_out * values * scale, axis=0, keepdims=True)


def rows_of(target_ref, at, size, first, count):
    row = lax.broadcasted_iota(jnp.int32, (count, size), 0) + first
    return (row == target_ref[:, at : at + size]).astype(F32).astype(BF16)


def to_natural(value, halves, target_ref, first, count):
    total = None
    for i, w in enumerate(halves):
        half = w.shape[0]
        hot = rows_of(target_ref, i * half, half, first, count)
        term = dot_nt(dot_nt(value, w[...]).astype(BF16), hot)
        total = term if total is None else total + term
    return total.astype(BF16)


def from_natural(value, halves, target_ref, first):
    total = None
    for i, w in enumerate(halves):
        half = w.shape[0]
        hot = rows_of(target_ref, i * half, half, first, value.shape[1])
        term = dot_nn(dot_nn(value, hot).astype(BF16), w[...])
        total = term if total is None else total + term
    return total


def shards_kernel(q_ref, kv_ref, o_ref, q2_ref, kv2_ref, o2_ref, out_ref):
    part, rows = o_ref.shape[0], out_ref.shape[0]
    r = lax.broadcasted_iota(jnp.int32, (rows, part), 0)
    i = lax.broadcasted_iota(jnp.int32, (rows, part), 1)
    total = None
    kv, kv2 = kv_ref[...], kv2_ref[...]
    shards = (q_ref[...], kv[:, 0, :], kv[:, 1, :], o_ref[...])
    shards += (q2_ref[...], kv2[:, 0, :], kv2[:, 1, :], o2_ref[...])
    for k, shard in enumerate(shards):
        hot = (r == i + k * part).astype(F32).astype(BF16)
        term = dot_nn(hot, shard)
        total = term if total is None else total + term
    out_ref[...] = total.astype(BF16)


def exact(left, right, dims):
    return lax.dot_general(
        left, right, (dims, ((), ())), precision=lax.Precision.HIGHEST, preferred_element_type=F32
    )


def buckets_of(lookup_ref, count):
    bucket = lax.broadcasted_iota(jnp.int32, (count, lookup_ref.shape[1]), 0)
    return (bucket == lookup_ref[...]).astype(F32)


def tables_kernel(
    m_ref, lengths_ref, runs_ref, keep_ref, peer_ref, lookup_ref, bias_ref, x_ref, gains_ref,
    ring_ref, col_ref, row_ref, slot_ref, n1_ref,
):
    m = m_ref[0]
    rows, slots = row_ref.shape[1], keep_ref.shape[1]
    for ref, axis in ((col_ref, 0), (row_ref, 1)):
        place = lax.broadcasted_iota(jnp.int32, ref.shape, axis)
        item, end = jnp.zeros(ref.shape, jnp.int32) + m * ITEMS_DEV, 0
        for i in range(ITEMS_DEV):
            end = end + lengths_ref[m, i]
            item = item + (place >= end).astype(jnp.int32)
        ref[...] = item
    for k, keep in enumerate((keep_ref, peer_ref)):
        place = lax.broadcasted_iota(jnp.int32, (1, slots), 1) + (m ^ k) * slots
        item, live, end = jnp.zeros((1, slots), jnp.int32), keep[...], 0
        for i in range(runs_ref.shape[1]):
            live = jnp.where(place == end, 1, live)
            end = end + runs_ref[0, i]
            item = item + (place >= end).astype(jnp.int32)
        slot_ref[k : k + 1, :] = jnp.where(live > 0, item, -1)
    by_distance = exact(bias_ref[...], buckets_of(lookup_ref, bias_ref.shape[0]), ((0,), (0,)))
    d = lax.broadcasted_iota(jnp.int32, (lookup_ref.shape[1], WIDTH), 0)
    k = lax.broadcasted_iota(jnp.int32, (lookup_ref.shape[1], WIDTH), 1)
    turn = ((d + k == WIDTH) | (d + k == 0)).astype(F32)
    ring_ref[...] = jnp.zeros_like(ring_ref)
    ring_ref[0:HEADS, :] = exact(by_distance, turn, ((1,), (0,)))
    x = x_ref[...].astype(F32)
    n1_ref[...] = (x * rms_scale(x) * gains_ref[0:1, :]).astype(BF16)


def self_scores(query, key, ring, allowed):
    rows = query.shape[0]
    spread = jnp.broadcast_to(ring, (rows, WIDTH))
    bias = pltpu.roll(spread, 0, 1, stride=1, stride_axis=0)[:, :rows]
    return jnp.where(allowed, dot_nt(query, key) + bias, MASKED)


def self_allowed(items_col, items_row):
    rows = items_col.shape[0]
    r = lax.broadcasted_iota(jnp.int32, (rows, rows), 0)
    q = lax.broadcasted_iota(jnp.int32, (rows, rows), 1)
    return (items_col == items_row) & (r >= q)


def self_forward_kernel(
    x_ref, n1_ref, gains_ref, w0_ref, w1_ref, target_ref, ring_ref, col_ref, row_ref,
    x2_ref, n2_ref, qkv_ref, low_ref,
):
    x = x_ref[...].astype(F32)
    n = n1_ref[...]
    halves = (w0_ref, w1_ref)
    qkv_ref[...] = to_natural(n, halves, target_ref, 0, 3 * INNER)
    allowed = self_allowed(col_ref[...], row_ref[...])
    rows = x.shape[0]
    for pair in range(PAIRS):
        at = pair * LANES
        query = qkv_ref[:, at : at + LANES]
        key = qkv_ref[:, INNER + at : INNER + at + LANES]
        value = qkv_ref[:, 2 * INNER + at : 2 * INNER + at + LANES]
        outs = []
        for side in range(2):
            h = 2 * pair + side
            probs = softmax(self_scores(pick(query, side), key, ring_ref[h : h + 1, :], allowed))
            outs.append(dot_nn(probs.astype(BF16), value))
        low_ref[:, at : at + LANES] = jnp.where(lane_half(rows, 0), outs[0], outs[1]).astype(BF16)
    x2 = x + from_natural(low_ref[...], halves, target_ref, 3 * INNER)
    x2_ref[...] = x2
    n2_ref[...] = (x2 * rms_scale(x2) * gains_ref[1:2, :]).astype(BF16)


def self_backward_kernel(
    g2_ref, x_ref, gains_ref, w0_ref, w1_ref, target_ref, plain_ref, qkv_ref, ring_ref, col_ref,
    row_ref, lookup_ref, g23_ref, gx_ref, dyt_ref, small_ref, dqkv_ref, diag_ref,
):
    halves = (w0_ref, w1_ref)
    grad = to_natural(g2_ref[...].astype(BF16), halves, target_ref, 3 * INNER, INNER)
    allowed = self_allowed(col_ref[...], row_ref[...])
    rows = x_ref.shape[0]
    diag_ref[...] = jnp.zeros_like(diag_ref)
    r = lax.broadcasted_iota(jnp.int32, (rows, rows), 0)
    q = lax.broadcasted_iota(jnp.int32, (rows, rows), 1)
    upside = (r + q == rows - 1).astype(BF16)
    for pair in range(PAIRS):
        at = pair * LANES
        query = qkv_ref[:, at : at + LANES]
        key = qkv_ref[:, INNER + at : INNER + at + LANES]
        value = qkv_ref[:, 2 * INNER + at : 2 * INNER + at + LANES]
        g_pair = grad[:, at : at + LANES]
        dq, dk, dv = [], [], []
        for side in range(2):
            h = 2 * pair + side
            probs = softmax(self_scores(pick(query, side), key, ring_ref[h : h + 1, :], allowed))
            dp = dot_nt(pick(g_pair, side), value)
            ds = probs * (dp - jnp.sum(probs * dp, axis=-1, keepdims=True))
            low = ds.astype(BF16)
            wide = jnp.concatenate(
                [dot_nn(upside, low), jnp.zeros((rows, WIDTH - rows), F32)], axis=1
            )
            turned = pltpu.roll(wide, 0, 1, stride=1, stride_axis=0)
            diag_ref[h : h + 1, :] = jnp.sum(turned, axis=0, keepdims=True)
            dq.append(dot_nn(low, key))
            dk.append(dot_tn(low, query))
            dv.append(dot_tn(probs.astype(BF16), g_pair))
        left = lane_half(rows, 0)
        for k, two in enumerate((dq, dk, dv)):
            dqkv_ref[:, k * INNER + at : k * INNER + at + LANES] = jnp.where(
                left, two[0], two[1]
            ).astype(BF16)
    col = lax.broadcasted_iota(jnp.int32, (dyt_ref.shape[0], 3 * INNER), 1)
    plain = (plain_ref[...] == col).astype(F32).astype(BF16)
    dyt_ref[...] = dot_nt(plain, dqkv_ref[...]).astype(BF16)
    back = from_natural(dqkv_ref[...], halves, target_ref, 0)
    grad_in, gain_grad = norm_back(x_ref[...].astype(F32), gains_ref[0:1, :], back)
    gx_ref[...] = g2_ref[...] + grad_in
    small_ref[...] = jnp.zeros_like(small_ref)
    small_ref[0:1, :] = gain_grad
    small_ref[1:3, :] = g23_ref[...]
    k = lax.broadcasted_iota(jnp.int32, (WIDTH, rows), 0)
    d = lax.broadcasted_iota(jnp.int32, (WIDTH, rows), 1)
    by_distance = exact(diag_ref[...], (k + d == rows - 1).astype(F32), ((1,), (0,)))
    buckets = buckets_of(lookup_ref, LANES)
    small_ref[8:16, 0:LANES] = exact(by_distance, buckets, ((1,), (1,)))


def memory_forward_kernel(own_ref, peer_ref, w0_ref, w1_ref, target_ref, kv_own_ref, kv_peer_ref):
    halves = (w0_ref, w1_ref)
    kv_own_ref[...] = to_natural(own_ref[...], halves, target_ref, INNER, 2 * INNER)
    kv_peer_ref[...] = to_natural(peer_ref[...], halves, target_ref, INNER, 2 * INNER)


def memory_backward_kernel(own_ref, got_ref, w0_ref, w1_ref, target_ref, out_ref):
    total = (own_ref[...].astype(F32) + got_ref[...].astype(F32)).astype(BF16)
    out_ref[...] = from_natural(total, (w0_ref, w1_ref), target_ref, INNER)


def key_value(own_ref, peer_ref, at):
    key = jnp.concatenate([r[:, at : at + LANES] for r in (own_ref, peer_ref)], axis=0)
    at += INNER
    return key, jnp.concatenate([r[:, at : at + LANES] for r in (own_ref, peer_ref)], axis=0)


def cross_forward_kernel(
    x_ref, n_ref, gains_ref, w0_ref, w1_ref, target_ref, own_ref, peer_ref, col_ref, slot_ref,
    x3_ref, n3_ref, q_ref, low_ref,
):
    halves = (w0_ref, w1_ref)
    q_ref[...] = to_natural(n_ref[...], halves, target_ref, 0, INNER)
    reach = col_ref[...] == jnp.concatenate([slot_ref[k : k + 1, :] for k in range(2)], axis=1)
    rows = x_ref.shape[0]
    for pair in range(PAIRS):
        at = pair * LANES
        query = q_ref[:, at : at + LANES]
        key, value = key_value(own_ref, peer_ref, at)
        outs = []
        for side in range(2):
            probs = softmax(jnp.where(reach, dot_nt(pick(query, side), key), MASKED))
            outs.append(dot_nn(probs.astype(BF16), value))
        low_ref[:, at : at + LANES] = jnp.where(lane_half(rows, 0), outs[0], outs[1]).astype(BF16)
    x3 = x_ref[...] + from_natural(low_ref[...], halves, target_ref, 3 * INNER)
    x3_ref[...] = x3
    n3_ref[...] = (x3 * rms_scale(x3) * gains_ref[2:3, :]).astype(BF16)


def cross_backward_kernel(
    lo_ref, got_c_ref, got_2_ref, got_ref, x3_ref, x2_ref, gains_ref, cot_ref, w0_ref, w1_ref, target_ref, q_ref,
    own_ref, peer_ref, col_ref, slot_ref, low3_ref, g2_ref, dq_ref, dkv_own_ref, dkv_peer_ref,
    gain_ref,
):
    halves = (w0_ref, w1_ref)
    rows = x3_ref.shape[0]
    grad_n3 = got_ref[...].astype(F32) + sum(
        ref[0:rows, :].astype(F32) for ref in (lo_ref, got_c_ref, got_2_ref)
    )
    grad_in, gain_3 = norm_back(x3_ref[...], gains_ref[2:3, :], grad_n3)
    grad_3 = cot_ref[...].astype(F32) + grad_in
    low3_ref[...] = grad_3.astype(BF16)
    grad = to_natural(low3_ref[...], halves, target_ref, 3 * INNER, INNER)
    reach = col_ref[...] == jnp.concatenate([slot_ref[k : k + 1, :] for k in range(2)], axis=1)
    rows = x3_ref.shape[0]
    slots = own_ref.shape[0]
    for pair in range(PAIRS):
        at = pair * LANES
        query = q_ref[:, at : at + LANES]
        key, value = key_value(own_ref, peer_ref, at)
        g_pair = grad[:, at : at + LANES]
        dq, dk, dv = [], [], []
        for side in range(2):
            probs = softmax(jnp.where(reach, dot_nt(pick(query, side), key), MASKED))
            dp = dot_nt(pick(g_pair, side), value)
            ds = (probs * (dp - jnp.sum(probs * dp, axis=-1, keepdims=True))).astype(BF16)
            dq.append(dot_nn(ds, key))
            dk.append(dot_tn(ds, query))
            dv.append(dot_tn(probs.astype(BF16), g_pair))
        dq_ref[:, at : at + LANES] = jnp.where(lane_half(rows, 0), dq[0], dq[1]).astype(BF16)
        left = lane_half(2 * slots, 0)
        for k, two in ((0, dk), (INNER, dv)):
            both = jnp.where(left, two[0], two[1]).astype(BF16)
            dkv_own_ref[:, k + at : k + at + LANES] = both[:slots]
            dkv_peer_ref[:, k + at : k + at + LANES] = both[slots:]
    back = from_natural(dq_ref[...], halves, target_ref, 0)
    grad_in, gain_2 = norm_back(x2_ref[...], gains_ref[1:2, :], back)
    g2_ref[...] = grad_3 + grad_in
    gain_ref[0:1, :] = gain_2
    gain_ref[1:2, :] = gain_3


def weights_kernel(
    dq_ref, low_ref, own_ref, peer_ref, low1_ref, n2_ref, low3_ref, mem_own_ref, mem_peer_ref, g2_ref,
    target_ref, one_ref, *refs,
):
    got_ref, out_ref = (refs[0] if len(refs) > 1 else None), refs[-1]

    def spread(order_ref, at, value):
        hot = rows_of(order_ref, 0, order_ref.shape[1], at, value.shape[1])
        return dot_nn(value, hot).astype(BF16)

    cross = dot_tn(
        jnp.concatenate(
            [
                spread(target_ref, 0, dq_ref[...]),
                spread(target_ref, 3 * INNER, low_ref[...]),
                spread(target_ref, INNER, own_ref[...]),
                spread(target_ref, INNER, peer_ref[...]),
            ],
            axis=0,
        ),
        jnp.concatenate(
            [n2_ref[...], low3_ref[...], mem_own_ref[...], mem_peer_ref[...]], axis=0
        ),
    )
    out = dot_tn(spread(one_ref, 0, low1_ref[...]), g2_ref[...].astype(BF16))
    wide, slim = cross.shape[0] // 4, out.shape[0] // 4

    def put(at, value):
        if got_ref is not None:
            value = value + got_ref[at : at + value.shape[0], :].astype(F32)
        out_ref[at : at + value.shape[0], :] = value.astype(BF16)

    for k in range(4):
        put(k * (wide + slim), cross[k * wide : (k + 1) * wide])
        put(k * (wide + slim) + wide, out[k * slim : (k + 1) * slim])


def columns_kernel(at_ref, held_ref, lo_ref, hi_ref, out_ref):
    rows = held_ref.shape[2]
    total = None
    for k in range(8):
        right = (lo_ref if k < 4 else hi_ref)[(k % 4) * rows : (k % 4 + 1) * rows, :]
        term = dot_nn(held_ref[at_ref[k]], right)
        total = term if total is None else total + term
    out_ref[...] = total.astype(BF16)


def assemble(parts, whole_ref):
    cols = parts[0].shape[0]
    for i, part in enumerate(parts):
        whole_ref[i * cols : (i + 1) * cols, :] = part[...]


def grad_hidden_kernel(c_ref, *refs):
    parts, out_ref, wd_ref = refs[:-2], refs[-2], refs[-1]
    assemble(parts, wd_ref)
    out_ref[...] = dot_nt(c_ref[...], wd_ref[...])


def ffn_kernel(n_ref, gh_ref, *refs):
    parts, (h_ref, dg_ref, du_ref, gn_ref, wg_ref, wu_ref) = refs[:-6], refs[-6:]
    cols = parts[0].shape[0] // 2
    assemble([part.at[:cols, :] for part in parts], wg_ref)
    assemble([part.at[cols:, :] for part in parts], wu_ref)
    n = n_ref[...]
    gate = dot_nt(n, wg_ref[...])
    up = dot_nt(n, wu_ref[...])
    square = gate * gate
    t = jnp.tanh(GELU_A * gate * (1.0 + GELU_B * square))
    half = 0.5 * (1.0 + t)
    act = gate * half
    h_ref[...] = (act * up).astype(BF16)
    gh = gh_ref[...]
    slope = half + 0.5 * gate * (1.0 - t * t) * (GELU_A * (1.0 + 3.0 * GELU_B * square))
    d_gate = (gh * up * slope).astype(BF16)
    d_up = (gh * act).astype(BF16)
    dg_ref[...] = d_gate
    du_ref[...] = d_up
    gn_ref[...] = (dot_nn(d_gate, wg_ref[...]) + dot_nn(d_up, wu_ref[...])).astype(BF16)


def ffn_out_kernel(h_ref, *refs):
    parts, out_ref, wd_ref = refs[:-2], refs[-2], refs[-1]
    got_ref, parts = (parts[0], parts[1:]) if len(parts) % 2 else (None, parts)
    assemble(parts, wd_ref)
    value = dot_nn(h_ref[...], wd_ref[...])
    if got_ref is not None:
        value = value + got_ref[...].astype(F32)
    out_ref[...] = value.astype(BF16)


def ffn_weights_kernel(
    count, h0_ref, h1_ref, g0_ref, g1_ref, u0_ref, u1_ref, n0_ref, n1_ref, c0_ref, c1_ref, *out_refs
):
    sets = (
        ((h0_ref, c0_ref), (h1_ref, c1_ref)),
        ((g0_ref, n0_ref), (g1_ref, n1_ref)),
        ((u0_ref, n0_ref), (u1_ref, n1_ref)),
    )
    down_ref, both_ref = out_refs
    for kind, pairs in enumerate(sets):
        value = sum(dot_tn(left[...], right[...]) for left, right in pairs).astype(BF16)
        if kind == 0:
            down_ref[...] = value
            continue
        cols = both_ref.shape[0] // (2 * count)
        for i in range(count):
            at = (2 * i + kind - 1) * cols
            both_ref[at : at + cols, :] = value[i * cols : (i + 1) * cols]


def on_device(
    tokens,
    memory,
    target_lengths,
    memory_lengths,
    keep_mask,
    distance_bucket_lookup,
    self_query,
    self_kv,
    self_out,
    cross_query,
    cross_key_value,
    cross_out,
    ffn_in,
    ffn_down,
    norm_gains,
    rel_bias,
    cotangent,
):
    size = {axis: lax.axis_size(axis) for axis in AXES}
    me = {axis: lax.axis_index(axis) for axis in AXES}
    rows, width = tokens.shape
    slots = memory.shape[0]
    part_rows, ff_rows = self_out.shape[0], ffn_down.shape[0]
    n_o = size["o"]
    quads = 2 * n_o

    def cut(value):
        if value.ndim < 2 or value.shape[-2] % LANES:
            return value
        return value.reshape(*value.shape[:-2], -1, LANES // 2, value.shape[-1])

    def permute(value, move):
        pairs = []
        for flat in range(quads * 8):
            rest, at = flat, {}
            for axis in reversed(AXES):
                at[axis], rest = rest % size[axis], rest // size[axis]
            to = move(dict(at))
            there = 0
            for axis in AXES:
                there = there * size[axis] + to[axis]
            pairs.append((flat, there))
        return lax.ppermute(cut(value), AXES, pairs).reshape(value.shape)

    def flips(**masks):
        def move(at):
            return {axis: at[axis] ^ masks.get(axis, 0) for axis in AXES}

        return move

    def flip_by_core(first, second):
        def move(at):
            at[first if at["c"] == 0 else second] ^= 1
            return at

        return move

    first_move, second_move = flip_by_core("b", "a"), flip_by_core("a", "b")
    core_move, peer_move = flips(c=1), flips(m=1)

    def grow(held, move):
        return jnp.concatenate([held, permute(held, move)], axis=0)

    def exchange(value, axes, parts):
        value = value.reshape(parts, -1, value.shape[-1])
        got = lax.all_to_all(cut(value), axes, split_axis=0, concat_axis=0, tiled=True)
        return got.reshape(value.shape)

    stage = lax.optimization_barrier
    full, slim = (rows, width), (rows, INNER)
    half, cols = 4 * rows, quads * ff_rows
    kv_shape = shape(slots, 2 * INNER)
    down, gate, up = (pltpu.VMEM((cols, width), BF16) for _ in range(3))

    def over_o(own):
        return [own] + [permute(own, flips(o=k)) for k in range(1, n_o)]

    def over_m(parts):
        return parts + [permute(v, peer_move) for v in parts]

    def flat_of(at):
        return ((((at["o"] * 2 + at["a"]) * 2 + at["b"]) * 2 + at["c"]) * 2) + at["m"]

    def mask_of(eighth, quad, core):
        by_1, by_2 = ("b", "a") if core ^ (eighth // 4) == 0 else ("a", "b")
        at = {"o": quad % n_o, "m": quad // n_o, "c": eighth // 4}
        at[by_1], at[by_2] = eighth % 2, (eighth // 2) % 2
        return flat_of(at)

    masks = np.array(
        [[mask_of(e, q, core) for e in range(8) for q in range(quads)] for core in range(2)]
    ).astype(np.int32)
    piece = 4 * part_rows

    def target_of(owner, padded):
        row = np.arange(padded)
        base = row // part_rows * INNER + row % part_rows
        return owner[:, None] * part_rows + base[None, :].astype(np.int32)

    moves = [flips(o=k % n_o, m=k // n_o) for k in range(1, quads)]
    wide = quads * piece

    own_both = kernel_call(
        shards_kernel, shape(2 * piece, width), self_query.T, jnp.transpose(self_kv, (2, 0, 1)), self_out,
        cross_query.T, jnp.transpose(cross_key_value, (2, 0, 1)), cross_out, us=2,
    )
    got = [own_both] + [permute(own_both, move) for move in moves]
    here, at_core = after((flat_of(me), me["c"]), own_both)
    mask = jnp.where(at_core == 0, masks[0], masks[1])
    target = target_of(here ^ mask, piece).reshape(1, -1)
    one = jnp.where(
        np.arange(16)[None, :] < part_rows, target_of(here ^ mask, 16), -1
    ).reshape(1, -1)
    om_bits = flat_of({"o": n_o - 1, "a": 0, "b": 0, "c": 0, "m": 1})
    quad_masks = masks[0, :quads]
    owner = (np.arange(8, dtype=np.int32)[:, None] * 2) | ((here & om_bits) ^ quad_masks)[None, :]
    plain = target_of(owner.reshape(-1), 40).reshape(-1, 1)
    eight_at = ((here ^ mask[::quads]) // 2) % 8
    both = jnp.concatenate([v[:piece] for v in got] + [v[piece:] for v in got], axis=0)
    cot_1 = grow(cotangent, first_move)
    keep = keep_mask.reshape(1, -1)
    peer_keep = permute(keep, peer_move)
    own_gu = jnp.swapaxes(ffn_in, 1, 2).reshape(2 * ff_rows, width)

    def two_halves(held, got):
        half = held.shape[0] // 2
        return [jnp.concatenate([held[at : at + half], got[at : at + half]], axis=0) for at in (0, half)]

    both, cot_1, peer_keep, memory, own_down, target, one, plain, eight_at = stage(
        (both, cot_1, peer_keep, memory, ffn_down, target, one, plain, eight_at)
    )
    targets, ones = (jnp.split(v, 2, axis=1) for v in (target, one))
    both = jnp.concatenate(two_halves(both, permute(both, first_move)), axis=0)
    down_o = over_o(own_down)
    peer_memory = permute(memory, peer_move)
    lookup = distance_bucket_lookup.reshape(1, -1)
    ring, items_col, items_row, slot, own_1 = kernel_call(
        tables_kernel,
        [
            shape(8, WIDTH, kind=F32), shape(rows, 1, kind=jnp.int32), shape(1, rows, kind=jnp.int32),
            shape(2, slots, kind=jnp.int32), shape(*full),
        ],
        me["m"].reshape(1), target_lengths[0], memory_lengths, keep, peer_keep, lookup, rel_bias,
        tokens, norm_gains, scalars=3,
    )

    both, down_o, own_gu, ring, own_1 = stage((both, down_o, own_gu, ring, own_1))
    self_lo, cross_lo = two_halves(both, permute(both, second_move))
    w_down = over_m(down_o)
    gu_o = over_o(own_gu)
    gu_m = permute(own_gu, peer_move)

    self_lo, cross_lo, peer_memory, cot_1, gu_o, gu_m, w_down, target = stage(
        (self_lo, cross_lo, peer_memory, cot_1, gu_o, gu_m, w_down, target)
    )
    w_self = (self_lo, permute(self_lo, core_move))

    w_self, cross_lo, cot_1 = stage((w_self, cross_lo, cot_1))
    x_2, n_2, qkv, low_1 = kernel_call(
        self_forward_kernel,
        [shape(*full, kind=F32), shape(*full), shape(rows, 3 * INNER), shape(*slim)],
        tokens, own_1, norm_gains, *w_self, target, ring, items_col, items_row,
    )
    w_cross = (cross_lo, permute(cross_lo, core_move))
    cot_lo = grow(cot_1, second_move)

    x_2, w_cross, gu_o = stage((x_2, w_cross, gu_o))
    kv_own, kv_peer = kernel_call(
        memory_forward_kernel, [kv_shape] * 2, memory, peer_memory, *w_cross, target
    )
    x_3, n_3, q_2, low_2 = kernel_call(
        cross_forward_kernel,
        [shape(*full, kind=F32), shape(*full), shape(*slim), shape(*slim)],
        x_2, n_2, norm_gains, *w_cross, target, kv_own, kv_peer, items_col, slot,
    )
    w_gu = gu_o + [gu_m] + [permute(v, peer_move) for v in gu_o[1:]]

    x_3, n_3, cot_lo, w_gu = stage((x_3, n_3, cot_lo, w_gu))
    n_1 = grow(n_3, first_move)
    cot_hi = permute(cot_lo, core_move)

    def grad_hidden(value):
        return kernel_call(
            grad_hidden_kernel, shape(half, cols, kind=F32), value, *w_down, scratch=[down]
        )

    gh_lo = grad_hidden(cot_lo)

    n_1, cot_hi, gh_lo = stage((n_1, cot_hi, gh_lo))
    n_lo = grow(n_1, second_move)
    gh_hi = grad_hidden(cot_hi)

    def ffn(value, gh):
        return kernel_call(
            ffn_kernel,
            [shape(half, cols), shape(half, cols), shape(half, cols), shape(half, width)],
            value, gh, *w_gu, scratch=[gate, up],
        )

    n_lo, gh_hi, own_1 = stage((n_lo, gh_hi, own_1))
    n_hi = permute(n_lo, core_move)
    lo_f = ffn(n_lo, gh_lo)
    one_1 = grow(own_1, first_move)

    n_hi, lo_f, one_1 = stage((n_hi, lo_f, one_1))
    hi_f = ffn(n_hi, gh_hi)

    (h_lo, g_lo, u_lo, gn_lo), (h_hi, g_hi, u_hi, gn_hi), one_1 = stage((lo_f, hi_f, one_1))
    got_c = permute(gn_hi, core_move)

    def ffn_out(*args):
        return kernel_call(ffn_out_kernel, shape(half, width), *args, *w_down, scratch=[down])

    out_hi = ffn_out(h_hi)

    def summed(at, end, *parts):
        return sum(v[at:end].astype(F32) for v in parts).astype(BF16)

    got_c, out_hi, h_lo = stage((got_c, out_hi, h_lo))
    got_2 = permute(summed(2 * rows, 4 * rows, gn_lo, got_c), second_move)
    out_got = permute(out_hi, core_move)
    grad_down, grad_gu = kernel_call(
        lambda *refs: ffn_weights_kernel(quads, *refs),
        [shape(cols, width), shape(2 * cols, width)],
        h_lo, h_hi, g_lo, g_hi, u_lo, u_hi, n_lo, n_hi, cot_lo, cot_hi,
    )

    got_2, out_got, grad_down, grad_gu, one_1 = stage((got_2, out_got, grad_down, grad_gu, one_1))
    got_1 = permute(summed(rows, 2 * rows, gn_lo, got_c, got_2), first_move)
    out_lo = ffn_out(h_lo, out_got)
    down_m = permute(grad_down[cols // 2 :], peer_move)

    got_1, out_lo, grad_gu, one_1 = stage((got_1, out_lo, grad_gu, one_1))
    low_3, grad_2, dq, dkv_own, dkv_peer, gains_23 = kernel_call(
        cross_backward_kernel,
        [
            shape(*full), shape(*full, kind=F32), shape(*slim), kv_shape, kv_shape,
            shape(2, width, kind=F32),
        ],
        gn_lo, got_c, got_2, got_1, x_3, x_2, norm_gains, cotangent, *w_cross, target, q_2, kv_own,
        kv_peer, items_col, slot,
    )
    n1_lo = grow(one_1, second_move)
    gu_m = permute(grad_gu[cols:], peer_move)

    low_3, grad_2, dq, dkv_own, dkv_peer, gains_23, down_m, n1_lo = stage(
        (low_3, grad_2, dq, dkv_own, dkv_peer, gains_23, down_m, n1_lo)
    )
    operands = (dq, low_2, dkv_own, dkv_peer, low_1, n_2, low_3, memory, peer_memory, grad_2)
    stack = shape(4 * quads * (piece + 16), width)
    sent = kernel_call(weights_kernel, stack, *operands, targets[1], ones[1])
    n1_hi = permute(n1_lo, core_move)

    def over_back(part, grad, got):
        return [
            permute(summed(k * part, (k + 1) * part, grad, got), flips(o=k)) for k in range(1, n_o)
        ]

    sent, grad_2, dkv_peer, n1_hi = stage((sent, grad_2, dkv_peer, n1_hi))
    cross_c = permute(sent, core_move)
    dkv_got = permute(dkv_peer, peer_move)
    out_2 = permute(out_lo[2 * rows :], second_move)
    grad_tokens, dyt, small = kernel_call(
        self_backward_kernel,
        [shape(*full, kind=F32), shape(8 * quads * 40, rows), shape(16, width, kind=F32)],
        grad_2, tokens, norm_gains, *w_self, target, plain, qkv, ring, items_col, items_row, lookup,
        gains_23, scratch=[pltpu.VMEM((rows, 3 * INNER), BF16), pltpu.VMEM((8, WIDTH), F32)],
    )
    down_b = over_back(ff_rows, grad_down, down_m)

    cross_c, grad_tokens, dyt, small, gu_m, down_b, out_2 = stage(
        (cross_c, grad_tokens, dyt, small, gu_m, down_b, out_2)
    )
    held = exchange(dyt, GROUP, 8)
    cross_part = kernel_call(weights_kernel, stack, *operands, targets[0], ones[0], cross_c)
    small = small + permute(small, core_move)
    gu_b = over_back(2 * ff_rows, grad_gu, gu_m)

    held, cross_part, dkv_got, small = stage((held, cross_part, dkv_got, small))
    quarter = cross_part.shape[0] // 4
    cross_2 = permute(cross_part[2 * quarter :], second_move)
    part_self = kernel_call(
        columns_kernel, shape(quads * 40, width), eight_at, held, n1_lo, n1_hi, scalars=1
    )
    small = small + permute(small, second_move)

    cross_2, part_self, small, gu_b = stage((cross_2, part_self, small, gu_b))
    cross_1 = permute(summed(quarter, 2 * quarter, cross_part, cross_2), first_move)
    out_1 = permute(summed(rows, 2 * rows, out_lo, out_2), first_move)
    grad_memory = kernel_call(
        memory_backward_kernel, shape(slots, width, kind=F32), dkv_own, dkv_got, *w_cross, target
    )
    small = small + permute(small, first_move)

    cross_1, small, grad_memory, out_1 = stage((cross_1, small, grad_memory, out_1))
    cross_sum = cross_part[:quarter] + cross_2[:quarter].astype(F32) + cross_1.astype(F32)

    def pieces(k):
        at, end = k * piece, wide + k * 16
        return jnp.concatenate(
            [cross_sum[at : at + piece], cross_sum[end : end + 16], part_self[k * 40 : k * 40 + 40]],
            axis=0,
        )

    pieces_got = [permute(pieces(k + 1).astype(BF16), move) for k, move in enumerate(moves)]
    small_got = [permute(small, move) for move in moves]
    block_out = summed(0, rows, x_3, out_lo, out_2, out_1)

    pieces_got, small_got, block_out = stage((pieces_got, small_got, block_out))
    total = pieces(0) + sum(g.astype(F32) for g in pieces_got)
    small = small + sum(small_got)
    sum_cross, sum_self = total[: piece + 16], total[piece + 16 :]

    def back_sum(part, *parts):
        return sum(v[:part].astype(F32) for v in parts)

    sum_down = back_sum(ff_rows, grad_down, down_m, *down_b)
    sum_gu = back_sum(2 * ff_rows, grad_gu, gu_m, *gu_b)

    def three(total):
        query, key, value = (total[k * part_rows : (k + 1) * part_rows] for k in range(3))
        return query.T, jnp.transpose(jnp.stack([key, value], axis=1), (1, 2, 0))

    squery, skv = three(sum_self)
    cquery, ckv = three(sum_cross)
    fin = jnp.swapaxes(sum_gu.reshape(2, ff_rows, width), 1, 2)
    base = 4 * part_rows
    return (
        block_out,
        grad_tokens,
        grad_memory,
        squery,
        skv,
        sum_cross[base : base + part_rows],
        cquery,
        ckv,
        sum_cross[3 * part_rows : base],
        fin,
        sum_down,
        small[:3],
        small[8 : 8 + HEADS, : rel_bias.shape[0]].T,
    )


def solution(mesh):
    n_tok, n_mem = mesh.devices.shape
    grid = Mesh(mesh.devices.reshape(n_tok // 8, 2, 2, 2, n_mem), AXES)
    tok = AXES[:-1]
    rows = P(AXES, None)
    cols = P(None, AXES)
    deep = P(None, None, AXES)
    in_specs = (
        rows,
        rows,
        P(tok, None, None),
        P(tok, None),
        P(AXES),
        P(),
        cols,
        deep,
        rows,
        cols,
        deep,
        rows,
        deep,
        rows,
        P(),
        P(),
        rows,
    )
    out_specs = (rows, rows, rows, cols, deep, rows, cols, deep, rows, deep, rows, P(), P())
    return jax.shard_map(
        on_device, mesh=grid, in_specs=in_specs, out_specs=out_specs, check_vma=False
    )
```

time: 513 us -> 405 us (0.79)
  matrix products: 48 us -> 0 us
  other arithmetic: 63.8 us -> 18.6 us
  local copies, waits for them, and re-layouts: 67.2 us -> 35.2 us
  Pallas kernels: 64.7 us -> 79 us
    dot_general x14 -> x0, matrix products: 47.7 us -> none  [the longest x6 21.9 us: dot_nn(): lax.dot_general(left, right, (((1,), (0,)), ((), ())), preferred_element_...]
    slice x22 -> x15, local copies, waits for them, and re-layouts: 21.2 us -> 5.85 us  [the longest x2 1.49 us: two_halves(): got[at:at + half]]
    pallas_call x5 -> x18, Pallas kernels: 64.7 us -> 79 us  [kernel_call(): pl.pallas_call(kernel, out_shape=out_shape, in_specs=[pl.BlockSpec(memory...]
    convert_element_type x2 -> x0, local copies, waits for them, and re-layouts: 12.2 us -> none  [scatter_all(): kept = held[:half].astype(F32)]
    convert_element_type x14 -> x8, other arithmetic: 18.9 us -> 7.91 us  [the longest x7 7.87 us: summed(): return sum((v[at:end].astype(F32) for v in parts)).astype(BF16)]
    unnamed x141 -> x208, local copies, waits for them, and re-layouts: 15.4 us -> 26 us
    concatenate x4 -> x1, local copies, waits for them, and re-layouts: 9.55 us -> 0.99 us  [on_device(): jnp.concatenate([v[:piece] for v in got] + [v[piece:] for v in got], axis=0)]
    concatenate x9 -> x11, other arithmetic: 13.3 us -> 5.39 us  [the longest x6 3.96 us: grow(): return jnp.concatenate([held, permute(held, move)], axis=0)]
  transfers between devices with their start and end apart: 49 -> 48, of which waited for: 23 -> 23; matrix products, arithmetic and copies ran while one was open for 29% -> 6% of each run, Pallas kernels for 3% -> 18%
where the time goes in v2:
time: 405 us; the launch traced here: 400 us
  waiting for transfers between devices  207 us (51%)
  Pallas kernels  79 us (20%)
  starting transfers between devices  57.8 us (14%)
  local copies, waits for them, and re-layouts  35.2 us (9%)
  other arithmetic  18.6 us (5%)
    ppermute x47, waiting for transfers between devices, permute(): return lax.ppermute(cut(value), AXES, pairs).reshape(value.shape)  207 us
    pallas_call x18, Pallas kernels, kernel_call(): pl.pallas_call(kernel, out_shape=out_shape, in_specs=[pl.BlockSpec(memory...  79 us
    ppermute x47, starting transfers between devices, permute(): return lax.ppermute(cut(value), AXES, pairs).reshape(value.shape)  53.6 us
    unnamed x208, local copies, waits for them, and re-layouts  26 us
  transfers between devices with their start and end apart: 48, of which 23 were waited for; matrix products, arithmetic and copies ran while one was open for 6% of the time, Pallas kernels for 18%

profile of v2, /device:TPU:0, one launch (start us, length us, event | category | flops | bytes accessed | tf_op | source)
XLA Modules:
  0.0 400.1 jit_solution(10823063536859394988)
XLA Ops:
  6.5 4.1 %collective-permute-start = (bf16[96,1472]{1,0:T(8,128)(2,1)S(1)}, bf16[96,1472]{1,0:T(8,128)(2,1)S(1)}, u32[]{:S(2)}, u32[]{:S(2)}) collective-permute-start(bf16[96,1472]{1,0:T(8,128)(2,1)S(1)} %shard_map.336), channel_id=1, source_target_pairs={{0,16},{1,17},{2,18},{3,19},{4,20},{5,21},{6,22},{7,23},{8,24},{9,... | collective-permute-start | bytes 847880 | tf_op jit(solution)/shard_map/ppermute | solution.py:499
  17.4 13.6 %collective-permute-done = bf16[96,1472]{1,0:T(8,128)(2,1)S(1)} collective-permute-done((bf16[96,1472]{1,0:T(8,128)(2,1)S(1)}, bf16[96,1472]{1,0:T(8,128)(2,1)S(1)}, u32[]{:S(2)}, u32[]{:S(2)}) %collective-permute-start) | collective-permute-done | bytes 282656 | tf_op jit(solution)/shard_map/ppermute | solution.py:499
  31.1 6.6 %collective-permute-done.2 = bf16[96,1472]{1,0:T(8,128)(2,1)} collective-permute-done((bf16[96,1472]{1,0:T(8,128)(2,1)S(1)}, bf16[96,1472]{1,0:T(8,128)(2,1)}, u32[]{:S(2)}, u32[]{:S(2)}) %collective-permute-start.2) | collective-permute-done | bytes 282656 | tf_op jit(solution)/shard_map/ppermute | solution.py:499
  44.7 13.5 %collective-permute-done.5 = bf16[6,64,1472]{2,1,0:T(8,128)(2,1)} collective-permute-done((bf16[6,64,1472]{2,1,0:T(8,128)(2,1)S(1)}, bf16[6,64,1472]{2,1,0:T(8,128)(2,1)}, u32[]{:S(2)}, u32[]{:S(2)}) %collective-permute-start.5) | collective-permute-done | bytes 1130528 | tf_op jit(solution)/shard_map/ppermute | solution.py:499
  66.6 36.9 %collective-permute-done.7 = bf16[12,64,1472]{2,1,0:T(8,128)(2,1)S(1)} collective-permute-done((bf16[12,64,1472]{2,1,0:T(8,128)(2,1)S(1)}, bf16[12,64,1472]{2,1,0:T(8,128)(2,1)S(1)}, u32[]{:S(2)}, u32[]{:S(2)}) %collective-permute-start.7) | collective-permute-done | bytes 2261024 | tf_op jit(solution)/shard_map/ppermute | solution.py:499
  105.7 7.1 %collective-permute-done.12.refs_3_.refs_4_ = bf16[112,1472]{1,0:T(8,128)(2,1)S(1)} collective-permute-done((bf16[112,1472]{1,0:T(8,128)(2,1)S(1)}, bf16[112,1472]{1,0:T(8,128)(2,1)S(1)}, u32[]{:S(2)}, u32[]{:S(2)}) %collective-permute-start.12) | collective-permute-done | bytes 329760 | tf_op jit(solution)/shard_map/ppermute | solution.py:499
  112.9 4.5 %collective-permute-done.13 = bf16[12,64,1472]{2,1,0:T(8,128)(2,1)S(1)} collective-permute-done((bf16[12,64,1472]{2,1,0:T(8,128)(2,1)S(1)}, bf16[12,64,1472]{2,1,0:T(8,128)(2,1)S(1)}, u32[]{:S(2)}, u32[]{:S(2)}) %collective-permute-start.13) | collective-permute-done | bytes 2261024 | tf_op jit(solution)/shard_map/ppermute | solution.py:499
  118.7 5.5 %shard_map.338 = (f32[192,1472]{1,0:T(8,128)S(1)}, bf16[192,1472]{1,0:T(8,128)(2,1)S(1)}, bf16[192,1152]{1,0:T(8,128)(2,1)S(1)}, bf16[192,384]{1,0:T(8,128)(2,1)S(1)}) custom-call(bf16[192,1472]{1,0:T(8,128)(2,1)S(1)} %copy-done.25, bf16[192,1472]{1,0:T(8,128)(2,1)S(1)} %get-tuple-element.223.n1_ref, f32[3,1472]{1,0:T(4,128)S(1)} %copy-done.43, ...), custom_call_target="tpu_custom_call" | custom-call | flops 5000000000 | bytes 1 | tf_op jit(solution)/shard_map/pallas_call | solution.py:41
  124.3 9.4 %collective-permute-done.15 = bf16[6,64,1472]{2,1,0:T(8,128)(2,1)S(1)} collective-permute-done((bf16[6,64,1472]{2,1,0:T(8,128)(2,1)S(1)}, bf16[6,64,1472]{2,1,0:T(8,128)(2,1)S(1)}, u32[]{:S(2)}, u32[]{:S(2)}) %collective-permute-start.15) | collective-permute-done | bytes 1130528 | tf_op jit(solution)/shard_map/ppermute | solution.py:499
  134.5 4.7 %shard_map.339 = (bf16[288,768]{1,0:T(8,128)(2,1)S(1)}, bf16[288,768]{1,0:T(8,128)(2,1)S(1)}) custom-call(bf16[288,1472]{1,0:T(8,128)(2,1)S(1)} %copy-done.19, bf16[288,1472]{1,0:T(8,128)(2,1)S(1)} %collective-permute-done.8.peer_ref.mem_peer_ref, bf16[768,1472]{1,0:T(8,128)(2,1)S(1)} %get-tuple-element.193.w0_ref, bf16[768,1472]{1,0:T(8,128)(2,1)S(1)} %bitcast.78, ...), custom_call_target="tpu_custom_call" | custom-call | flops 5000000000 | bytes 1 | tf_op jit(solution)/shard_map/pallas_call | solution.py:41
  139.2 6.8 %shard_map.340 = (f32[192,1472]{1,0:T(8,128)S(1)}, bf16[192,1472]{1,0:T(8,128)(2,1)S(1)}, bf16[192,384]{1,0:T(8,128)(2,1)S(1)}, bf16[192,384]{1,0:T(8,128)(2,1)S(1)}) custom-call(f32[192,1472]{1,0:T(8,128)S(1)} %get-tuple-element.191.x_ref.x2_ref, bf16[192,1472]{1,0:T(8,128)(2,1)S(1)} %get-tuple-element.192.n_ref.n2_ref, f32[3,1472]{1,0:T(4,128)S(1)} %copy-done.43, ...), custom_call_target="tpu_custom_call" | custom-call | flops 5000000000 | bytes 1 | tf_op jit(solution)/shard_map/pallas_call | solution.py:41
  146.1 4.8 %collective-permute-done.16.refs_3_ = bf16[224,1472]{1,0:T(8,128)(2,1)S(1)} collective-permute-done((bf16[224,1472]{1,0:T(8,128)(2,1)S(1)}, bf16[224,1472]{1,0:T(8,128)(2,1)S(1)}, u32[]{:S(2)}, u32[]{:S(2)}) %collective-permute-start.16) | collective-permute-done | bytes 659488 | tf_op jit(solution)/shard_map/ppermute | solution.py:499
  153.8 7.0 %collective-permute-done.17 = bf16[192,1472]{1,0:T(8,128)(2,1)S(1)} collective-permute-done((bf16[192,1472]{1,0:T(8,128)(2,1)S(1)}, bf16[192,1472]{1,0:T(8,128)(2,1)S(1)}, u32[]{:S(2)}, u32[]{:S(2)}) %collective-permute-start.17) | collective-permute-done | bytes 565280 | tf_op jit(solution)/shard_map/ppermute | solution.py:499
  163.5 13.6 %collective-permute-done.19 = bf16[6,64,1472]{2,1,0:T(8,128)(2,1)S(1)} collective-permute-done((bf16[6,64,1472]{2,1,0:T(8,128)(2,1)S(1)}, bf16[6,64,1472]{2,1,0:T(8,128)(2,1)S(1)}, u32[]{:S(2)}, u32[]{:S(2)}) %collective-permute-start.19) | collective-permute-done | bytes 1130528 | tf_op jit(solution)/shard_map/ppermute | solution.py:499
  179.0 5.2 %shard_map.343 = (bf16[768,448]{1,0:T(8,128)(2,1)S(1)}, bf16[768,448]{1,0:T(8,128)(2,1)S(1)}, bf16[768,448]{1,0:T(8,128)(2,1)S(1)}, bf16[768,1472]{1,0:T(8,128)(2,1)S(1)}) custom-call(bf16[768,1472]{1,0:T(8,128)(2,1)S(1)} %pad_maximum_fusion.4.n_ref.refs_6_, f32[768,448]{1,0:T(8,128)S(1)} %shard_map.341.gh_ref, bf16[224,1472]{1,0:T(8,128)(2,1)S(1)} %bitcast.94, ...), custom_call_target="tpu_custom_call" | custom-call | flops 5000000000 | bytes 1 | tf_op jit(solution)/shard_map/pallas_call | solution.py:41
  188.5 5.2 %shard_map.344 = (bf16[768,448]{1,0:T(8,128)(2,1)S(1)}, bf16[768,448]{1,0:T(8,128)(2,1)S(1)}, bf16[768,448]{1,0:T(8,128)(2,1)S(1)}, bf16[768,1472]{1,0:T(8,128)(2,1)S(1)}) custom-call(bf16[768,1472]{1,0:T(8,128)(2,1)S(1)} %bitcast.87, f32[768,448]{1,0:T(8,128)S(1)} %shard_map.342.gh_ref, bf16[224,1472]{1,0:T(8,128)(2,1)S(1)} %bitcast.95, ...), custom_call_target="tpu_custom_call" | custom-call | flops 5000000000 | bytes 1 | tf_op jit(solution)/shard_map/pallas_call | solution.py:41
  200.2 6.6 %shard_map.346 = (bf16[448,1472]{1,0:T(8,128)(2,1)S(1)}, bf16[896,1472]{1,0:T(8,128)(2,1)S(1)}) custom-call(bf16[768,448]{1,0:T(8,128)(2,1)S(1)} %copy-done.62, bf16[768,448]{1,0:T(8,128)(2,1)S(1)} %copy-done.68, bf16[768,448]{1,0:T(8,128)(2,1)S(1)} %copy-done.64, bf16[768,448]{1,0:T(8,128)(2,1)S(1)} %get-tuple-element.243.refs_3_, ...), custom_call_target="tpu_custom_call" | custom-call | flops 5000000000 | bytes 1 | tf_op jit(solution)/shard_map/pallas_call | solution.py:41
  206.9 8.2 %collective-permute-done.23 = bf16[6,64,1472]{2,1,0:T(8,128)(2,1)S(1)} collective-permute-done((bf16[6,64,1472]{2,1,0:T(8,128)(2,1)S(1)}, bf16[6,64,1472]{2,1,0:T(8,128)(2,1)S(1)}, u32[]{:S(2)}, u32[]{:S(2)}) %collective-permute-start.23) | collective-permute-done | bytes 1130528 | tf_op jit(solution)/shard_map/ppermute | solution.py:499
  218.4 6.9 %collective-permute-done.25.got_ref = bf16[192,1472]{1,0:T(8,128)(2,1)S(1)} collective-permute-done((bf16[192,1472]{1,0:T(8,128)(2,1)S(1)}, bf16[192,1472]{1,0:T(8,128)(2,1)S(1)}, u32[]{:S(2)}, u32[]{:S(2)}) %collective-permute-start.25) | collective-permute-done | bytes 565280 | tf_op jit(solution)/shard_map/ppermute | solution.py:499
  227.1 9.0 %shard_map.348 = (bf16[192,1472]{1,0:T(8,128)(2,1)S(1)}, f32[192,1472]{1,0:T(8,128)S(1)}, bf16[192,384]{1,0:T(8,128)(2,1)S(1)}, bf16[288,768]{1,0:T(8,128)(2,1)S...) custom-call(bf16[768,1472]{1,0:T(8,128)(2,1)S(1)} %get-tuple-element.235.lo_ref, ...), custom_call_target="tpu_custom_call" | custom-call | flops 5000000000 | bytes 1 | tf_op jit(solution)/shard_map/pallas_call | solution.py:41
  236.1 5.4 %collective-permute-done.27 = bf16[6,64,1472]{2,1,0:T(8,128)(2,1)S(1)} collective-permute-done((bf16[6,64,1472]{2,1,0:T(8,128)(2,1)S(1)}, bf16[6,64,1472]{2,1,0:T(8,128)(2,1)S(1)}, u32[]{:S(2)}, u32[]{:S(2)}) %collective-permute-start.27) | collective-permute-done | bytes 1130528 | tf_op jit(solution)/shard_map/ppermute | solution.py:499
  243.7 5.9 %shard_map.349 = bf16[1024,1472]{1,0:T(8,128)(2,1)} custom-call(bf16[192,384]{1,0:T(8,128)(2,1)S(1)} %get-tuple-element.264.dq_ref, bf16[192,384]{1,0:T(8,128)(2,1)S(1)} %copy-done.78, bf16[288,768]{1,0:T(8,128)(2,1)S(1)} %get-tuple-element.266.own_ref, bf16[288,768]{1,0:T(8,128)(2,1)S(1)} %get-tuple-element.286.peer_ref, bf16[192,384]{1,0:T(8,128)(2,1)S(1)} %copy-done.75, ...), custom_call_target="tpu_custom_call" | custom-call | flops 5000000000 | bytes 1 | tf_op jit(solution)/shard_map/pallas_call | solution.py:41
  266.8 9.5 %shard_map.350 = (f32[192,1472]{1,0:T(8,128)}, bf16[1280,192]{1,0:T(8,128)(2,1)}, f32[16,1472]{1,0:T(8,128)S(1)}) custom-call(f32[192,1472]{1,0:T(8,128)S(1)} %copy-done.50, bf16[192,1472]{1,0:T(8,128)(2,1)S(1)} %copy-done.26, f32[3,1472]{1,0:T(4,128)S(1)} %copy-done.43, bf16[768,1472]{1,0:T(8,128)(2,1)S(1)} %copy-done.8, bf16[768,1472]{1,0:T(8,128)(2,1)S(1)} %bitcast.83, ...), custom_call_target="tpu_custom_call" | custom-call | flops 5000000000 | bytes 1 | tf_op jit(solution)/shard_map/pallas_call | solution.py:41
  276.9 7.9 %collective-permute-done.30 = bf16[448,1472]{1,0:T(8,128)(2,1)} collective-permute-done((bf16[448,1472]{1,0:T(8,128)(2,1)}, bf16[448,1472]{1,0:T(8,128)(2,1)}, u32[]{:S(2)}, u32[]{:S(2)}) %collective-permute-start.30) | collective-permute-done | bytes 1318944 | tf_op jit(solution)/shard_map/ppermute | solution.py:499
  284.8 4.2 %all-to-all-start = ((bf16[8,160,192]{2,1,0:T(8,128)(2,1)}), bf16[8,160,192]{2,1,0:T(8,128)(2,1)}, u32[]{:S(2)}, u32[]{:S(2)}) async-start(bf16[8,160,192]{2,1,0:T(8,128)(2,1)} %bitcast.41), calls=%async_computation | async-start | bytes 1310720 | tf_op jit(solution)/shard_map/all_to_all | solution.py:522
  300.3 6.1 %shard_map.351 = bf16[1024,1472]{1,0:T(8,128)(2,1)S(1)} custom-call(bf16[192,384]{1,0:T(8,128)(2,1)S(1)} %get-tuple-element.264.dq_ref, bf16[192,384]{1,0:T(8,128)(2,1)S(1)} %copy-done.79, bf16[288,768]{1,0:T(8,128)(2,1)S(1)} %copy-done.55, bf16[288,768]{1,0:T(8,128)(2,1)S(1)} %copy-done.28, bf16[192,384]{1,0:T(8,128)(2,1)S(1)} %copy-done.76, ...), custom_call_target="tpu_custom_call" | custom-call | flops 5000000000 | bytes 1 | tf_op jit(solution)/shard_map/pallas_call | solution.py:41
  316.5 4.6 %shard_map.353 = f32[288,1472]{1,0:T(8,128)} custom-call(bf16[288,768]{1,0:T(8,128)(2,1)S(1)} %copy-done.56, bf16[288,768]{1,0:T(8,128)(2,1)} %collective-permute-done.33.got_ref, bf16[768,1472]{1,0:T(8,128)(2,1)S(1)} %copy-done.6, bf16[768,1472]{1,0:T(8,128)(2,1)S(1)} %bitcast.81, s32[1,1536]{1,0:T(1,128)S(1)} %add.175.target_ref), custom_call_target="tpu_custom_call" | custom-call | flops 5000000000 | bytes 1 | tf_op jit(solution)/shard_map/pallas_call | solution.py:41
  324.9 18.0 %collective-permute-done.36 = f32[16,1472]{1,0:T(8,128)S(1)} collective-permute-done((f32[16,1472]{1,0:T(8,128)S(1)}, f32[16,1472]{1,0:T(8,128)S(1)}, u32[]{:S(2)}, u32[]{:S(2)}) %collective-permute-start.36) | collective-permute-done | bytes 94240 | tf_op jit(solution)/shard_map/ppermute | solution.py:499
  347.8 8.8 %collective-permute-done.38 = bf16[4,64,1472]{2,1,0:T(8,128)(2,1)S(1)} collective-permute-done((bf16[4,64,1472]{2,1,0:T(8,128)(2,1)S(1)}, bf16[4,64,1472]{2,1,0:T(8,128)(2,1)S(1)}, u32[]{:S(2)}, u32[]{:S(2)}) %collective-permute-start.38) | collective-permute-done | bytes 753696 | tf_op jit(solution)/shard_map/ppermute | solution.py:499
  366.3 7.0 %collective-permute-done.44 = f32[16,1472]{1,0:T(8,128)S(1)} collective-permute-done((f32[16,1472]{1,0:T(8,128)S(1)}, f32[16,1472]{1,0:T(8,128)S(1)}, u32[]{:S(2)}, u32[]{:S(2)}) %collective-permute-start.44) | collective-permute-done | bytes 94240 | tf_op jit(solution)/shard_map/ppermute | solution.py:499
  375.9 6.3 %collective-permute-done.43 = bf16[104,1472]{1,0:T(8,128)(2,1)S(1)} collective-permute-done((bf16[104,1472]{1,0:T(8,128)(2,1)S(1)}, bf16[104,1472]{1,0:T(8,128)(2,1)S(1)}, u32[]{:S(2)}, u32[]{:S(2)}) %collective-permute-start.43) | collective-permute-done | bytes 306208 | tf_op jit(solution)/shard_map/ppermute | solution.py:499
  382.2 13.6 %collective-permute-done.41 = bf16[104,1472]{1,0:T(8,128)(2,1)S(1)} collective-permute-done((bf16[104,1472]{1,0:T(8,128)(2,1)S(1)}, bf16[104,1472]{1,0:T(8,128)(2,1)S(1)}, u32[]{:S(2)}, u32[]{:S(2)}) %collective-permute-start.41) | collective-permute-done | bytes 306208 | tf_op jit(solution)/shard_map/ppermute | solution.py:499
  (352 shorter events, 120.8 us)
Async XLA Ops:
  6.5 24.6 %collective-permute-start = (bf16[96,1472]{1,0:T(8,128)(2,1)S(1)}, bf16[96,1472]{1,0:T(8,128)(2,1)S(1)}, u32[]{:S(2)}, u32[]{:S(2)}) collective-permute-start(bf16[96,1472]{1,0:T(8,128)(2,1)S(1)} %shard_map.336), channel_id=1, source_target_pairs={{0,16},{1,17},{2,18},{3,19},{4,20},{5,21},{6,22},{7,23},{8,24},{9,... | collective-permute-start | bytes 847880 | tf_op jit(solution)/shard_map/ppermute | solution.py:499
  10.6 20.5 %collective-permute-start.1 = (bf16[96,1472]{1,0:T(8,128)(2,1)S(1)}, bf16[96,1472]{1,0:T(8,128)(2,1)S(1)}, u32[]{:S(2)}, u32[]{:S(2)}) collective-permute-start(bf16[96,1472]{1,0:T(8,128)(2,1)S(1)} %shard_map.336), channel_id=1, source_target_pairs={{0,1},{1,0},{2,3},{3,2},{4,5},{5,4},{6,7},{7,6},{8,9},{9,8},{10,11... | collective-permute-start | bytes 847880 | tf_op jit(solution)/shard_map/ppermute | solution.py:499
  12.1 25.6 %collective-permute-start.2 = (bf16[96,1472]{1,0:T(8,128)(2,1)S(1)}, bf16[96,1472]{1,0:T(8,128)(2,1)}, u32[]{:S(2)}, u32[]{:S(2)}) collective-permute-start(bf16[96,1472]{1,0:T(8,128)(2,1)S(1)} %shard_map.336), channel_id=1, source_target_pairs={{0,17},{1,16},{2,19},{3,18},{4,21},{5,20},{6,23},{7,22},{8,25},{9,... | collective-permute-start | bytes 847880 | tf_op jit(solution)/shard_map/ppermute | solution.py:499
  12.1 29.8 %collective-permute-start.4 = (s32[1,288]{1,0:T(1,128)S(1)}, s32[1,288]{1,0:T(1,128)S(1)}, u32[]{:S(2)}, u32[]{:S(2)}) collective-permute-start(s32[1,288]{1,0:T(1,128)S(1)} %reshape.249.keep_ref), channel_id=1, source_target_pairs={{0,1},{1,0},{2,3},{3,2},{4,5},{5,4},{6,7},{7,6},{8,9},{9,8},{10,11... | collective-permute-start | bytes 3464 | tf_op jit(solution)/shard_map/ppermute | solution.py:499
  13.9 25.8 %collective-permute-start.3 = (bf16[192,1472]{1,0:T(8,128)(2,1)S(1)}, bf16[192,1472]{1,0:T(8,128)(2,1)}, u32[]{:S(2)}, u32[]{:S(2)}) collective-permute-start(bf16[192,1472]{1,0:T(8,128)(2,1)S(1)} %copy-done.12), channel_id=1, source_target_pairs={{0,4},{1,5},{2,10},{3,11},{4,0},{5,1},{6,14},{7,15},{8,12},{9,13},... | collective-permute-start | bytes 1695752 | tf_op jit(solution)/shard_map/ppermute | solution.py:499
  41.9 16.3 %collective-permute-start.5 = (bf16[6,64,1472]{2,1,0:T(8,128)(2,1)S(1)}, bf16[6,64,1472]{2,1,0:T(8,128)(2,1)}, u32[]{:S(2)}, u32[]{:S(2)}) collective-permute-start(bf16[6,64,1472]{2,1,0:T(8,128)(2,1)S(1)} %bitcast.114), channel_id=1, source_target_pairs={{0,4},{1,5},{2,10},{3,11},{4,0},{5,1},{6,14},{7,15},{8,12},{9,13},... | collective-permute-start | bytes 3391496 | tf_op jit(solution)/shard_map/ppermute | solution.py:499
  43.5 16.3 %collective-permute-start.6 = (bf16[112,1472]{1,0:T(8,128)(2,1)S(1)}, bf16[112,1472]{1,0:T(8,128)(2,1)S(1)}, u32[]{:S(2)}, u32[]{:S(2)}) collective-permute-start(bf16[112,1472]{1,0:T(8,128)(2,1)S(1)} %copy-done.29), channel_id=1, source_target_pairs={{0,16},{1,17},{2,18},{3,19},{4,20},{5,21},{6,22},{7,23},{8,24},{9,... | collective-permute-start | bytes 989192 | tf_op jit(solution)/shard_map/ppermute | solution.py:499
  59.8 43.7 %collective-permute-start.7 = (bf16[12,64,1472]{2,1,0:T(8,128)(2,1)S(1)}, bf16[12,64,1472]{2,1,0:T(8,128)(2,1)S(1)}, u32[]{:S(2)}, u32[]{:S(2)}) collective-permute-start(bf16[12,64,1472]{2,1,0:T(8,128)(2,1)S(1)} %bitcast.103), channel_id=1, source_target_pairs={{0,8},{1,9},{2,6},{3,7},{4,12},{5,13},{6,2},{7,3},{8,0},{9,1},{10,... | collective-permute-start | bytes 6782984 | tf_op jit(solution)/shard_map/ppermute | solution.py:499
  60.8 44.9 %collective-permute-start.8 = (bf16[288,1472]{1,0:T(8,128)(2,1)S(1)}, bf16[288,1472]{1,0:T(8,128)(2,1)S(1)}, u32[]{:S(2)}, u32[]{:S(2)}) collective-permute-start(bf16[288,1472]{1,0:T(8,128)(2,1)S(1)} %copy-done.19), channel_id=1, source_target_pairs={{0,1},{1,0},{2,3},{3,2},{4,5},{5,4},{6,7},{7,6},{8,9},{9,8},{10,11... | collective-permute-start | bytes 2543624 | tf_op jit(solution)/shard_map/ppermute | solution.py:499
  61.2 51.6 %collective-permute-start.10 = (bf16[224,1472]{1,0:T(8,128)(2,1)S(1)}, bf16[224,1472]{1,0:T(8,128)(2,1)S(1)}, u32[]{:S(2)}, u32[]{:S(2)}) collective-permute-start(bf16[224,1472]{1,0:T(8,128)(2,1)S(1)} %bitcast.92), channel_id=1, source_target_pairs={{0,1},{1,0},{2,3},{3,2},{4,5},{5,4},{6,7},{7,6},{8,9},{9,8},{10,11... | collective-permute-start | bytes 1978376 | tf_op jit(solution)/shard_map/ppermute | solution.py:499
  62.8 50.0 %collective-permute-start.9 = (bf16[224,1472]{1,0:T(8,128)(2,1)S(1)}, bf16[224,1472]{1,0:T(8,128)(2,1)S(1)}, u32[]{:S(2)}, u32[]{:S(2)}) collective-permute-start(bf16[224,1472]{1,0:T(8,128)(2,1)S(1)} %bitcast.93), channel_id=1, source_target_pairs={{0,16},{1,17},{2,18},{3,19},{4,20},{5,21},{6,22},{7,23},{8,24},{9,... | collective-permute-start | bytes 1978376 | tf_op jit(solution)/shard_map/ppermute | solution.py:499
  66.0 39.7 %collective-permute-start.11 = (bf16[112,1472]{1,0:T(8,128)(2,1)S(1)}, bf16[112,1472]{1,0:T(8,128)(2,1)S(1)}, u32[]{:S(2)}, u32[]{:S(2)}) collective-permute-start(bf16[112,1472]{1,0:T(8,128)(2,1)S(1)} %copy-done.29), channel_id=1, source_target_pairs={{0,1},{1,0},{2,3},{3,2},{4,5},{5,4},{6,7},{7,6},{8,9},{9,8},{10,11... | collective-permute-start | bytes 989192 | tf_op jit(solution)/shard_map/ppermute | solution.py:499
  117.4 16.6 %collective-permute-start.14 = (bf16[12,64,1472]{2,1,0:T(8,128)(2,1)S(1)}, bf16[12,64,1472]{2,1,0:T(8,128)(2,1)S(1)}, u32[]{:S(2)}, u32[]{:S(2)}) collective-permute-start(bf16[12,64,1472]{2,1,0:T(8,128)(2,1)S(1)} %bitcast.71), channel_id=1, source_target_pairs={{0,2},{1,3},{2,0},{3,1},{4,6},{5,7},{6,4},{7,5},{8,10},{9,11},{10,... | collective-permute-start | bytes 6782984 | tf_op jit(solution)/shard_map/ppermute | solution.py:499
  134.0 16.9 %collective-permute-start.16 = (bf16[224,1472]{1,0:T(8,128)(2,1)S(1)}, bf16[224,1472]{1,0:T(8,128)(2,1)S(1)}, u32[]{:S(2)}, u32[]{:S(2)}) collective-permute-start(bf16[224,1472]{1,0:T(8,128)(2,1)S(1)} %collective-permute-done.9.refs_1_), channel_id=1, source_target_pairs={{0,1},{1,0},{2,3},{3,2},{4,5},{5,4},{6,7},{7,6},{8,9},{9,8},{10,11... | collective-permute-start | bytes 1978376 | tf_op jit(solution)/shard_map/ppermute | solution.py:499
  160.9 16.3 %collective-permute-start.19 = (bf16[6,64,1472]{2,1,0:T(8,128)(2,1)S(1)}, bf16[6,64,1472]{2,1,0:T(8,128)(2,1)S(1)}, u32[]{:S(2)}, u32[]{:S(2)}) collective-permute-start(bf16[6,64,1472]{2,1,0:T(8,128)(2,1)S(1)} %bitcast.108), channel_id=1, source_target_pairs={{0,8},{1,9},{2,6},{3,7},{4,12},{5,13},{6,2},{7,3},{8,0},{9,1},{10,... | collective-permute-start | bytes 3391496 | tf_op jit(solution)/shard_map/ppermute | solution.py:499
  198.4 16.7 %collective-permute-start.24 = (bf16[12,64,1472]{2,1,0:T(8,128)(2,1)S(1)}, bf16[12,64,1472]{2,1,0:T(8,128)(2,1)S(1)}, u32[]{:S(2)}, u32[]{:S(2)}) collective-permute-start(bf16[12,64,1472]{2,1,0:T(8,128)(2,1)S(1)} %bitcast.90), channel_id=1, source_target_pairs={{0,2},{1,3},{2,0},{3,1},{4,6},{5,7},{6,4},{7,5},{8,10},{9,11},{10,... | collective-permute-start | bytes 6782984 | tf_op jit(solution)/shard_map/ppermute | solution.py:499
  198.9 16.3 %collective-permute-start.23 = (bf16[6,64,1472]{2,1,0:T(8,128)(2,1)S(1)}, bf16[6,64,1472]{2,1,0:T(8,128)(2,1)S(1)}, u32[]{:S(2)}, u32[]{:S(2)}) collective-permute-start(bf16[6,64,1472]{2,1,0:T(8,128)(2,1)S(1)} %bitcast.116), channel_id=1, source_target_pairs={{0,8},{1,9},{2,6},{3,7},{4,12},{5,13},{6,2},{7,3},{8,0},{9,1},{10,... | collective-permute-start | bytes 3391496 | tf_op jit(solution)/shard_map/ppermute | solution.py:499
  225.3 16.2 %collective-permute-start.27 = (bf16[6,64,1472]{2,1,0:T(8,128)(2,1)S(1)}, bf16[6,64,1472]{2,1,0:T(8,128)(2,1)S(1)}, u32[]{:S(2)}, u32[]{:S(2)}) collective-permute-start(bf16[6,64,1472]{2,1,0:T(8,128)(2,1)S(1)} %bitcast.107), channel_id=1, source_target_pairs={{0,8},{1,9},{2,6},{3,7},{4,12},{5,13},{6,2},{7,3},{8,0},{9,1},{10,... | collective-permute-start | bytes 3391496 | tf_op jit(solution)/shard_map/ppermute | solution.py:499
  249.6 35.2 %collective-permute-start.29 = (bf16[16,64,1472]{2,1,0:T(8,128)(2,1)}, bf16[16,64,1472]{2,1,0:T(8,128)(2,1)}, u32[]{:S(2)}, u32[]{:S(2)}) collective-permute-start(bf16[16,64,1472]{2,1,0:T(8,128)(2,1)} %bitcast.37), channel_id=1, source_target_pairs={{0,2},{1,3},{2,0},{3,1},{4,6},{5,7},{6,4},{7,5},{8,10},{9,11},{10,... | collective-permute-start | bytes 9043976 | tf_op jit(solution)/shard_map/ppermute | solution.py:499
  251.4 33.4 %collective-permute-start.30 = (bf16[448,1472]{1,0:T(8,128)(2,1)}, bf16[448,1472]{1,0:T(8,128)(2,1)}, u32[]{:S(2)}, u32[]{:S(2)}) collective-permute-start(bf16[448,1472]{1,0:T(8,128)(2,1)} %slice.247), channel_id=1, source_target_pairs={{0,1},{1,0},{2,3},{3,2},{4,5},{5,4},{6,7},{7,6},{8,9},{9,8},{10,11... | collective-permute-start | bytes 3956744 | tf_op jit(solution)/shard_map/ppermute | solution.py:499
  253.0 23.9 %collective-permute-start.32 = (bf16[6,64,1472]{2,1,0:T(8,128)(2,1)}, bf16[6,64,1472]{2,1,0:T(8,128)(2,1)}, u32[]{:S(2)}, u32[]{:S(2)}) collective-permute-start(bf16[6,64,1472]{2,1,0:T(8,128)(2,1)} %bitcast.39), channel_id=1, source_target_pairs={{0,8},{1,9},{2,6},{3,7},{4,12},{5,13},{6,2},{7,3},{8,0},{9,1},{10,... | collective-permute-start | bytes 3391496 | tf_op jit(solution)/shard_map/ppermute | solution.py:499
  255.6 29.2 %collective-permute-start.31 = (bf16[112,1472]{1,0:T(8,128)(2,1)S(1)}, bf16[112,1472]{1,0:T(8,128)(2,1)}, u32[]{:S(2)}, u32[]{:S(2)}) collective-permute-start(bf16[112,1472]{1,0:T(8,128)(2,1)S(1)} %add_convert_fusion.6), channel_id=1, source_target_pairs={{0,16},{1,17},{2,18},{3,19},{4,20},{5,21},{6,22},{7,23},{8,24},{9,... | collective-permute-start | bytes 989192 | tf_op jit(solution)/shard_map/ppermute | solution.py:499
  258.6 47.8 %collective-permute-start.33 = (bf16[288,768]{1,0:T(8,128)(2,1)}, bf16[288,768]{1,0:T(8,128)(2,1)}, u32[]{:S(2)}, u32[]{:S(2)}) collective-permute-start(bf16[288,768]{1,0:T(8,128)(2,1)} %copy-done.27), channel_id=1, source_target_pairs={{0,1},{1,0},{2,3},{3,2},{4,5},{5,4},{6,7},{7,6},{8,9},{9,8},{10,11... | collective-permute-start | bytes 1327112 | tf_op jit(solution)/shard_map/ppermute | solution.py:499
  284.8 21.6 %all-to-all-start = ((bf16[8,160,192]{2,1,0:T(8,128)(2,1)}), bf16[8,160,192]{2,1,0:T(8,128)(2,1)}, u32[]{:S(2)}, u32[]{:S(2)}) async-start(bf16[8,160,192]{2,1,0:T(8,128)(2,1)} %bitcast.41), calls=%async_computation | async-start | bytes 1310720 | tf_op jit(solution)/shard_map/all_to_all | solution.py:522
  291.2 56.6 %collective-permute-start.40 = (bf16[192,1472]{1,0:T(8,128)(2,1)}, bf16[192,1472]{1,0:T(8,128)(2,1)}, u32[]{:S(2)}, u32[]{:S(2)}) collective-permute-start(bf16[192,1472]{1,0:T(8,128)(2,1)} %add_convert_fusion.4), channel_id=1, source_target_pairs={{0,4},{1,5},{2,10},{3,11},{4,0},{5,1},{6,14},{7,15},{8,12},{9,13},... | collective-permute-start | bytes 1695752 | tf_op jit(solution)/shard_map/ppermute | solution.py:499
  306.6 36.3 %collective-permute-start.35 = (bf16[8,64,1472]{2,1,0:T(8,128)(2,1)S(1)}, bf16[8,64,1472]{2,1,0:T(8,128)(2,1)S(1)}, u32[]{:S(2)}, u32[]{:S(2)}) collective-permute-start(bf16[8,64,1472]{2,1,0:T(8,128)(2,1)S(1)} %bitcast.113), channel_id=1, source_target_pairs={{0,8},{1,9},{2,6},{3,7},{4,12},{5,13},{6,2},{7,3},{8,0},{9,1},{10,... | collective-permute-start | bytes 4521992 | tf_op jit(solution)/shard_map/ppermute | solution.py:499
  309.6 33.3 %collective-permute-start.37 = (bf16[224,1472]{1,0:T(8,128)(2,1)S(1)}, bf16[224,1472]{1,0:T(8,128)(2,1)S(1)}, u32[]{:S(2)}, u32[]{:S(2)}) collective-permute-start(bf16[224,1472]{1,0:T(8,128)(2,1)S(1)} %add_convert_fusion.2), channel_id=1, source_target_pairs={{0,16},{1,17},{2,18},{3,19},{4,20},{5,21},{6,22},{7,23},{8,24},{9,... | collective-permute-start | bytes 1978376 | tf_op jit(solution)/shard_map/ppermute | solution.py:499
  321.1 21.8 %collective-permute-start.36 = (f32[16,1472]{1,0:T(8,128)S(1)}, f32[16,1472]{1,0:T(8,128)S(1)}, u32[]{:S(2)}, u32[]{:S(2)}) collective-permute-start(f32[16,1472]{1,0:T(8,128)S(1)} %add.190), channel_id=1, source_target_pairs={{0,8},{1,9},{2,6},{3,7},{4,12},{5,13},{6,2},{7,3},{8,0},{9,1},{10,... | collective-permute-start | bytes 282632 | tf_op jit(solution)/shard_map/ppermute | solution.py:499
  357.0 16.4 %collective-permute-start.44 = (f32[16,1472]{1,0:T(8,128)S(1)}, f32[16,1472]{1,0:T(8,128)S(1)}, u32[]{:S(2)}, u32[]{:S(2)}) collective-permute-start(f32[16,1472]{1,0:T(8,128)S(1)} %add.195), channel_id=1, source_target_pairs={{0,16},{1,17},{2,18},{3,19},{4,20},{5,21},{6,22},{7,23},{8,24},{9,... | collective-permute-start | bytes 282632 | tf_op jit(solution)/shard_map/ppermute | solution.py:499
  361.8 20.4 %collective-permute-start.43 = (bf16[104,1472]{1,0:T(8,128)(2,1)S(1)}, bf16[104,1472]{1,0:T(8,128)(2,1)S(1)}, u32[]{:S(2)}, u32[]{:S(2)}) collective-permute-start(bf16[104,1472]{1,0:T(8,128)(2,1)S(1)} %pad_maximum_fusion.11), channel_id=1, source_target_pairs={{0,17},{1,16},{2,19},{3,18},{4,21},{5,20},{6,23},{7,22},{8,25},{9,... | collective-permute-start | bytes 918536 | tf_op jit(solution)/shard_map/ppermute | solution.py:499
  364.7 17.6 %collective-permute-start.42 = (bf16[104,1472]{1,0:T(8,128)(2,1)S(1)}, bf16[104,1472]{1,0:T(8,128)(2,1)S(1)}, u32[]{:S(2)}, u32[]{:S(2)}) collective-permute-start(bf16[104,1472]{1,0:T(8,128)(2,1)S(1)} %pad_maximum_fusion.10), channel_id=1, source_target_pairs={{0,1},{1,0},{2,3},{3,2},{4,5},{5,4},{6,7},{7,6},{8,9},{9,8},{10,11... | collective-permute-start | bytes 918536 | tf_op jit(solution)/shard_map/ppermute | solution.py:499
  373.3 22.5 %collective-permute-start.41 = (bf16[104,1472]{1,0:T(8,128)(2,1)S(1)}, bf16[104,1472]{1,0:T(8,128)(2,1)S(1)}, u32[]{:S(2)}, u32[]{:S(2)}) collective-permute-start(bf16[104,1472]{1,0:T(8,128)(2,1)S(1)} %pad_maximum_fusion.9), channel_id=1, source_target_pairs={{0,16},{1,17},{2,18},{3,19},{4,20},{5,21},{6,22},{7,23},{8,24},{9,... | collective-permute-start | bytes 918536 | tf_op jit(solution)/shard_map/ppermute | solution.py:499
  (115 other events, 1583.1 us)

commit v3 on v2

--- a/solution.py
+++ b/solution.py
@@ -244,9 +244,8 @@
             dqkv_ref[:, k * INNER + at : k * INNER + at + LANES] = jnp.where(
                 left, two[0], two[1]
             ).astype(BF16)
-    col = lax.broadcasted_iota(jnp.int32, (dyt_ref.shape[0], 3 * INNER), 1)
-    plain = (plain_ref[...] == col).astype(F32).astype(BF16)
-    dyt_ref[...] = dot_nt(plain, dqkv_ref[...]).astype(BF16)
+    plain = rows_of(plain_ref, 0, plain_ref.shape[1], 0, 3 * INNER)
+    dyt_ref[...] = dot_nn(dqkv_ref[...], plain).T.astype(BF16)
     back = from_natural(dqkv_ref[...], halves, target_ref, 0)
     grad_in, gain_grad = norm_back(x_ref[...].astype(F32), gains_ref[0:1, :], back)
     gx_ref[...] = g2_ref[...] + grad_in
@@ -257,7 +256,9 @@
     d = lax.broadcasted_iota(jnp.int32, (WIDTH, rows), 1)
     by_distance = exact(diag_ref[...], (k + d == rows - 1).astype(F32), ((1,), (0,)))
     buckets = buckets_of(lookup_ref, LANES)
-    small_ref[8:16, 0:LANES] = exact(by_distance, buckets, ((1,), (1,)))
+    by_bucket = exact(by_distance, buckets, ((1,), (1,)))
+    for h in range(HEADS):
+        small_ref[3:4, h * LANES : (h + 1) * LANES] = by_bucket[h : h + 1, :]
 
 
 def memory_forward_kernel(own_ref, peer_ref, w0_ref, w1_ref, target_ref, kv_own_ref, kv_peer_ref):
@@ -344,16 +345,18 @@
 
 def weights_kernel(
     dq_ref, low_ref, own_ref, peer_ref, low1_ref, n2_ref, low3_ref, mem_own_ref, mem_peer_ref, g2_ref,
-    target_ref, one_ref, *refs,
+    target_ref, one_ref, *out_refs,
 ):
-    got_ref, out_ref = (refs[0] if len(refs) > 1 else None), refs[-1]
-
-    def spread(order_ref, at, value):
-        hot = rows_of(order_ref, 0, order_ref.shape[1], at, value.shape[1])
-        return dot_nn(value, hot).astype(BF16)
-
-    cross = dot_tn(
-        jnp.concatenate(
+    right = jnp.concatenate([n2_ref[...], low3_ref[...], mem_own_ref[...], mem_peer_ref[...]], axis=0)
+    right_out = g2_ref[...].astype(BF16)
+    for i, out_ref in enumerate(out_refs):
+
+        def spread(order_ref, first, value):
+            size = order_ref.shape[1] // 2
+            hot = rows_of(order_ref, i * size, size, first, value.shape[1])
+            return dot_nn(value, hot).astype(BF16)
+
+        left = jnp.concatenate(
             [
                 spread(target_ref, 0, dq_ref[...]),
                 spread(target_ref, 3 * INNER, low_ref[...]),
@@ -361,22 +364,14 @@
                 spread(target_ref, INNER, peer_ref[...]),
             ],
             axis=0,
-        ),
-        jnp.concatenate(
-            [n2_ref[...], low3_ref[...], mem_own_ref[...], mem_peer_ref[...]], axis=0
-        ),
-    )
-    out = dot_tn(spread(one_ref, 0, low1_ref[...]), g2_ref[...].astype(BF16))
-    wide, slim = cross.shape[0] // 4, out.shape[0] // 4
-
-    def put(at, value):
-        if got_ref is not None:
-            value = value + got_ref[at : at + value.shape[0], :].astype(F32)
-        out_ref[at : at + value.shape[0], :] = value.astype(BF16)
-
-    for k in range(4):
-        put(k * (wide + slim), cross[k * wide : (k + 1) * wide])
-        put(k * (wide + slim) + wide, out[k * slim : (k + 1) * slim])
+        )
+        cross = dot_tn(left, right).astype(BF16)
+        out = dot_tn(spread(one_ref, 0, low1_ref[...]), right_out).astype(BF16)
+        wide, slim = cross.shape[0] // 4, out.shape[0] // 4
+        for k in range(4):
+            at = k * (wide + slim)
+            out_ref[at : at + wide, :] = cross[k * wide : (k + 1) * wide]
+            out_ref[at + wide : at + wide + slim, :] = out[k * slim : (k + 1) * slim]
 
 
 def columns_kernel(at_ref, held_ref, lo_ref, hi_ref, out_ref):
@@ -434,23 +429,15 @@
 
 
 def ffn_weights_kernel(
-    count, h0_ref, h1_ref, g0_ref, g1_ref, u0_ref, u1_ref, n0_ref, n1_ref, c0_ref, c1_ref, *out_refs
+    h0_ref, h1_ref, g0_ref, g1_ref, u0_ref, u1_ref, n0_ref, n1_ref, c0_ref, c1_ref, *out_refs
 ):
     sets = (
         ((h0_ref, c0_ref), (h1_ref, c1_ref)),
         ((g0_ref, n0_ref), (g1_ref, n1_ref)),
         ((u0_ref, n0_ref), (u1_ref, n1_ref)),
     )
-    down_ref, both_ref = out_refs
-    for kind, pairs in enumerate(sets):
-        value = sum(dot_tn(left[...], right[...]) for left, right in pairs).astype(BF16)
-        if kind == 0:
-            down_ref[...] = value
-            continue
-        cols = both_ref.shape[0] // (2 * count)
-        for i in range(count):
-            at = (2 * i + kind - 1) * cols
-            both_ref[at : at + cols, :] = value[i * cols : (i + 1) * cols]
+    for out_ref, pairs in zip(out_refs, sets):
+        out_ref[...] = sum(dot_tn(left[...], right[...]) for left, right in pairs).astype(BF16)
 
 
 def on_device(
@@ -528,12 +515,6 @@
     kv_shape = shape(slots, 2 * INNER)
     down, gate, up = (pltpu.VMEM((cols, width), BF16) for _ in range(3))
 
-    def over_o(own):
-        return [own] + [permute(own, flips(o=k)) for k in range(1, n_o)]
-
-    def over_m(parts):
-        return parts + [permute(v, peer_move) for v in parts]
-
     def flat_of(at):
         return ((((at["o"] * 2 + at["a"]) * 2 + at["b"]) * 2 + at["c"]) * 2) + at["m"]
 
@@ -570,7 +551,7 @@
     om_bits = flat_of({"o": n_o - 1, "a": 0, "b": 0, "c": 0, "m": 1})
     quad_masks = masks[0, :quads]
     owner = (np.arange(8, dtype=np.int32)[:, None] * 2) | ((here & om_bits) ^ quad_masks)[None, :]
-    plain = target_of(owner.reshape(-1), 40).reshape(-1, 1)
+    plain = target_of(owner.reshape(-1), 40).reshape(1, -1)
     eight_at = ((here ^ mask[::quads]) // 2) % 8
     both = jnp.concatenate([v[:piece] for v in got] + [v[piece:] for v in got], axis=0)
     cot_1 = grow(cotangent, first_move)
@@ -582,12 +563,10 @@
         half = held.shape[0] // 2
         return [jnp.concatenate([held[at : at + half], got[at : at + half]], axis=0) for at in (0, half)]
 
-    both, cot_1, peer_keep, memory, own_down, target, one, plain, eight_at = stage(
-        (both, cot_1, peer_keep, memory, ffn_down, target, one, plain, eight_at)
-    )
-    targets, ones = (jnp.split(v, 2, axis=1) for v in (target, one))
+    both, cot_1, peer_keep, memory, target, one, plain, eight_at, own_down = stage(
+        (both, cot_1, peer_keep, memory, target, one, plain, eight_at, ffn_down)
+    )
     both = jnp.concatenate(two_halves(both, permute(both, first_move)), axis=0)
-    down_o = over_o(own_down)
     peer_memory = permute(memory, peer_move)
     lookup = distance_bucket_lookup.reshape(1, -1)
     ring, items_col, items_row, slot, own_1 = kernel_call(
@@ -600,27 +579,31 @@
         tokens, norm_gains, scalars=3,
     )
 
-    both, down_o, own_gu, ring, own_1 = stage((both, down_o, own_gu, ring, own_1))
+    def over_o(own):
+        return [own] + [permute(own, flips(o=k)) for k in range(1, n_o)]
+
+    def over_m(parts, own_m):
+        return parts + [own_m] + [permute(v, peer_move) for v in parts[1:]]
+
+    down_o, down_m = over_o(own_down), permute(own_down, peer_move)
+
+    both, ring, own_1, own_gu, down_o, down_m = stage((both, ring, own_1, own_gu, down_o, down_m))
     self_lo, cross_lo = two_halves(both, permute(both, second_move))
-    w_down = over_m(down_o)
-    gu_o = over_o(own_gu)
-    gu_m = permute(own_gu, peer_move)
-
-    self_lo, cross_lo, peer_memory, cot_1, gu_o, gu_m, w_down, target = stage(
-        (self_lo, cross_lo, peer_memory, cot_1, gu_o, gu_m, w_down, target)
+    gu_o, gu_m = over_o(own_gu), permute(own_gu, peer_move)
+    w_down = over_m(down_o, down_m)
+
+    self_lo, cross_lo, peer_memory, gu_o, gu_m, target, w_down = stage(
+        (self_lo, cross_lo, peer_memory, gu_o, gu_m, target, w_down)
     )
     w_self = (self_lo, permute(self_lo, core_move))
-
-    w_self, cross_lo, cot_1 = stage((w_self, cross_lo, cot_1))
+    w_cross = (cross_lo, permute(cross_lo, core_move))
+
+    w_self, w_cross, cot_1, gu_o = stage((w_self, w_cross, cot_1, gu_o))
     x_2, n_2, qkv, low_1 = kernel_call(
         self_forward_kernel,
         [shape(*full, kind=F32), shape(*full), shape(rows, 3 * INNER), shape(*slim)],
         tokens, own_1, norm_gains, *w_self, target, ring, items_col, items_row,
     )
-    w_cross = (cross_lo, permute(cross_lo, core_move))
-    cot_lo = grow(cot_1, second_move)
-
-    x_2, w_cross, gu_o = stage((x_2, w_cross, gu_o))
     kv_own, kv_peer = kernel_call(
         memory_forward_kernel, [kv_shape] * 2, memory, peer_memory, *w_cross, target
     )
@@ -629,7 +612,8 @@
         [shape(*full, kind=F32), shape(*full), shape(*slim), shape(*slim)],
         x_2, n_2, norm_gains, *w_cross, target, kv_own, kv_peer, items_col, slot,
     )
-    w_gu = gu_o + [gu_m] + [permute(v, peer_move) for v in gu_o[1:]]
+    cot_lo = grow(cot_1, second_move)
+    w_gu = over_m(gu_o, gu_m)
 
     x_3, n_3, cot_lo, w_gu = stage((x_3, n_3, cot_lo, w_gu))
     n_1 = grow(n_3, first_move)
@@ -637,12 +621,12 @@
 
     def grad_hidden(value):
         return kernel_call(
-            grad_hidden_kernel, shape(half, cols, kind=F32), value, *w_down, scratch=[down]
+            grad_hidden_kernel, shape(half, cols, kind=F32), value, *w_down, scratch=[down], us=2
         )
 
     gh_lo = grad_hidden(cot_lo)
 
-    n_1, cot_hi, gh_lo = stage((n_1, cot_hi, gh_lo))
+    n_1, cot_hi, gh_lo, own_1 = stage((n_1, cot_hi, gh_lo, own_1))
     n_lo = grow(n_1, second_move)
     gh_hi = grad_hidden(cot_hi)
 
@@ -658,14 +642,16 @@
     lo_f = ffn(n_lo, gh_lo)
     one_1 = grow(own_1, first_move)
 
-    n_hi, lo_f, one_1 = stage((n_hi, lo_f, one_1))
+    n_hi, lo_f = stage((n_hi, lo_f))
     hi_f = ffn(n_hi, gh_hi)
 
-    (h_lo, g_lo, u_lo, gn_lo), (h_hi, g_hi, u_hi, gn_hi), one_1 = stage((lo_f, hi_f, one_1))
+    (h_lo, g_lo, u_lo, gn_lo), (h_hi, g_hi, u_hi, gn_hi) = stage((lo_f, hi_f))
     got_c = permute(gn_hi, core_move)
 
     def ffn_out(*args):
-        return kernel_call(ffn_out_kernel, shape(half, width), *args, *w_down, scratch=[down])
+        return kernel_call(
+            ffn_out_kernel, shape(half, width), *args, *w_down, scratch=[down], us=2
+        )
 
     out_hi = ffn_out(h_hi)
 
@@ -675,18 +661,31 @@
     got_c, out_hi, h_lo = stage((got_c, out_hi, h_lo))
     got_2 = permute(summed(2 * rows, 4 * rows, gn_lo, got_c), second_move)
     out_got = permute(out_hi, core_move)
-    grad_down, grad_gu = kernel_call(
-        lambda *refs: ffn_weights_kernel(quads, *refs),
-        [shape(cols, width), shape(2 * cols, width)],
+    grad_down, grad_gate, grad_up = kernel_call(
+        ffn_weights_kernel,
+        [shape(cols, width)] * 3,
         h_lo, h_hi, g_lo, g_hi, u_lo, u_hi, n_lo, n_hi, cot_lo, cot_hi,
     )
 
-    got_2, out_got, grad_down, grad_gu, one_1 = stage((got_2, out_got, grad_down, grad_gu, one_1))
+    got_2, out_got, grad_down = stage((got_2, out_got, grad_down))
     got_1 = permute(summed(rows, 2 * rows, gn_lo, got_c, got_2), first_move)
     out_lo = ffn_out(h_lo, out_got)
-    down_m = permute(grad_down[cols // 2 :], peer_move)
-
-    got_1, out_lo, grad_gu, one_1 = stage((got_1, out_lo, grad_gu, one_1))
+
+    def over_m_back(grad):
+        return permute(grad[cols // 2 :], peer_move)
+
+    def over_o_back(grad, got):
+        return [
+            permute(summed(k * ff_rows, (k + 1) * ff_rows, grad, got), flips(o=k))
+            for k in range(1, n_o)
+        ]
+
+    def back_sum(part, *parts):
+        return sum(v[:part].astype(F32) for v in parts)
+
+    down_m = over_m_back(grad_down)
+
+    got_1, out_lo, one_1 = stage((got_1, out_lo, one_1))
     low_3, grad_2, dq, dkv_own, dkv_peer, gains_23 = kernel_call(
         cross_backward_kernel,
         [
@@ -694,84 +693,82 @@
             shape(2, width, kind=F32),
         ],
         gn_lo, got_c, got_2, got_1, x_3, x_2, norm_gains, cotangent, *w_cross, target, q_2, kv_own,
-        kv_peer, items_col, slot,
+        kv_peer, items_col, slot, us=8,
     )
     n1_lo = grow(one_1, second_move)
-    gu_m = permute(grad_gu[cols:], peer_move)
-
-    low_3, grad_2, dq, dkv_own, dkv_peer, gains_23, down_m, n1_lo = stage(
-        (low_3, grad_2, dq, dkv_own, dkv_peer, gains_23, down_m, n1_lo)
-    )
-    operands = (dq, low_2, dkv_own, dkv_peer, low_1, n_2, low_3, memory, peer_memory, grad_2)
-    stack = shape(4 * quads * (piece + 16), width)
-    sent = kernel_call(weights_kernel, stack, *operands, targets[1], ones[1])
-    n1_hi = permute(n1_lo, core_move)
-
-    def over_back(part, grad, got):
-        return [
-            permute(summed(k * part, (k + 1) * part, grad, got), flips(o=k)) for k in range(1, n_o)
-        ]
-
-    sent, grad_2, dkv_peer, n1_hi = stage((sent, grad_2, dkv_peer, n1_hi))
-    cross_c = permute(sent, core_move)
-    dkv_got = permute(dkv_peer, peer_move)
-    out_2 = permute(out_lo[2 * rows :], second_move)
+
+    grad_2, dq, down_m, grad_gate, dkv_peer = stage((grad_2, dq, down_m, grad_gate, dkv_peer))
     grad_tokens, dyt, small = kernel_call(
         self_backward_kernel,
-        [shape(*full, kind=F32), shape(8 * quads * 40, rows), shape(16, width, kind=F32)],
+        [shape(*full, kind=F32), shape(8 * quads * 40, rows), shape(4, width, kind=F32)],
         grad_2, tokens, norm_gains, *w_self, target, plain, qkv, ring, items_col, items_row, lookup,
-        gains_23, scratch=[pltpu.VMEM((rows, 3 * INNER), BF16), pltpu.VMEM((8, WIDTH), F32)],
-    )
-    down_b = over_back(ff_rows, grad_down, down_m)
-
-    cross_c, grad_tokens, dyt, small, gu_m, down_b, out_2 = stage(
-        (cross_c, grad_tokens, dyt, small, gu_m, down_b, out_2)
-    )
+        gains_23, scratch=[pltpu.VMEM((rows, 3 * INNER), BF16), pltpu.VMEM((8, WIDTH), F32)], us=8,
+    )
+    gate_m = over_m_back(grad_gate)
+
+    grad_tokens, dyt, small, n1_lo, down_m = stage((grad_tokens, dyt, small, n1_lo, down_m))
     held = exchange(dyt, GROUP, 8)
-    cross_part = kernel_call(weights_kernel, stack, *operands, targets[0], ones[0], cross_c)
+    stack = shape(4 * quads * (piece + 16), width)
+    kept, sent = kernel_call(
+        weights_kernel, [stack] * 2,
+        dq, low_2, dkv_own, dkv_peer, low_1, n_2, low_3, memory, peer_memory, grad_2, target, one, us=10,
+    )
+    n1_hi = permute(n1_lo, core_move)
     small = small + permute(small, core_move)
-    gu_b = over_back(2 * ff_rows, grad_gu, gu_m)
-
-    held, cross_part, dkv_got, small = stage((held, cross_part, dkv_got, small))
-    quarter = cross_part.shape[0] // 4
-    cross_2 = permute(cross_part[2 * quarter :], second_move)
+    down_b = over_o_back(grad_down, down_m)
+
+    held, sent, small, n1_hi, gate_m, grad_up, out_lo, dkv_peer = stage(
+        (held, sent, small, n1_hi, gate_m, grad_up, out_lo, dkv_peer)
+    )
+    cross_c = permute(sent, core_move)
     part_self = kernel_call(
-        columns_kernel, shape(quads * 40, width), eight_at, held, n1_lo, n1_hi, scalars=1
-    )
-    small = small + permute(small, second_move)
-
-    cross_2, part_self, small, gu_b = stage((cross_2, part_self, small, gu_b))
-    cross_1 = permute(summed(quarter, 2 * quarter, cross_part, cross_2), first_move)
-    out_1 = permute(summed(rows, 2 * rows, out_lo, out_2), first_move)
+        columns_kernel, shape(quads * 40, width), eight_at, held, n1_lo, n1_hi, scalars=1, us=2
+    )
+    out_2 = permute(out_lo[2 * rows :], second_move)
+    small = small + sum(permute(small, flips(a=k // 2, b=k % 2)) for k in range(1, 4))
+    up_m = over_m_back(grad_up)
+    dkv_got = permute(dkv_peer, peer_move)
+
+    cross_c, part_self, down_b, out_2, dkv_got = stage((cross_c, part_self, down_b, out_2, dkv_got))
+    quarter = kept.shape[0] // 4
+    cross_2 = permute(summed(2 * quarter, 4 * quarter, kept, cross_c), second_move)
+    self_got = [permute(part_self[k * 40 + 40 : k * 40 + 80], move) for k, move in enumerate(moves)]
+    gate_b = over_o_back(grad_gate, gate_m)
+    sum_down = back_sum(ff_rows, grad_down, down_m, *down_b)
+
+    cross_2, self_got, small, up_m, dkv_got, sum_down = stage(
+        (cross_2, self_got, small, up_m, dkv_got, sum_down)
+    )
+    cross_1 = permute(summed(quarter, 2 * quarter, kept, cross_c, cross_2), first_move)
+    small_got = [permute(small, move) for move in moves]
+    up_b = over_o_back(grad_up, up_m)
     grad_memory = kernel_call(
         memory_backward_kernel, shape(slots, width, kind=F32), dkv_own, dkv_got, *w_cross, target
     )
-    small = small + permute(small, first_move)
-
-    cross_1, small, grad_memory, out_1 = stage((cross_1, small, grad_memory, out_1))
-    cross_sum = cross_part[:quarter] + cross_2[:quarter].astype(F32) + cross_1.astype(F32)
+    sum_self = back_sum(40, part_self, *self_got)
+
+    cross_1, small_got, gate_b, sum_self, grad_memory = stage(
+        (cross_1, small_got, gate_b, sum_self, grad_memory)
+    )
 
     def pieces(k):
-        at, end = k * piece, wide + k * 16
         return jnp.concatenate(
-            [cross_sum[at : at + piece], cross_sum[end : end + 16], part_self[k * 40 : k * 40 + 40]],
+            [
+                sum(v[at:end].astype(F32) for v in (kept, cross_c, cross_2, cross_1))
+                for at, end in ((k * piece, k * piece + piece), (wide + k * 16, wide + k * 16 + 16))
+            ],
             axis=0,
         )
 
     pieces_got = [permute(pieces(k + 1).astype(BF16), move) for k, move in enumerate(moves)]
-    small_got = [permute(small, move) for move in moves]
+    out_1 = permute(summed(rows, 2 * rows, out_lo, out_2), first_move)
+    sum_gate = back_sum(ff_rows, grad_gate, gate_m, *gate_b)
+    small = small + sum(small_got)
+
+    pieces_got, out_1, sum_gate, up_b, small = stage((pieces_got, out_1, sum_gate, up_b, small))
+    sum_cross = pieces(0) + sum(g.astype(F32) for g in pieces_got)
+    sum_up = back_sum(ff_rows, grad_up, up_m, *up_b)
     block_out = summed(0, rows, x_3, out_lo, out_2, out_1)
-
-    pieces_got, small_got, block_out = stage((pieces_got, small_got, block_out))
-    total = pieces(0) + sum(g.astype(F32) for g in pieces_got)
-    small = small + sum(small_got)
-    sum_cross, sum_self = total[: piece + 16], total[piece + 16 :]
-
-    def back_sum(part, *parts):
-        return sum(v[:part].astype(F32) for v in parts)
-
-    sum_down = back_sum(ff_rows, grad_down, down_m, *down_b)
-    sum_gu = back_sum(2 * ff_rows, grad_gu, gu_m, *gu_b)
 
     def three(total):
         query, key, value = (total[k * part_rows : (k + 1) * part_rows] for k in range(3))
@@ -779,7 +776,7 @@
 
     squery, skv = three(sum_self)
     cquery, ckv = three(sum_cross)
-    fin = jnp.swapaxes(sum_gu.reshape(2, ff_rows, width), 1, 2)
+    fin = jnp.swapaxes(jnp.stack([sum_gate, sum_up]), 1, 2)
     base = 4 * part_rows
     return (
         block_out,
@@ -794,7 +791,7 @@
         fin,
         sum_down,
         small[:3],
-        small[8 : 8 + HEADS, : rel_bias.shape[0]].T,
+        small[3, : HEADS * LANES].reshape(HEADS, LANES)[:, : rel_bias.shape[0]].T,
     )
 
 

time: 405 us -> 379 us (0.936)
  waiting for transfers between devices: 207 us -> 183 us
  starting transfers between devices: 57.8 us -> 68.7 us
  local copies, waits for them, and re-layouts: 35.2 us -> 30 us
    ppermute x47 -> x53, waiting for transfers between devices: 207 us -> 183 us  [permute(): return lax.ppermute(cut(value), AXES, pairs).reshape(value.shape)]
    ppermute x47 -> x53, starting transfers between devices: 53.6 us -> 64.2 us  [permute(): return lax.ppermute(cut(value), AXES, pairs).reshape(value.shape)]
    pallas_call x18 -> x17, Pallas kernels: 79 us -> 75.2 us  [kernel_call(): pl.pallas_call(kernel, out_shape=out_shape, in_specs=[pl.BlockSpec(memory...]
    unnamed x208 -> x176, local copies, waits for them, and re-layouts: 26 us -> 23.4 us
  transfers between devices with their start and end apart: 48 -> 54, of which waited for: 23 -> 20; matrix products, arithmetic and copies ran while one was open for 6% -> 5% of each run, Pallas kernels for 18% -> 18%
where the time goes in v3:
time: 379 us; the launch traced here: 375 us
  waiting for transfers between devices  183 us (48%)
  Pallas kernels  75.2 us (20%)
  starting transfers between devices  68.7 us (18%)
  local copies, waits for them, and re-layouts  30 us (8%)
  other arithmetic  14.8 us (4%)
    ppermute x53, waiting for transfers between devices, permute(): return lax.ppermute(cut(value), AXES, pairs).reshape(value.shape)  183 us
    pallas_call x17, Pallas kernels, kernel_call(): pl.pallas_call(kernel, out_shape=out_shape, in_specs=[pl.BlockSpec(memory...  75.2 us
    ppermute x53, starting transfers between devices, permute(): return lax.ppermute(cut(value), AXES, pairs).reshape(value.shape)  64.2 us
    unnamed x176, local copies, waits for them, and re-layouts  23.4 us
  transfers between devices with their start and end apart: 54, of which 20 were waited for; matrix products, arithmetic and copies ran while one was open for 5% of the time, Pallas kernels for 18%

profile of v3, /device:TPU:0, one launch (start us, length us, event | category | flops | bytes accessed | tf_op | source)
XLA Modules:
  0.0 374.6 jit_solution(11727009705123009098)
XLA Ops:
  6.5 5.1 %collective-permute-start.2 = (bf16[96,1472]{1,0:T(8,128)(2,1)S(1)}, bf16[96,1472]{1,0:T(8,128)(2,1)S(1)}, u32[]{:S(2)}, u32[]{:S(2)}) collective-permute-start(bf16[96,1472]{1,0:T(8,128)(2,1)S(1)} %shard_map.336), channel_id=1, source_target_pairs={{0,17},{1,16},{2,19},{3,18},{4,21},{5,20},{6,23},{7,22},{8,25},{9,... | collective-permute-start | bytes 847880 | tf_op jit(solution)/shard_map/ppermute | solution.py:486
  16.3 21.3 %collective-permute-done = bf16[96,1472]{1,0:T(8,128)(2,1)S(1)} collective-permute-done((bf16[96,1472]{1,0:T(8,128)(2,1)S(1)}, bf16[96,1472]{1,0:T(8,128)(2,1)S(1)}, u32[]{:S(2)}, u32[]{:S(2)}) %collective-permute-start) | collective-permute-done | bytes 282656 | tf_op jit(solution)/shard_map/ppermute | solution.py:486
  45.9 13.0 %collective-permute-done.5 = bf16[6,64,1472]{2,1,0:T(8,128)(2,1)} collective-permute-done((bf16[6,64,1472]{2,1,0:T(8,128)(2,1)S(1)}, bf16[6,64,1472]{2,1,0:T(8,128)(2,1)}, u32[]{:S(2)}, u32[]{:S(2)}) %collective-permute-start.5) | collective-permute-done | bytes 1130528 | tf_op jit(solution)/shard_map/ppermute | solution.py:486
  67.3 36.9 %collective-permute-done.8 = bf16[12,64,1472]{2,1,0:T(8,128)(2,1)S(1)} collective-permute-done((bf16[12,64,1472]{2,1,0:T(8,128)(2,1)S(1)}, bf16[12,64,1472]{2,1,0:T(8,128)(2,1)S(1)}, u32[]{:S(2)}, u32[]{:S(2)}) %collective-permute-start.8) | collective-permute-done | bytes 2261024 | tf_op jit(solution)/shard_map/ppermute | solution.py:486
  106.2 4.0 %collective-permute-done.14 = bf16[12,64,1472]{2,1,0:T(8,128)(2,1)S(1)} collective-permute-done((bf16[12,64,1472]{2,1,0:T(8,128)(2,1)S(1)}, bf16[12,64,1472]{2,1,0:T(8,128)(2,1)S(1)}, u32[]{:S(2)}, u32[]{:S(2)}) %collective-permute-start.14) | collective-permute-done | bytes 2261024 | tf_op jit(solution)/shard_map/ppermute | solution.py:486
  110.2 3.4 collective-permute-done.13
  116.0 4.7 %shard_map.339 = (bf16[288,768]{1,0:T(8,128)(2,1)S(1)}, bf16[288,768]{1,0:T(8,128)(2,1)S(1)}) custom-call(bf16[288,1472]{1,0:T(8,128)(2,1)S(1)} %copy-done.25, bf16[288,1472]{1,0:T(8,128)(2,1)S(1)} %collective-permute-done.9.peer_ref.mem_peer_ref, bf16[768,1472]{1,0:T(8,128)(2,1)S(1)} %get-tuple-element.195.w0_ref, bf16[768,1472]{1,0:T(8,128)(2,1)S(1)} %bitcast.82, ...), custom_call_target="tpu_custom_call" | custom-call | flops 5000000000 | bytes 1 | tf_op jit(solution)/shard_map/pallas_call | solution.py:41
  120.7 5.6 %shard_map.338 = (f32[192,1472]{1,0:T(8,128)S(1)}, bf16[192,1472]{1,0:T(8,128)(2,1)S(1)}, bf16[192,1152]{1,0:T(8,128)(2,1)S(1)}, bf16[192,384]{1,0:T(8,128)(2,1)S(1)}) custom-call(bf16[192,1472]{1,0:T(8,128)(2,1)S(1)} %copy-done.31, bf16[192,1472]{1,0:T(8,128)(2,1)S(1)} %get-tuple-element.251.n1_ref, f32[3,1472]{1,0:T(4,128)S(1)} %copy-done.41, ...), custom_call_target="tpu_custom_call" | custom-call | flops 5000000000 | bytes 1 | tf_op jit(solution)/shard_map/pallas_call | solution.py:41
  126.3 6.8 %shard_map.340 = (f32[192,1472]{1,0:T(8,128)S(1)}, bf16[192,1472]{1,0:T(8,128)(2,1)S(1)}, bf16[192,384]{1,0:T(8,128)(2,1)S(1)}, bf16[192,384]{1,0:T(8,128)(2,1)S(1)}) custom-call(f32[192,1472]{1,0:T(8,128)S(1)} %get-tuple-element.193.x_ref.x2_ref, bf16[192,1472]{1,0:T(8,128)(2,1)S(1)} %get-tuple-element.194.n_ref.n2_ref, f32[3,1472]{1,0:T(4,128)S(1)} %copy-done.41, ...), custom_call_target="tpu_custom_call" | custom-call | flops 5000000000 | bytes 1 | tf_op jit(solution)/shard_map/pallas_call | solution.py:41
  136.8 7.0 %collective-permute-done.17 = bf16[192,1472]{1,0:T(8,128)(2,1)S(1)} collective-permute-done((bf16[192,1472]{1,0:T(8,128)(2,1)S(1)}, bf16[192,1472]{1,0:T(8,128)(2,1)S(1)}, u32[]{:S(2)}, u32[]{:S(2)}) %collective-permute-start.17) | collective-permute-done | bytes 565280 | tf_op jit(solution)/shard_map/ppermute | solution.py:486
  146.4 13.7 %collective-permute-done.19 = bf16[6,64,1472]{2,1,0:T(8,128)(2,1)S(1)} collective-permute-done((bf16[6,64,1472]{2,1,0:T(8,128)(2,1)S(1)}, bf16[6,64,1472]{2,1,0:T(8,128)(2,1)S(1)}, u32[]{:S(2)}, u32[]{:S(2)}) %collective-permute-start.19) | collective-permute-done | bytes 1130528 | tf_op jit(solution)/shard_map/ppermute | solution.py:486
  160.4 5.2 %shard_map.343 = (bf16[768,448]{1,0:T(8,128)(2,1)S(1)}, bf16[768,448]{1,0:T(8,128)(2,1)S(1)}, bf16[768,448]{1,0:T(8,128)(2,1)S(1)}, bf16[768,1472]{1,0:T(8,128)(2,1)S(1)}) custom-call(bf16[768,1472]{1,0:T(8,128)(2,1)S(1)} %pad_maximum_fusion.4.n_ref.n0_ref, f32[768,448]{1,0:T(8,128)S(1)} %shard_map.341.gh_ref, bf16[224,1472]{1,0:T(8,128)(2,1)S(1)} %bitcast.97, ...), custom_call_target="tpu_custom_call" | custom-call | flops 5000000000 | bytes 1 | tf_op jit(solution)/shard_map/pallas_call | solution.py:41
  165.7 5.2 %shard_map.344 = (bf16[768,448]{1,0:T(8,128)(2,1)S(1)}, bf16[768,448]{1,0:T(8,128)(2,1)S(1)}, bf16[768,448]{1,0:T(8,128)(2,1)S(1)}, bf16[768,1472]{1,0:T(8,128)(2,1)S(1)}) custom-call(bf16[768,1472]{1,0:T(8,128)(2,1)S(1)} %bitcast.91, f32[768,448]{1,0:T(8,128)S(1)} %shard_map.342.gh_ref, bf16[224,1472]{1,0:T(8,128)(2,1)S(1)} %bitcast.98, ...), custom_call_target="tpu_custom_call" | custom-call | flops 5000000000 | bytes 1 | tf_op jit(solution)/shard_map/pallas_call | solution.py:41
  178.2 6.6 %shard_map.346 = (bf16[448,1472]{1,0:T(8,128)(2,1)S(1)}, bf16[448,1472]{1,0:T(8,128)(2,1)S(1)}, bf16[448,1472]{1,0:T(8,128)(2,1)S(1)}) custom-call(bf16[768,448]{1,0:T(8,128)(2,1)S(1)} %get-tuple-element.243.h0_ref.h_ref, bf16[768,448]{1,0:T(8,128)(2,1)S(1)} %get-tuple-element.239.h_ref.h1_ref, bf16[768,448]{1,0:T(8,128)(2,1)S(1)} %get-tuple-element.244.g0_ref, ...), custom_call_target="tpu_custom_call" | custom-call | flops 5000000000 | bytes 1 | tf_op jit(solution)/shard_map/pallas_call | solution.py:41
  184.8 14.2 %collective-permute-done.22 = bf16[6,64,1472]{2,1,0:T(8,128)(2,1)S(1)} collective-permute-done((bf16[6,64,1472]{2,1,0:T(8,128)(2,1)S(1)}, bf16[6,64,1472]{2,1,0:T(8,128)(2,1)S(1)}, u32[]{:S(2)}, u32[]{:S(2)}) %collective-permute-start.22) | collective-permute-done | bytes 1130528 | tf_op jit(solution)/shard_map/ppermute | solution.py:486
  206.2 4.3 %collective-permute-done.24.got_ref = bf16[192,1472]{1,0:T(8,128)(2,1)S(1)} collective-permute-done((bf16[192,1472]{1,0:T(8,128)(2,1)S(1)}, bf16[192,1472]{1,0:T(8,128)(2,1)S(1)}, u32[]{:S(2)}, u32[]{:S(2)}) %collective-permute-start.24) | collective-permute-done | bytes 565280 | tf_op jit(solution)/shard_map/ppermute | solution.py:486
  211.3 9.0 %shard_map.348 = (bf16[192,1472]{1,0:T(8,128)(2,1)S(1)}, f32[192,1472]{1,0:T(8,128)S(1)}, bf16[192,384]{1,0:T(8,128)(2,1)S(1)}, bf16[288,768]{1,0:T(8,128)(2,1)S...) custom-call(bf16[768,1472]{1,0:T(8,128)(2,1)S(1)} %get-tuple-element.237.lo_ref, ...), custom_call_target="tpu_custom_call" | custom-call | flops 8000000000 | bytes 1 | tf_op jit(solution)/shard_map/pallas_call | solution.py:41
  220.4 9.5 %shard_map.349 = (f32[192,1472]{1,0:T(8,128)}, bf16[1280,192]{1,0:T(8,128)(2,1)}, f32[4,1472]{1,0:T(4,128)S(1)}) custom-call(f32[192,1472]{1,0:T(8,128)S(1)} %get-tuple-element.259.g2_ref, bf16[192,1472]{1,0:T(8,128)(2,1)S(1)} %copy-done.31, f32[3,1472]{1,0:T(4,128)S(1)} %copy-done.41, bf16[768,1472]{1,0:T(8,128)(2,1)S(1)} %get-tuple-element.187.w0_ref, ...), custom_call_target="tpu_custom_call" | custom-call | flops 8000000000 | bytes 1 | tf_op jit(solution)/shard_map/pallas_call | solution.py:41
  234.0 4.5 %all-to-all-start = ((bf16[8,160,192]{2,1,0:T(8,128)(2,1)}), bf16[8,160,192]{2,1,0:T(8,128)(2,1)}, u32[]{:S(2)}, u32[]{:S(2)}) async-start(bf16[8,160,192]{2,1,0:T(8,128)(2,1)} %bitcast.35), calls=%async_computation | async-start | bytes 1310720 | tf_op jit(solution)/shard_map/all_to_all | solution.py:509
  247.6 8.0 %shard_map.350 = (bf16[1024,1472]{1,0:T(8,128)(2,1)S(1)}, bf16[1024,1472]{1,0:T(8,128)(2,1)S(1)}) custom-call(bf16[192,384]{1,0:T(8,128)(2,1)S(1)} %copy-done.67, bf16[192,384]{1,0:T(8,128)(2,1)S(1)} %copy-done.63, bf16[288,768]{1,0:T(8,128)(2,1)S(1)} %copy-done.56, bf16[288,768]{1,0:T(8,128)(2,1)S(1)} %copy-done.33, bf16[192,384]{1,0:T(8,128)(2,1)S(1)} %copy-done.65, ...), custom_call_target="tpu_custom_call" | custom-call | flops 10000000000 | bytes 1 | tf_op jit(solution)/shard_map/pallas_call | solution.py:41
  262.1 3.3 collective-permute-start.32
  268.5 3.8 %shard_map.351 = bf16[160,1472]{1,0:T(8,128)(2,1)S(1)} custom-call(s32[8]{0:T(128)S(1)} %and_select_fusion.at_ref, bf16[8,160,192]{2,1,0:T(8,128)(2,1)} %all-to-all-done.held_ref, bf16[768,1472]{1,0:T(8,128)(2,1)} %pad_maximum_fusion.5.lo_ref, bf16[768,1472]{1,0:T(8,128)(2,1)} %bitcast.37.hi_ref), custom_call_target="tpu_custom_call" | custom-call | flops 2000000000 | bytes 1 | tf_op jit(solution)/shard_map/pallas_call | solution.py:41
  272.3 10.4 %collective-permute-done.32 = bf16[112,1472]{1,0:T(8,128)(2,1)S(1)} collective-permute-done((bf16[112,1472]{1,0:T(8,128)(2,1)S(1)}, bf16[112,1472]{1,0:T(8,128)(2,1)S(1)}, u32[]{:S(2)}, u32[]{:S(2)}) %collective-permute-start.32) | collective-permute-done | bytes 329760 | tf_op jit(solution)/shard_map/ppermute | solution.py:486
  282.7 4.9 %collective-permute-start.40 = (f32[4,1472]{1,0:T(4,128)S(1)}, f32[4,1472]{1,0:T(4,128)S(1)}, u32[]{:S(2)}, u32[]{:S(2)}) collective-permute-start(f32[4,1472]{1,0:T(4,128)S(1)} %add.282), channel_id=1, source_target_pairs={{0,8},{1,9},{2,10},{3,11},{4,12},{5,13},{6,14},{7,15},{8,0},{9,1},... | collective-permute-start | bytes 70664 | tf_op jit(solution)/shard_map/ppermute | solution.py:486
  293.4 3.4 collective-permute-start.36
  297.9 4.5 %collective-permute-done.42 = bf16[224,1472]{1,0:T(8,128)(2,1)S(1)} collective-permute-done((bf16[224,1472]{1,0:T(8,128)(2,1)S(1)}, bf16[224,1472]{1,0:T(8,128)(2,1)S(1)}, u32[]{:S(2)}, u32[]{:S(2)}) %collective-permute-start.42) | collective-permute-done | bytes 659488 | tf_op jit(solution)/shard_map/ppermute | solution.py:486
  302.4 21.8 %collective-permute-done.38 = bf16[40,1472]{1,0:T(8,128)(2,1)S(1)} collective-permute-done((bf16[40,1472]{1,0:T(8,128)(2,1)S(1)}, bf16[40,1472]{1,0:T(8,128)(2,1)S(1)}, u32[]{:S(2)}, u32[]{:S(2)}) %collective-permute-start.38) | collective-permute-done | bytes 117792 | tf_op jit(solution)/shard_map/ppermute | solution.py:486
  326.9 9.8 %collective-permute-done.35 = bf16[8,64,1472]{2,1,0:T(8,128)(2,1)S(1)} collective-permute-done((bf16[8,64,1472]{2,1,0:T(8,128)(2,1)S(1)}, bf16[8,64,1472]{2,1,0:T(8,128)(2,1)S(1)}, u32[]{:S(2)}, u32[]{:S(2)}) %collective-permute-start.35) | collective-permute-done | bytes 1507360 | tf_op jit(solution)/shard_map/ppermute | solution.py:486
  343.5 3.4 shard_map.352
  349.4 4.1 %collective-permute-done.43 = bf16[4,64,1472]{2,1,0:T(8,128)(2,1)S(1)} collective-permute-done((bf16[4,64,1472]{2,1,0:T(8,128)(2,1)S(1)}, bf16[4,64,1472]{2,1,0:T(8,128)(2,1)S(1)}, u32[]{:S(2)}, u32[]{:S(2)}) %collective-permute-start.43) | collective-permute-done | bytes 753696 | tf_op jit(solution)/shard_map/ppermute | solution.py:486
  361.7 4.2 %collective-permute-done.48 = bf16[64,1472]{1,0:T(8,128)(2,1)S(1)} collective-permute-done((bf16[64,1472]{1,0:T(8,128)(2,1)S(1)}, bf16[64,1472]{1,0:T(8,128)(2,1)S(1)}, u32[]{:S(2)}, u32[]{:S(2)}) %collective-permute-start.48) | collective-permute-done | bytes 188448 | tf_op jit(solution)/shard_map/ppermute | solution.py:486
  365.9 3.6 collective-permute-done.50
  (330 shorter events, 107.0 us)
Async XLA Ops:
  6.5 31.1 %collective-permute-start.2 = (bf16[96,1472]{1,0:T(8,128)(2,1)S(1)}, bf16[96,1472]{1,0:T(8,128)(2,1)S(1)}, u32[]{:S(2)}, u32[]{:S(2)}) collective-permute-start(bf16[96,1472]{1,0:T(8,128)(2,1)S(1)} %shard_map.336), channel_id=1, source_target_pairs={{0,17},{1,16},{2,19},{3,18},{4,21},{5,20},{6,23},{7,22},{8,25},{9,... | collective-permute-start | bytes 847880 | tf_op jit(solution)/shard_map/ppermute | solution.py:486
  11.6 26.0 %collective-permute-start.1 = (bf16[96,1472]{1,0:T(8,128)(2,1)S(1)}, bf16[96,1472]{1,0:T(8,128)(2,1)S(1)}, u32[]{:S(2)}, u32[]{:S(2)}) collective-permute-start(bf16[96,1472]{1,0:T(8,128)(2,1)S(1)} %shard_map.336), channel_id=1, source_target_pairs={{0,1},{1,0},{2,3},{3,2},{4,5},{5,4},{6,7},{7,6},{8,9},{9,8},{10,11... | collective-permute-start | bytes 847880 | tf_op jit(solution)/shard_map/ppermute | solution.py:486
  12.1 25.5 %collective-permute-start = (bf16[96,1472]{1,0:T(8,128)(2,1)S(1)}, bf16[96,1472]{1,0:T(8,128)(2,1)S(1)}, u32[]{:S(2)}, u32[]{:S(2)}) collective-permute-start(bf16[96,1472]{1,0:T(8,128)(2,1)S(1)} %shard_map.336), channel_id=1, source_target_pairs={{0,16},{1,17},{2,18},{3,19},{4,20},{5,21},{6,22},{7,23},{8,24},{9,... | collective-permute-start | bytes 847880 | tf_op jit(solution)/shard_map/ppermute | solution.py:486
  12.2 30.4 %collective-permute-start.4 = (s32[1,288]{1,0:T(1,128)S(1)}, s32[1,288]{1,0:T(1,128)S(1)}, u32[]{:S(2)}, u32[]{:S(2)}) collective-permute-start(s32[1,288]{1,0:T(1,128)S(1)} %reshape.246.keep_ref), channel_id=1, source_target_pairs={{0,1},{1,0},{2,3},{3,2},{4,5},{5,4},{6,7},{7,6},{8,9},{9,8},{10,11... | collective-permute-start | bytes 3464 | tf_op jit(solution)/shard_map/ppermute | solution.py:486
  13.9 26.5 %collective-permute-start.3 = (bf16[192,1472]{1,0:T(8,128)(2,1)S(1)}, bf16[192,1472]{1,0:T(8,128)(2,1)}, u32[]{:S(2)}, u32[]{:S(2)}) collective-permute-start(bf16[192,1472]{1,0:T(8,128)(2,1)S(1)} %copy-done.12), channel_id=1, source_target_pairs={{0,4},{1,5},{2,10},{3,11},{4,0},{5,1},{6,14},{7,15},{8,12},{9,13},... | collective-permute-start | bytes 1695752 | tf_op jit(solution)/shard_map/ppermute | solution.py:486
  42.6 16.3 %collective-permute-start.5 = (bf16[6,64,1472]{2,1,0:T(8,128)(2,1)S(1)}, bf16[6,64,1472]{2,1,0:T(8,128)(2,1)}, u32[]{:S(2)}, u32[]{:S(2)}) collective-permute-start(bf16[6,64,1472]{2,1,0:T(8,128)(2,1)S(1)} %bitcast.123), channel_id=1, source_target_pairs={{0,4},{1,5},{2,10},{3,11},{4,0},{5,1},{6,14},{7,15},{8,12},{9,13},... | collective-permute-start | bytes 3391496 | tf_op jit(solution)/shard_map/ppermute | solution.py:486
  60.5 43.7 %collective-permute-start.8 = (bf16[12,64,1472]{2,1,0:T(8,128)(2,1)S(1)}, bf16[12,64,1472]{2,1,0:T(8,128)(2,1)S(1)}, u32[]{:S(2)}, u32[]{:S(2)}) collective-permute-start(bf16[12,64,1472]{2,1,0:T(8,128)(2,1)S(1)} %bitcast.106), channel_id=1, source_target_pairs={{0,8},{1,9},{2,6},{3,7},{4,12},{5,13},{6,2},{7,3},{8,0},{9,1},{10,... | collective-permute-start | bytes 6782984 | tf_op jit(solution)/shard_map/ppermute | solution.py:486
  61.4 44.2 %collective-permute-start.9 = (bf16[288,1472]{1,0:T(8,128)(2,1)S(1)}, bf16[288,1472]{1,0:T(8,128)(2,1)S(1)}, u32[]{:S(2)}, u32[]{:S(2)}) collective-permute-start(bf16[288,1472]{1,0:T(8,128)(2,1)S(1)} %copy-done.25), channel_id=1, source_target_pairs={{0,1},{1,0},{2,3},{3,2},{4,5},{5,4},{6,7},{7,6},{8,9},{9,8},{10,11... | collective-permute-start | bytes 2543624 | tf_op jit(solution)/shard_map/ppermute | solution.py:486
  61.9 43.7 %collective-permute-start.11 = (bf16[224,1472]{1,0:T(8,128)(2,1)S(1)}, bf16[224,1472]{1,0:T(8,128)(2,1)S(1)}, u32[]{:S(2)}, u32[]{:S(2)}) collective-permute-start(bf16[224,1472]{1,0:T(8,128)(2,1)S(1)} %bitcast.95), channel_id=1, source_target_pairs={{0,1},{1,0},{2,3},{3,2},{4,5},{5,4},{6,7},{7,6},{8,9},{9,8},{10,11... | collective-permute-start | bytes 1978376 | tf_op jit(solution)/shard_map/ppermute | solution.py:486
  63.4 42.2 %collective-permute-start.10 = (bf16[224,1472]{1,0:T(8,128)(2,1)S(1)}, bf16[224,1472]{1,0:T(8,128)(2,1)S(1)}, u32[]{:S(2)}, u32[]{:S(2)}) collective-permute-start(bf16[224,1472]{1,0:T(8,128)(2,1)S(1)} %bitcast.96), channel_id=1, source_target_pairs={{0,16},{1,17},{2,18},{3,19},{4,20},{5,21},{6,22},{7,23},{8,24},{9,... | collective-permute-start | bytes 1978376 | tf_op jit(solution)/shard_map/ppermute | solution.py:486
  66.6 39.0 %collective-permute-start.12 = (bf16[112,1472]{1,0:T(8,128)(2,1)S(1)}, bf16[112,1472]{1,0:T(8,128)(2,1)S(1)}, u32[]{:S(2)}, u32[]{:S(2)}) collective-permute-start(bf16[112,1472]{1,0:T(8,128)(2,1)S(1)} %collective-permute-done.6.refs_1_.refs_2_), channel_id=1, source_target_pairs={{0,1},{1,0},{2,3},{3,2},{4,5},{5,4},{6,7},{7,6},{8,9},{9,8},{10,11... | collective-permute-start | bytes 989192 | tf_op jit(solution)/shard_map/ppermute | solution.py:486
  113.6 20.2 %collective-permute-start.16 = (bf16[224,1472]{1,0:T(8,128)(2,1)S(1)}, bf16[224,1472]{1,0:T(8,128)(2,1)S(1)}, u32[]{:S(2)}, u32[]{:S(2)}) collective-permute-start(bf16[224,1472]{1,0:T(8,128)(2,1)S(1)} %collective-permute-done.10.refs_1_), channel_id=1, source_target_pairs={{0,1},{1,0},{2,3},{3,2},{4,5},{5,4},{6,7},{7,6},{8,9},{9,8},{10,11... | collective-permute-start | bytes 1978376 | tf_op jit(solution)/shard_map/ppermute | solution.py:486
  114.4 18.8 %collective-permute-start.15 = (bf16[6,64,1472]{2,1,0:T(8,128)(2,1)S(1)}, bf16[6,64,1472]{2,1,0:T(8,128)(2,1)S(1)}, u32[]{:S(2)}, u32[]{:S(2)}) collective-permute-start(bf16[6,64,1472]{2,1,0:T(8,128)(2,1)S(1)} %bitcast.109), channel_id=1, source_target_pairs={{0,8},{1,9},{2,6},{3,7},{4,12},{5,13},{6,2},{7,3},{8,0},{9,1},{10,... | collective-permute-start | bytes 3391496 | tf_op jit(solution)/shard_map/ppermute | solution.py:486
  175.6 23.4 %collective-permute-start.23 = (bf16[12,64,1472]{2,1,0:T(8,128)(2,1)S(1)}, bf16[12,64,1472]{2,1,0:T(8,128)(2,1)S(1)}, u32[]{:S(2)}, u32[]{:S(2)}) collective-permute-start(bf16[12,64,1472]{2,1,0:T(8,128)(2,1)S(1)} %bitcast.93), channel_id=1, source_target_pairs={{0,2},{1,3},{2,0},{3,1},{4,6},{5,7},{6,4},{7,5},{8,10},{9,11},{10,... | collective-permute-start | bytes 6782984 | tf_op jit(solution)/shard_map/ppermute | solution.py:486
  176.4 22.6 %collective-permute-start.22 = (bf16[6,64,1472]{2,1,0:T(8,128)(2,1)S(1)}, bf16[6,64,1472]{2,1,0:T(8,128)(2,1)S(1)}, u32[]{:S(2)}, u32[]{:S(2)}) collective-permute-start(bf16[6,64,1472]{2,1,0:T(8,128)(2,1)S(1)} %bitcast.126), channel_id=1, source_target_pairs={{0,8},{1,9},{2,6},{3,7},{4,12},{5,13},{6,2},{7,3},{8,0},{9,1},{10,... | collective-permute-start | bytes 3391496 | tf_op jit(solution)/shard_map/ppermute | solution.py:486
  177.6 24.1 %collective-permute-start.25 = (bf16[192,1472]{1,0:T(8,128)(2,1)S(1)}, bf16[192,1472]{1,0:T(8,128)(2,1)S(1)}, u32[]{:S(2)}, u32[]{:S(2)}) collective-permute-start(bf16[192,1472]{1,0:T(8,128)(2,1)S(1)} %get-tuple-element.251.n1_ref), channel_id=1, source_target_pairs={{0,4},{1,5},{2,10},{3,11},{4,0},{5,1},{6,14},{7,15},{8,12},{9,13},... | collective-permute-start | bytes 1695752 | tf_op jit(solution)/shard_map/ppermute | solution.py:486
  201.8 18.6 %collective-permute-start.26 = (bf16[224,1472]{1,0:T(8,128)(2,1)S(1)}, bf16[224,1472]{1,0:T(8,128)(2,1)S(1)}, u32[]{:S(2)}, u32[]{:S(2)}) collective-permute-start(bf16[224,1472]{1,0:T(8,128)(2,1)S(1)} %slice.320), channel_id=1, source_target_pairs={{0,1},{1,0},{2,3},{3,2},{4,5},{5,4},{6,7},{7,6},{8,9},{9,8},{10,11... | collective-permute-start | bytes 1978376 | tf_op jit(solution)/shard_map/ppermute | solution.py:486
  210.6 19.4 %collective-permute-start.27 = (bf16[6,64,1472]{2,1,0:T(8,128)(2,1)S(1)}, bf16[6,64,1472]{2,1,0:T(8,128)(2,1)S(1)}, u32[]{:S(2)}, u32[]{:S(2)}) collective-permute-start(bf16[6,64,1472]{2,1,0:T(8,128)(2,1)S(1)} %bitcast.110), channel_id=1, source_target_pairs={{0,8},{1,9},{2,6},{3,7},{4,12},{5,13},{6,2},{7,3},{8,0},{9,1},{10,... | collective-permute-start | bytes 3391496 | tf_op jit(solution)/shard_map/ppermute | solution.py:486
  231.6 25.7 %collective-permute-start.29 = (bf16[12,64,1472]{2,1,0:T(8,128)(2,1)}, bf16[12,64,1472]{2,1,0:T(8,128)(2,1)}, u32[]{:S(2)}, u32[]{:S(2)}) collective-permute-start(bf16[12,64,1472]{2,1,0:T(8,128)(2,1)} %bitcast.36), channel_id=1, source_target_pairs={{0,2},{1,3},{2,0},{3,1},{4,6},{5,7},{6,4},{7,5},{8,10},{9,11},{10,... | collective-permute-start | bytes 6782984 | tf_op jit(solution)/shard_map/ppermute | solution.py:486
  232.5 24.8 %collective-permute-start.30 = (bf16[224,1472]{1,0:T(8,128)(2,1)}, bf16[224,1472]{1,0:T(8,128)(2,1)}, u32[]{:S(2)}, u32[]{:S(2)}) collective-permute-start(bf16[224,1472]{1,0:T(8,128)(2,1)} %slice.321), channel_id=1, source_target_pairs={{0,1},{1,0},{2,3},{3,2},{4,5},{5,4},{6,7},{7,6},{8,9},{9,8},{10,11... | collective-permute-start | bytes 1978376 | tf_op jit(solution)/shard_map/ppermute | solution.py:486
  234.0 23.3 %all-to-all-start = ((bf16[8,160,192]{2,1,0:T(8,128)(2,1)}), bf16[8,160,192]{2,1,0:T(8,128)(2,1)}, u32[]{:S(2)}, u32[]{:S(2)}) async-start(bf16[8,160,192]{2,1,0:T(8,128)(2,1)} %bitcast.35), calls=%async_computation | async-start | bytes 1310720 | tf_op jit(solution)/shard_map/all_to_all | solution.py:509
  238.5 17.1 %collective-permute-start.28 = (f32[4,1472]{1,0:T(4,128)S(1)}, f32[4,1472]{1,0:T(4,128)S(1)}, u32[]{:S(2)}, u32[]{:S(2)}) collective-permute-start(f32[4,1472]{1,0:T(4,128)S(1)} %get-tuple-element.277), channel_id=1, source_target_pairs={{0,2},{1,3},{2,0},{3,1},{4,6},{5,7},{6,4},{7,5},{8,10},{9,11},{10,... | collective-permute-start | bytes 70664 | tf_op jit(solution)/shard_map/ppermute | solution.py:486
  257.3 33.4 %collective-permute-start.31 = (bf16[16,64,1472]{2,1,0:T(8,128)(2,1)}, bf16[16,64,1472]{2,1,0:T(8,128)(2,1)S(1)}, u32[]{:S(2)}, u32[]{:S(2)}) collective-permute-start(bf16[16,64,1472]{2,1,0:T(8,128)(2,1)} %bitcast.81), channel_id=1, source_target_pairs={{0,2},{1,3},{2,0},{3,1},{4,6},{5,7},{6,4},{7,5},{8,10},{9,11},{10,... | collective-permute-start | bytes 9043976 | tf_op jit(solution)/shard_map/ppermute | solution.py:486
  259.0 31.2 %collective-permute-start.33 = (bf16[6,64,1472]{2,1,0:T(8,128)(2,1)S(1)}, bf16[6,64,1472]{2,1,0:T(8,128)(2,1)S(1)}, u32[]{:S(2)}, u32[]{:S(2)}) collective-permute-start(bf16[6,64,1472]{2,1,0:T(8,128)(2,1)S(1)} %bitcast.127), channel_id=1, source_target_pairs={{0,8},{1,9},{2,6},{3,7},{4,12},{5,13},{6,2},{7,3},{8,0},{9,1},{10,... | collective-permute-start | bytes 3391496 | tf_op jit(solution)/shard_map/ppermute | solution.py:486
  262.1 20.5 %collective-permute-start.32 = (bf16[112,1472]{1,0:T(8,128)(2,1)S(1)}, bf16[112,1472]{1,0:T(8,128)(2,1)S(1)}, u32[]{:S(2)}, u32[]{:S(2)}) collective-permute-start(bf16[112,1472]{1,0:T(8,128)(2,1)S(1)} %add_convert_fusion.8), channel_id=1, source_target_pairs={{0,16},{1,17},{2,18},{3,19},{4,20},{5,21},{6,22},{7,23},{8,24},{9,... | collective-permute-start | bytes 989192 | tf_op jit(solution)/shard_map/ppermute | solution.py:486
  265.4 25.8 %collective-permute-start.41 = (f32[4,1472]{1,0:T(4,128)S(1)}, f32[4,1472]{1,0:T(4,128)S(1)}, u32[]{:S(2)}, u32[]{:S(2)}) collective-permute-start(f32[4,1472]{1,0:T(4,128)S(1)} %add.282), channel_id=1, source_target_pairs={{0,12},{1,13},{2,14},{3,15},{4,8},{5,9},{6,10},{7,11},{8,4},{9,5},... | collective-permute-start | bytes 70664 | tf_op jit(solution)/shard_map/ppermute | solution.py:486
  266.9 20.7 %collective-permute-start.34 = (bf16[288,768]{1,0:T(8,128)(2,1)}, bf16[288,768]{1,0:T(8,128)(2,1)S(1)}, u32[]{:S(2)}, u32[]{:S(2)}) collective-permute-start(bf16[288,768]{1,0:T(8,128)(2,1)} %copy-done.32), channel_id=1, source_target_pairs={{0,1},{1,0},{2,3},{3,2},{4,5},{5,4},{6,7},{7,6},{8,9},{9,8},{10,11... | collective-permute-start | bytes 1327112 | tf_op jit(solution)/shard_map/ppermute | solution.py:486
  291.1 45.6 %collective-permute-start.35 = (bf16[8,64,1472]{2,1,0:T(8,128)(2,1)S(1)}, bf16[8,64,1472]{2,1,0:T(8,128)(2,1)S(1)}, u32[]{:S(2)}, u32[]{:S(2)}) collective-permute-start(bf16[8,64,1472]{2,1,0:T(8,128)(2,1)S(1)} %bitcast.119), channel_id=1, source_target_pairs={{0,8},{1,9},{2,6},{3,7},{4,12},{5,13},{6,2},{7,3},{8,0},{9,1},{10,... | collective-permute-start | bytes 4521992 | tf_op jit(solution)/shard_map/ppermute | solution.py:486
  292.4 31.9 %collective-permute-start.38 = (bf16[40,1472]{1,0:T(8,128)(2,1)S(1)}, bf16[40,1472]{1,0:T(8,128)(2,1)S(1)}, u32[]{:S(2)}, u32[]{:S(2)}) collective-permute-start(bf16[40,1472]{1,0:T(8,128)(2,1)S(1)} %get-tuple-element.363), channel_id=1, source_target_pairs={{0,17},{1,16},{2,19},{3,18},{4,21},{5,20},{6,23},{7,22},{8,25},{9,... | collective-permute-start | bytes 353288 | tf_op jit(solution)/shard_map/ppermute | solution.py:486
  292.4 31.8 %collective-permute-start.37 = (bf16[40,1472]{1,0:T(8,128)(2,1)S(1)}, bf16[40,1472]{1,0:T(8,128)(2,1)S(1)}, u32[]{:S(2)}, u32[]{:S(2)}) collective-permute-start(bf16[40,1472]{1,0:T(8,128)(2,1)S(1)} %get-tuple-element.364), channel_id=1, source_target_pairs={{0,1},{1,0},{2,3},{3,2},{4,5},{5,4},{6,7},{7,6},{8,9},{9,8},{10,11... | collective-permute-start | bytes 353288 | tf_op jit(solution)/shard_map/ppermute | solution.py:486
  293.4 33.5 %collective-permute-start.36 = (bf16[40,1472]{1,0:T(8,128)(2,1)S(1)}, bf16[40,1472]{1,0:T(8,128)(2,1)S(1)}, u32[]{:S(2)}, u32[]{:S(2)}) collective-permute-start(bf16[40,1472]{1,0:T(8,128)(2,1)S(1)} %get-tuple-element.365), channel_id=1, source_target_pairs={{0,16},{1,17},{2,18},{3,19},{4,20},{5,21},{6,22},{7,23},{8,24},{9,... | collective-permute-start | bytes 353288 | tf_op jit(solution)/shard_map/ppermute | solution.py:486
  302.4 44.5 %collective-permute-start.47 = (bf16[112,1472]{1,0:T(8,128)(2,1)S(1)}, bf16[112,1472]{1,0:T(8,128)(2,1)S(1)}, u32[]{:S(2)}, u32[]{:S(2)}) collective-permute-start(bf16[112,1472]{1,0:T(8,128)(2,1)S(1)} %add_convert_fusion.7), channel_id=1, source_target_pairs={{0,16},{1,17},{2,18},{3,19},{4,20},{5,21},{6,22},{7,23},{8,24},{9,... | collective-permute-start | bytes 989192 | tf_op jit(solution)/shard_map/ppermute | solution.py:486
  (105 other events, 1000.7 us)

commit v4 on v3

--- a/solution.py
+++ b/solution.py
@@ -22,6 +22,7 @@
 AXES = ("o", "a", "b", "c", "m")
 GROUP = ("a", "b", "c")
 VMEM = 24 * 1024 * 1024
+FETCH_VMEM = 56 * 1024 * 1024
 
 
 def dot_nn(left, right):
@@ -36,15 +37,44 @@
     return lax.dot_general(left, right, (((0,), (0,)), ((), ())), preferred_element_type=F32)
 
 
-def kernel_call(kernel, out_shape, *args, scratch=(), scalars=0, us=5, vmem=VMEM):
-    spaces = [pltpu.SMEM] * scalars + [pltpu.VMEM] * (len(args) - scalars)
+class Arriving:
+    def __init__(self, ref, copy):
+        self.ref, self.copy = ref, copy
+        self.shape, self.dtype = ref.shape, ref.dtype
+
+    def __getitem__(self, at):
+        if self.copy is not None:
+            self.copy.wait()
+            self.copy = None
+        return self.ref[at]
+
+
+def kernel_call(kernel, out_shape, *args, scratch=(), scalars=0, us=5, fetch=False):
+    count = len(args) - scalars
+    body, extra, space = kernel, [], pltpu.VMEM
+    if fetch:
+        space = pl.ANY
+        extra = [pltpu.VMEM(v.shape, v.dtype) for v in args] + [pltpu.SemaphoreType.DMA((count,))]
+
+        def body(*refs):
+            sources, results, held = refs[:count], refs[count : -count - 1], refs[-count - 1 : -1]
+            operands = []
+            for i, (source, ref) in enumerate(zip(sources, held)):
+                copy = pltpu.make_async_copy(source, ref, refs[-1].at[i])
+                copy.start()
+                operands.append(Arriving(ref, copy))
+            kernel(*operands, *results)
+            for operand in operands:
+                operand[...]
+
     return pl.pallas_call(
-        kernel,
+        body,
         out_shape=out_shape,
-        in_specs=[pl.BlockSpec(memory_space=space) for space in spaces],
+        in_specs=[pl.BlockSpec(memory_space=pltpu.SMEM)] * scalars
+        + [pl.BlockSpec(memory_space=space)] * count,
         out_specs=jax.tree.map(lambda _: pl.BlockSpec(memory_space=pltpu.VMEM), out_shape),
-        scratch_shapes=list(scratch),
-        compiler_params=pltpu.CompilerParams(vmem_limit_bytes=vmem),
+        scratch_shapes=list(scratch) + extra,
+        compiler_params=pltpu.CompilerParams(vmem_limit_bytes=FETCH_VMEM if fetch else VMEM),
         cost_estimate=pl.CostEstimate(flops=us * 1_000_000_000, bytes_accessed=1, transcendentals=0),
     )(*args)
 
@@ -122,6 +152,15 @@
         term = dot_nn(hot, shard)
         total = term if total is None else total + term
     out_ref[...] = total.astype(BF16)
+
+
+def join_kernel(*refs):
+    parts, out_ref = refs[:-1], refs[-1]
+    size = parts[0].shape[0] // 2
+    for i, part in enumerate(parts):
+        for k in range(2):
+            at = (k * len(parts) + i) * size
+            out_ref[at : at + size, :] = part[k * size : (k + 1) * size, :]
 
 
 def exact(left, right, dims):
@@ -398,9 +437,8 @@
 
 def ffn_kernel(n_ref, gh_ref, *refs):
     parts, (h_ref, dg_ref, du_ref, gn_ref, wg_ref, wu_ref) = refs[:-6], refs[-6:]
-    cols = parts[0].shape[0] // 2
-    assemble([part.at[:cols, :] for part in parts], wg_ref)
-    assemble([part.at[cols:, :] for part in parts], wu_ref)
+    assemble(parts[: len(parts) // 2], wg_ref)
+    assemble(parts[len(parts) // 2 :], wu_ref)
     n = n_ref[...]
     gate = dot_nt(n, wg_ref[...])
     up = dot_nt(n, wu_ref[...])
@@ -539,7 +577,7 @@
 
     own_both = kernel_call(
         shards_kernel, shape(2 * piece, width), self_query.T, jnp.transpose(self_kv, (2, 0, 1)), self_out,
-        cross_query.T, jnp.transpose(cross_key_value, (2, 0, 1)), cross_out, us=2,
+        cross_query.T, jnp.transpose(cross_key_value, (2, 0, 1)), cross_out, us=2, fetch=True,
     )
     got = [own_both] + [permute(own_both, move) for move in moves]
     here, at_core = after((flat_of(me), me["c"]), own_both)
@@ -553,11 +591,11 @@
     owner = (np.arange(8, dtype=np.int32)[:, None] * 2) | ((here & om_bits) ^ quad_masks)[None, :]
     plain = target_of(owner.reshape(-1), 40).reshape(1, -1)
     eight_at = ((here ^ mask[::quads]) // 2) % 8
-    both = jnp.concatenate([v[:piece] for v in got] + [v[piece:] for v in got], axis=0)
+    both = kernel_call(join_kernel, shape(2 * quads * piece, width), *got, us=1)
     cot_1 = grow(cotangent, first_move)
     keep = keep_mask.reshape(1, -1)
     peer_keep = permute(keep, peer_move)
-    own_gu = jnp.swapaxes(ffn_in, 1, 2).reshape(2 * ff_rows, width)
+    own_gate, own_up = jnp.swapaxes(ffn_in, 1, 2)
 
     def two_halves(held, got):
         half = held.shape[0] // 2
@@ -587,18 +625,21 @@
 
     down_o, down_m = over_o(own_down), permute(own_down, peer_move)
 
-    both, ring, own_1, own_gu, down_o, down_m = stage((both, ring, own_1, own_gu, down_o, down_m))
+    both, ring, own_1, own_gate, down_o, down_m = stage(
+        (both, ring, own_1, own_gate, down_o, down_m)
+    )
     self_lo, cross_lo = two_halves(both, permute(both, second_move))
-    gu_o, gu_m = over_o(own_gu), permute(own_gu, peer_move)
+    gate_o, gate_m = over_o(own_gate), permute(own_gate, peer_move)
     w_down = over_m(down_o, down_m)
 
-    self_lo, cross_lo, peer_memory, gu_o, gu_m, target, w_down = stage(
-        (self_lo, cross_lo, peer_memory, gu_o, gu_m, target, w_down)
-    )
+    self_lo, cross_lo, peer_memory, gate_o, gate_m, target, w_down, own_up = stage(
+        (self_lo, cross_lo, peer_memory, gate_o, gate_m, target, w_down, own_up)
+    )
+    up_o, up_m = over_o(own_up), permute(own_up, peer_move)
     w_self = (self_lo, permute(self_lo, core_move))
     w_cross = (cross_lo, permute(cross_lo, core_move))
 
-    w_self, w_cross, cot_1, gu_o = stage((w_self, w_cross, cot_1, gu_o))
+    w_self, w_cross, cot_1, gate_o = stage((w_self, w_cross, cot_1, gate_o))
     x_2, n_2, qkv, low_1 = kernel_call(
         self_forward_kernel,
         [shape(*full, kind=F32), shape(*full), shape(rows, 3 * INNER), shape(*slim)],
@@ -613,9 +654,10 @@
         x_2, n_2, norm_gains, *w_cross, target, kv_own, kv_peer, items_col, slot,
     )
     cot_lo = grow(cot_1, second_move)
-    w_gu = over_m(gu_o, gu_m)
-
-    x_3, n_3, cot_lo, w_gu = stage((x_3, n_3, cot_lo, w_gu))
+    w_gate = over_m(gate_o, gate_m)
+
+    x_3, n_3, cot_lo, w_gate, up_o, up_m = stage((x_3, n_3, cot_lo, w_gate, up_o, up_m))
+    w_up = over_m(up_o, up_m)
     n_1 = grow(n_3, first_move)
     cot_hi = permute(cot_lo, core_move)
 
@@ -626,7 +668,7 @@
 
     gh_lo = grad_hidden(cot_lo)
 
-    n_1, cot_hi, gh_lo, own_1 = stage((n_1, cot_hi, gh_lo, own_1))
+    n_1, cot_hi, gh_lo, own_1, w_up = stage((n_1, cot_hi, gh_lo, own_1, w_up))
     n_lo = grow(n_1, second_move)
     gh_hi = grad_hidden(cot_hi)
 
@@ -634,7 +676,7 @@
         return kernel_call(
             ffn_kernel,
             [shape(half, cols), shape(half, cols), shape(half, cols), shape(half, width)],
-            value, gh, *w_gu, scratch=[gate, up],
+            value, gh, *w_gate, *w_up, scratch=[gate, up],
         )
 
     n_lo, gh_hi, own_1 = stage((n_lo, gh_hi, own_1))
@@ -716,29 +758,35 @@
     n1_hi = permute(n1_lo, core_move)
     small = small + permute(small, core_move)
     down_b = over_o_back(grad_down, down_m)
-
-    held, sent, small, n1_hi, gate_m, grad_up, out_lo, dkv_peer = stage(
-        (held, sent, small, n1_hi, gate_m, grad_up, out_lo, dkv_peer)
+    out_2 = permute(out_lo[2 * rows :], second_move)
+
+    held, sent, small, n1_hi, gate_m, grad_up, out_2, dkv_peer, down_b = stage(
+        (held, sent, small, n1_hi, gate_m, grad_up, out_2, dkv_peer, down_b)
     )
     cross_c = permute(sent, core_move)
     part_self = kernel_call(
         columns_kernel, shape(quads * 40, width), eight_at, held, n1_lo, n1_hi, scalars=1, us=2
     )
-    out_2 = permute(out_lo[2 * rows :], second_move)
-    small = small + sum(permute(small, flips(a=k // 2, b=k % 2)) for k in range(1, 4))
+    self_got = [permute(part_self[k * 40 + 40 : k * 40 + 80], move) for k, move in enumerate(moves)]
+    small = small + permute(small, second_move)
+    out_1 = permute(summed(rows, 2 * rows, out_lo, out_2), first_move)
     up_m = over_m_back(grad_up)
     dkv_got = permute(dkv_peer, peer_move)
 
-    cross_c, part_self, down_b, out_2, dkv_got = stage((cross_c, part_self, down_b, out_2, dkv_got))
+    cross_c, part_self, small, gate_m, dkv_got, out_1 = stage(
+        (cross_c, part_self, small, gate_m, dkv_got, out_1)
+    )
+    gate_b = over_o_back(grad_gate, gate_m)
+    block_out = summed(0, rows, x_3, out_lo, out_2, out_1)
     quarter = kept.shape[0] // 4
     cross_2 = permute(summed(2 * quarter, 4 * quarter, kept, cross_c), second_move)
-    self_got = [permute(part_self[k * 40 + 40 : k * 40 + 80], move) for k, move in enumerate(moves)]
-    gate_b = over_o_back(grad_gate, gate_m)
+    small = small + permute(small, first_move)
     sum_down = back_sum(ff_rows, grad_down, down_m, *down_b)
 
-    cross_2, self_got, small, up_m, dkv_got, sum_down = stage(
-        (cross_2, self_got, small, up_m, dkv_got, sum_down)
-    )
+    cross_2, self_got, small, up_m, dkv_got, sum_down, block_out, gate_b = stage(
+        (cross_2, self_got, small, up_m, dkv_got, sum_down, block_out, gate_b)
+    )
+    sum_gate = back_sum(ff_rows, grad_gate, gate_m, *gate_b)
     cross_1 = permute(summed(quarter, 2 * quarter, kept, cross_c, cross_2), first_move)
     small_got = [permute(small, move) for move in moves]
     up_b = over_o_back(grad_up, up_m)
@@ -747,8 +795,8 @@
     )
     sum_self = back_sum(40, part_self, *self_got)
 
-    cross_1, small_got, gate_b, sum_self, grad_memory = stage(
-        (cross_1, small_got, gate_b, sum_self, grad_memory)
+    cross_1, small_got, sum_self, grad_memory, sum_gate = stage(
+        (cross_1, small_got, sum_self, grad_memory, sum_gate)
     )
 
     def pieces(k):
@@ -761,14 +809,11 @@
         )
 
     pieces_got = [permute(pieces(k + 1).astype(BF16), move) for k, move in enumerate(moves)]
-    out_1 = permute(summed(rows, 2 * rows, out_lo, out_2), first_move)
-    sum_gate = back_sum(ff_rows, grad_gate, gate_m, *gate_b)
     small = small + sum(small_got)
 
-    pieces_got, out_1, sum_gate, up_b, small = stage((pieces_got, out_1, sum_gate, up_b, small))
+    pieces_got, up_b, small = stage((pieces_got, up_b, small))
     sum_cross = pieces(0) + sum(g.astype(F32) for g in pieces_got)
     sum_up = back_sum(ff_rows, grad_up, up_m, *up_b)
-    block_out = summed(0, rows, x_3, out_lo, out_2, out_1)
 
     def three(total):
         query, key, value = (total[k * part_rows : (k + 1) * part_rows] for k in range(3))

time: 379 us -> 350 us (0.923)
  waiting for transfers between devices: 183 us -> 152 us
  local copies, waits for them, and re-layouts: 30 us -> 20.8 us
  starting transfers between devices: 68.7 us -> 74.6 us
    ppermute x53 -> x55, waiting for transfers between devices: 183 us -> 152 us  [permute(): return lax.ppermute(cut(value), AXES, pairs).reshape(value.shape)]
    unnamed x176 -> x153, local copies, waits for them, and re-layouts: 23.4 us -> 14.4 us
    ppermute x53 -> x55, starting transfers between devices: 64.2 us -> 70.1 us  [permute(): return lax.ppermute(cut(value), AXES, pairs).reshape(value.shape)]
    pallas_call x17 -> x18, Pallas kernels: 75.2 us -> 78.7 us  [kernel_call(): pl.pallas_call(body, out_shape=out_shape, in_specs=[pl.BlockSpec(memory_s...]
  transfers between devices with their start and end apart: 54 -> 56, of which waited for: 20 -> 20; matrix products, arithmetic and copies ran while one was open for 5% -> 6% of each run, Pallas kernels for 18% -> 20%
where the time goes in v4:
time: 350 us; the launch traced here: 346 us
  waiting for transfers between devices  152 us (43%)
  Pallas kernels  78.7 us (22%)
  starting transfers between devices  74.6 us (21%)
  local copies, waits for them, and re-layouts  20.8 us (6%)
  other arithmetic  17.5 us (5%)
    ppermute x55, waiting for transfers between devices, permute(): return lax.ppermute(cut(value), AXES, pairs).reshape(value.shape)  152 us
    pallas_call x18, Pallas kernels, kernel_call(): pl.pallas_call(body, out_shape=out_shape, in_specs=[pl.BlockSpec(memory_s...  78.7 us
    ppermute x55, starting transfers between devices, permute(): return lax.ppermute(cut(value), AXES, pairs).reshape(value.shape)  70.1 us
    unnamed x153, local copies, waits for them, and re-layouts  14.4 us
  transfers between devices with their start and end apart: 56, of which 20 were waited for; matrix products, arithmetic and copies ran while one was open for 6% of the time, Pallas kernels for 20%

profile of v4, /device:TPU:0, one launch (start us, length us, event | category | flops | bytes accessed | tf_op | source)
XLA Modules:
  0.0 345.8 jit_solution(15315669962164297521)
XLA Ops:
  3.4 5.1 %collective-permute-start.2 = (bf16[96,1472]{1,0:T(8,128)(2,1)}, bf16[96,1472]{1,0:T(8,128)(2,1)S(1)}, u32[]{:S(2)}, u32[]{:S(2)}) collective-permute-start(bf16[96,1472]{1,0:T(8,128)(2,1)} %shard_map.336.refs_0_), channel_id=1, source_target_pairs={{0,17},{1,16},{2,19},{3,18},{4,21},{5,20},{6,23},{7,22},{8,25},{9,... | collective-permute-start | bytes 847880 | tf_op jit(solution)/shard_map/ppermute | solution.py:524
  13.2 16.0 %collective-permute-done.2.refs_3_ = bf16[96,1472]{1,0:T(8,128)(2,1)S(1)} collective-permute-done((bf16[96,1472]{1,0:T(8,128)(2,1)}, bf16[96,1472]{1,0:T(8,128)(2,1)S(1)}, u32[]{:S(2)}, u32[]{:S(2)}) %collective-permute-start.2) | collective-permute-done | bytes 282656 | tf_op jit(solution)/shard_map/ppermute | solution.py:524
  29.2 5.5 %collective-permute-done.refs_1_ = bf16[96,1472]{1,0:T(8,128)(2,1)S(1)} collective-permute-done((bf16[96,1472]{1,0:T(8,128)(2,1)}, bf16[96,1472]{1,0:T(8,128)(2,1)S(1)}, u32[]{:S(2)}, u32[]{:S(2)}) %collective-permute-start) | collective-permute-done | bytes 282656 | tf_op jit(solution)/shard_map/ppermute | solution.py:524
  42.5 11.9 %collective-permute-done.5 = bf16[6,64,1472]{2,1,0:T(8,128)(2,1)} collective-permute-done((bf16[6,64,1472]{2,1,0:T(8,128)(2,1)S(1)}, bf16[6,64,1472]{2,1,0:T(8,128)(2,1)}, u32[]{:S(2)}, u32[]{:S(2)}) %collective-permute-start.5) | collective-permute-done | bytes 1130528 | tf_op jit(solution)/shard_map/ppermute | solution.py:524
  62.8 29.6 %collective-permute-done.8 = bf16[12,64,1472]{2,1,0:T(8,128)(2,1)S(1)} collective-permute-done((bf16[12,64,1472]{2,1,0:T(8,128)(2,1)S(1)}, bf16[12,64,1472]{2,1,0:T(8,128)(2,1)S(1)}, u32[]{:S(2)}, u32[]{:S(2)}) %collective-permute-start.8) | collective-permute-done | bytes 2261024 | tf_op jit(solution)/shard_map/ppermute | solution.py:524
  98.5 3.4 collective-permute-done.13
  104.1 4.7 %shard_map.340 = (bf16[288,768]{1,0:T(8,128)(2,1)S(1)}, bf16[288,768]{1,0:T(8,128)(2,1)S(1)}) custom-call(bf16[288,1472]{1,0:T(8,128)(2,1)S(1)} %copy-done.21, bf16[288,1472]{1,0:T(8,128)(2,1)S(1)} %collective-permute-done.9.peer_ref.mem_peer_ref, bf16[768,1472]{1,0:T(8,128)(2,1)S(1)} %get-tuple-element.205.w0_ref, bf16[768,1472]{1,0:T(8,128)(2,1)S(1)} %bitcast.85, ...), custom_call_target="tpu_custom_call" | custom-call | flops 5000000000 | bytes 1 | tf_op jit(solution)/shard_map/pallas_call | solution.py:70
  108.8 5.5 %shard_map.339 = (f32[192,1472]{1,0:T(8,128)S(1)}, bf16[192,1472]{1,0:T(8,128)(2,1)S(1)}, bf16[192,1152]{1,0:T(8,128)(2,1)S(1)}, bf16[192,384]{1,0:T(8,128)(2,1)S(1)}) custom-call(bf16[192,1472]{1,0:T(8,128)(2,1)S(1)} %copy-done.26, bf16[192,1472]{1,0:T(8,128)(2,1)S(1)} %get-tuple-element.268.n1_ref, f32[3,1472]{1,0:T(4,128)S(1)} %copy-done.33, ...), custom_call_target="tpu_custom_call" | custom-call | flops 5000000000 | bytes 1 | tf_op jit(solution)/shard_map/pallas_call | solution.py:70
  114.5 6.8 %shard_map.341 = (f32[192,1472]{1,0:T(8,128)S(1)}, bf16[192,1472]{1,0:T(8,128)(2,1)S(1)}, bf16[192,384]{1,0:T(8,128)(2,1)S(1)}, bf16[192,384]{1,0:T(8,128)(2,1)S(1)}) custom-call(f32[192,1472]{1,0:T(8,128)S(1)} %get-tuple-element.203.x_ref.x2_ref, bf16[192,1472]{1,0:T(8,128)(2,1)S(1)} %get-tuple-element.204.n_ref.n2_ref, f32[3,1472]{1,0:T(4,128)S(1)} %copy-done.33, ...), custom_call_target="tpu_custom_call" | custom-call | flops 5000000000 | bytes 1 | tf_op jit(solution)/shard_map/pallas_call | solution.py:70
  121.3 3.6 %collective-permute-done.15 = bf16[6,64,1472]{2,1,0:T(8,128)(2,1)S(1)} collective-permute-done((bf16[6,64,1472]{2,1,0:T(8,128)(2,1)S(1)}, bf16[6,64,1472]{2,1,0:T(8,128)(2,1)S(1)}, u32[]{:S(2)}, u32[]{:S(2)}) %collective-permute-start.15) | collective-permute-done | bytes 1130528 | tf_op jit(solution)/shard_map/ppermute | solution.py:524
  129.5 5.7 %collective-permute-done.19 = bf16[192,1472]{1,0:T(8,128)(2,1)S(1)} collective-permute-done((bf16[192,1472]{1,0:T(8,128)(2,1)S(1)}, bf16[192,1472]{1,0:T(8,128)(2,1)S(1)}, u32[]{:S(2)}, u32[]{:S(2)}) %collective-permute-start.19) | collective-permute-done | bytes 565280 | tf_op jit(solution)/shard_map/ppermute | solution.py:524
  138.1 13.8 %collective-permute-done.22 = bf16[6,64,1472]{2,1,0:T(8,128)(2,1)S(1)} collective-permute-done((bf16[6,64,1472]{2,1,0:T(8,128)(2,1)S(1)}, bf16[6,64,1472]{2,1,0:T(8,128)(2,1)S(1)}, u32[]{:S(2)}, u32[]{:S(2)}) %collective-permute-start.22) | collective-permute-done | bytes 1130528 | tf_op jit(solution)/shard_map/ppermute | solution.py:524
  152.2 5.2 %shard_map.344 = (bf16[768,448]{1,0:T(8,128)(2,1)S(1)}, bf16[768,448]{1,0:T(8,128)(2,1)S(1)}, bf16[768,448]{1,0:T(8,128)(2,1)S(1)}, bf16[768,1472]{1,0:T(8,128)(2,1)S(1)}) custom-call(bf16[768,1472]{1,0:T(8,128)(2,1)S(1)} %pad_maximum_fusion.4.n_ref.n0_ref, f32[768,448]{1,0:T(8,128)S(1)} %shard_map.342.gh_ref, ...), custom_call_target="tpu_custom_call" | custom-call | flops 5000000000 | bytes 1 | tf_op jit(solution)/shard_map/pallas_call | solution.py:70
  157.4 5.2 %shard_map.345 = (bf16[768,448]{1,0:T(8,128)(2,1)S(1)}, bf16[768,448]{1,0:T(8,128)(2,1)S(1)}, bf16[768,448]{1,0:T(8,128)(2,1)S(1)}, bf16[768,1472]{1,0:T(8,128)(2,1)S(1)}) custom-call(bf16[768,1472]{1,0:T(8,128)(2,1)S(1)} %bitcast.93, f32[768,448]{1,0:T(8,128)S(1)} %shard_map.343.gh_ref, bf16[112,1472]{1,0:T(8,128)(2,1)S(1)} %get-tuple-element.232.refs_0_, ...), custom_call_target="tpu_custom_call" | custom-call | flops 5000000000 | bytes 1 | tf_op jit(solution)/shard_map/pallas_call | solution.py:70
  169.4 6.6 %shard_map.347 = (bf16[448,1472]{1,0:T(8,128)(2,1)S(1)}, bf16[448,1472]{1,0:T(8,128)(2,1)S(1)}, bf16[448,1472]{1,0:T(8,128)(2,1)S(1)}) custom-call(bf16[768,448]{1,0:T(8,128)(2,1)S(1)} %get-tuple-element.260.h0_ref.h_ref, bf16[768,448]{1,0:T(8,128)(2,1)S(1)} %get-tuple-element.256.h_ref.h1_ref, bf16[768,448]{1,0:T(8,128)(2,1)S(1)} %get-tuple-element.261.g0_ref, ...), custom_call_target="tpu_custom_call" | custom-call | flops 5000000000 | bytes 1 | tf_op jit(solution)/shard_map/pallas_call | solution.py:70
  176.0 14.6 %collective-permute-done.25 = bf16[6,64,1472]{2,1,0:T(8,128)(2,1)S(1)} collective-permute-done((bf16[6,64,1472]{2,1,0:T(8,128)(2,1)S(1)}, bf16[6,64,1472]{2,1,0:T(8,128)(2,1)S(1)}, u32[]{:S(2)}, u32[]{:S(2)}) %collective-permute-start.25) | collective-permute-done | bytes 1130528 | tf_op jit(solution)/shard_map/ppermute | solution.py:524
  194.8 6.0 %collective-permute-done.27.got_ref = bf16[192,1472]{1,0:T(8,128)(2,1)S(1)} collective-permute-done((bf16[192,1472]{1,0:T(8,128)(2,1)S(1)}, bf16[192,1472]{1,0:T(8,128)(2,1)S(1)}, u32[]{:S(2)}, u32[]{:S(2)}) %collective-permute-start.27) | collective-permute-done | bytes 565280 | tf_op jit(solution)/shard_map/ppermute | solution.py:524
  201.3 9.0 %shard_map.349 = (bf16[192,1472]{1,0:T(8,128)(2,1)S(1)}, f32[192,1472]{1,0:T(8,128)S(1)}, bf16[192,384]{1,0:T(8,128)(2,1)S(1)}, bf16[288,768]{1,0:T(8,128)(2,1)S...) custom-call(bf16[768,1472]{1,0:T(8,128)(2,1)S(1)} %get-tuple-element.254.lo_ref, ...), custom_call_target="tpu_custom_call" | custom-call | flops 8000000000 | bytes 1 | tf_op jit(solution)/shard_map/pallas_call | solution.py:70
  210.4 9.5 %shard_map.351 = (f32[192,1472]{1,0:T(8,128)}, bf16[1280,192]{1,0:T(8,128)(2,1)}, f32[4,1472]{1,0:T(4,128)S(1)}) custom-call(f32[192,1472]{1,0:T(8,128)S(1)} %get-tuple-element.283.g2_ref, bf16[192,1472]{1,0:T(8,128)(2,1)S(1)} %copy-done.26, f32[3,1472]{1,0:T(4,128)S(1)} %copy-done.33, bf16[768,1472]{1,0:T(8,128)(2,1)S(1)} %get-tuple-element.197.w0_ref, ...), custom_call_target="tpu_custom_call" | custom-call | flops 8000000000 | bytes 1 | tf_op jit(solution)/shard_map/pallas_call | solution.py:70
  226.4 4.5 %all-to-all-start = ((bf16[8,160,192]{2,1,0:T(8,128)(2,1)}), bf16[8,160,192]{2,1,0:T(8,128)(2,1)}, u32[]{:S(2)}, u32[]{:S(2)}) async-start(bf16[8,160,192]{2,1,0:T(8,128)(2,1)} %bitcast.36), calls=%async_computation | async-start | bytes 1310720 | tf_op jit(solution)/shard_map/all_to_all | solution.py:547
  231.4 4.4 %collective-permute-start.35 = (bf16[112,1472]{1,0:T(8,128)(2,1)S(1)}, bf16[112,1472]{1,0:T(8,128)(2,1)}, u32[]{:S(2)}, u32[]{:S(2)}) collective-permute-start(bf16[112,1472]{1,0:T(8,128)(2,1)S(1)} %add_convert_fusion.8), channel_id=1, source_target_pairs={{0,16},{1,17},{2,18},{3,19},{4,20},{5,21},{6,22},{7,23},{8,24},{9,... | collective-permute-start | bytes 989192 | tf_op jit(solution)/shard_map/ppermute | solution.py:524
  244.5 8.0 %shard_map.350 = (bf16[1024,1472]{1,0:T(8,128)(2,1)S(1)}, bf16[1024,1472]{1,0:T(8,128)(2,1)S(1)}) custom-call(bf16[192,384]{1,0:T(8,128)(2,1)S(1)} %copy-done.59, bf16[192,384]{1,0:T(8,128)(2,1)S(1)} %copy-done.55, bf16[288,768]{1,0:T(8,128)(2,1)S(1)} %copy-done.48, bf16[288,768]{1,0:T(8,128)(2,1)S(1)} %copy-done.28, bf16[192,384]{1,0:T(8,128)(2,1)S(1)} %copy-done.57, ...), custom_call_target="tpu_custom_call" | custom-call | flops 10000000000 | bytes 1 | tf_op jit(solution)/shard_map/pallas_call | solution.py:70
  254.3 4.4 %collective-permute-start.37 = (f32[4,1472]{1,0:T(4,128)S(1)}, f32[4,1472]{1,0:T(4,128)S(1)}, u32[]{:S(2)}, u32[]{:S(2)}) collective-permute-start(f32[4,1472]{1,0:T(4,128)S(1)} %add.279), channel_id=1, source_target_pairs={{0,8},{1,9},{2,6},{3,7},{4,12},{5,13},{6,2},{7,3},{8,0},{9,1},{10,... | collective-permute-start | bytes 70664 | tf_op jit(solution)/shard_map/ppermute | solution.py:524
  262.6 3.7 %shard_map.352 = bf16[160,1472]{1,0:T(8,128)(2,1)S(1)} custom-call(s32[8]{0:T(128)S(1)} %and_select_fusion.at_ref, bf16[8,160,192]{2,1,0:T(8,128)(2,1)} %all-to-all-done.held_ref, bf16[768,1472]{1,0:T(8,128)(2,1)} %pad_maximum_fusion.5.lo_ref, bf16[768,1472]{1,0:T(8,128)(2,1)} %bitcast.38.hi_ref), custom_call_target="tpu_custom_call" | custom-call | flops 2000000000 | bytes 1 | tf_op jit(solution)/shard_map/pallas_call | solution.py:70
  272.0 4.6 %collective-permute-start.40 = (bf16[8,64,1472]{2,1,0:T(8,128)(2,1)S(1)}, bf16[8,64,1472]{2,1,0:T(8,128)(2,1)S(1)}, u32[]{:S(2)}, u32[]{:S(2)}) collective-permute-start(bf16[8,64,1472]{2,1,0:T(8,128)(2,1)S(1)} %bitcast.113), channel_id=1, source_target_pairs={{0,8},{1,9},{2,6},{3,7},{4,12},{5,13},{6,2},{7,3},{8,0},{9,1},{10,... | collective-permute-start | bytes 4521992 | tf_op jit(solution)/shard_map/ppermute | solution.py:524
  286.0 15.4 %collective-permute-done.41 = bf16[40,1472]{1,0:T(8,128)(2,1)S(1)} collective-permute-done((bf16[40,1472]{1,0:T(8,128)(2,1)S(1)}, bf16[40,1472]{1,0:T(8,128)(2,1)S(1)}, u32[]{:S(2)}, u32[]{:S(2)}) %collective-permute-start.41) | collective-permute-done | bytes 117792 | tf_op jit(solution)/shard_map/ppermute | solution.py:524
  301.4 5.7 %collective-permute-done.46 = bf16[112,1472]{1,0:T(8,128)(2,1)S(1)} collective-permute-done((bf16[112,1472]{1,0:T(8,128)(2,1)S(1)}, bf16[112,1472]{1,0:T(8,128)(2,1)S(1)}, u32[]{:S(2)}, u32[]{:S(2)}) %collective-permute-start.46) | collective-permute-done | bytes 329760 | tf_op jit(solution)/shard_map/ppermute | solution.py:524
  307.1 3.4 collective-permute-start.50
  317.6 3.5 shard_map.353
  321.2 7.6 %collective-permute-done.47 = bf16[4,64,1472]{2,1,0:T(8,128)(2,1)S(1)} collective-permute-done((bf16[4,64,1472]{2,1,0:T(8,128)(2,1)S(1)}, bf16[4,64,1472]{2,1,0:T(8,128)(2,1)S(1)}, u32[]{:S(2)}, u32[]{:S(2)}) %collective-permute-start.47) | collective-permute-done | bytes 753696 | tf_op jit(solution)/shard_map/ppermute | solution.py:524
  329.9 3.9 %collective-permute-start.53 = (bf16[64,1472]{1,0:T(8,128)(2,1)S(1)}, bf16[64,1472]{1,0:T(8,128)(2,1)S(1)}, u32[]{:S(2)}, u32[]{:S(2)}) collective-permute-start(bf16[64,1472]{1,0:T(8,128)(2,1)S(1)} %pad_maximum_fusion.11), channel_id=1, source_target_pairs={{0,17},{1,16},{2,19},{3,18},{4,21},{5,20},{6,23},{7,22},{8,25},{9,... | collective-permute-start | bytes 565256 | tf_op jit(solution)/shard_map/ppermute | solution.py:524
  335.3 4.7 %collective-permute-done.51 = bf16[64,1472]{1,0:T(8,128)(2,1)S(1)} collective-permute-done((bf16[64,1472]{1,0:T(8,128)(2,1)S(1)}, bf16[64,1472]{1,0:T(8,128)(2,1)S(1)}, u32[]{:S(2)}, u32[]{:S(2)}) %collective-permute-start.51) | collective-permute-done | bytes 188448 | tf_op jit(solution)/shard_map/ppermute | solution.py:524
  (313 shorter events, 102.0 us)
Async XLA Ops:
  3.4 25.8 %collective-permute-start.2 = (bf16[96,1472]{1,0:T(8,128)(2,1)}, bf16[96,1472]{1,0:T(8,128)(2,1)S(1)}, u32[]{:S(2)}, u32[]{:S(2)}) collective-permute-start(bf16[96,1472]{1,0:T(8,128)(2,1)} %shard_map.336.refs_0_), channel_id=1, source_target_pairs={{0,17},{1,16},{2,19},{3,18},{4,21},{5,20},{6,23},{7,22},{8,25},{9,... | collective-permute-start | bytes 847880 | tf_op jit(solution)/shard_map/ppermute | solution.py:524
  8.5 20.7 %collective-permute-start.1 = (bf16[96,1472]{1,0:T(8,128)(2,1)}, bf16[96,1472]{1,0:T(8,128)(2,1)S(1)}, u32[]{:S(2)}, u32[]{:S(2)}) collective-permute-start(bf16[96,1472]{1,0:T(8,128)(2,1)} %shard_map.336.refs_0_), channel_id=1, source_target_pairs={{0,1},{1,0},{2,3},{3,2},{4,5},{5,4},{6,7},{7,6},{8,9},{9,8},{10,11... | collective-permute-start | bytes 847880 | tf_op jit(solution)/shard_map/ppermute | solution.py:524
  9.0 25.7 %collective-permute-start = (bf16[96,1472]{1,0:T(8,128)(2,1)}, bf16[96,1472]{1,0:T(8,128)(2,1)S(1)}, u32[]{:S(2)}, u32[]{:S(2)}) collective-permute-start(bf16[96,1472]{1,0:T(8,128)(2,1)} %shard_map.336.refs_0_), channel_id=1, source_target_pairs={{0,16},{1,17},{2,18},{3,19},{4,20},{5,21},{6,22},{7,23},{8,24},{9,... | collective-permute-start | bytes 847880 | tf_op jit(solution)/shard_map/ppermute | solution.py:524
  9.1 29.0 %collective-permute-start.4 = (s32[1,288]{1,0:T(1,128)S(1)}, s32[1,288]{1,0:T(1,128)S(1)}, u32[]{:S(2)}, u32[]{:S(2)}) collective-permute-start(s32[1,288]{1,0:T(1,128)S(1)} %reshape.243.keep_ref), channel_id=1, source_target_pairs={{0,1},{1,0},{2,3},{3,2},{4,5},{5,4},{6,7},{7,6},{8,9},{9,8},{10,11... | collective-permute-start | bytes 3464 | tf_op jit(solution)/shard_map/ppermute | solution.py:524
  10.8 25.0 %collective-permute-start.3 = (bf16[192,1472]{1,0:T(8,128)(2,1)S(1)}, bf16[192,1472]{1,0:T(8,128)(2,1)}, u32[]{:S(2)}, u32[]{:S(2)}) collective-permute-start(bf16[192,1472]{1,0:T(8,128)(2,1)S(1)} %copy-done.10), channel_id=1, source_target_pairs={{0,4},{1,5},{2,10},{3,11},{4,0},{5,1},{6,14},{7,15},{8,12},{9,13},... | collective-permute-start | bytes 1695752 | tf_op jit(solution)/shard_map/ppermute | solution.py:524
  56.0 36.4 %collective-permute-start.8 = (bf16[12,64,1472]{2,1,0:T(8,128)(2,1)S(1)}, bf16[12,64,1472]{2,1,0:T(8,128)(2,1)S(1)}, u32[]{:S(2)}, u32[]{:S(2)}) collective-permute-start(bf16[12,64,1472]{2,1,0:T(8,128)(2,1)S(1)} %bitcast.100), channel_id=1, source_target_pairs={{0,8},{1,9},{2,6},{3,7},{4,12},{5,13},{6,2},{7,3},{8,0},{9,1},{10,... | collective-permute-start | bytes 6782984 | tf_op jit(solution)/shard_map/ppermute | solution.py:524
  56.9 37.0 %collective-permute-start.9 = (bf16[288,1472]{1,0:T(8,128)(2,1)S(1)}, bf16[288,1472]{1,0:T(8,128)(2,1)S(1)}, u32[]{:S(2)}, u32[]{:S(2)}) collective-permute-start(bf16[288,1472]{1,0:T(8,128)(2,1)S(1)} %copy-done.21), channel_id=1, source_target_pairs={{0,1},{1,0},{2,3},{3,2},{4,5},{5,4},{6,7},{7,6},{8,9},{9,8},{10,11... | collective-permute-start | bytes 2543624 | tf_op jit(solution)/shard_map/ppermute | solution.py:524
  57.4 36.5 %collective-permute-start.11 = (bf16[112,1472]{1,0:T(8,128)(2,1)S(1)}, bf16[112,1472]{1,0:T(8,128)(2,1)S(1)}, u32[]{:S(2)}, u32[]{:S(2)}) collective-permute-start(bf16[112,1472]{1,0:T(8,128)(2,1)S(1)} %get-tuple-element.232.refs_0_), channel_id=1, source_target_pairs={{0,1},{1,0},{2,3},{3,2},{4,5},{5,4},{6,7},{7,6},{8,9},{9,8},{10,11... | collective-permute-start | bytes 989192 | tf_op jit(solution)/shard_map/ppermute | solution.py:524
  58.9 35.0 %collective-permute-start.10 = (bf16[112,1472]{1,0:T(8,128)(2,1)S(1)}, bf16[112,1472]{1,0:T(8,128)(2,1)S(1)}, u32[]{:S(2)}, u32[]{:S(2)}) collective-permute-start(bf16[112,1472]{1,0:T(8,128)(2,1)S(1)} %get-tuple-element.232.refs_0_), channel_id=1, source_target_pairs={{0,16},{1,17},{2,18},{3,19},{4,20},{5,21},{6,22},{7,23},{8,24},{9,... | collective-permute-start | bytes 989192 | tf_op jit(solution)/shard_map/ppermute | solution.py:524
  62.1 31.8 %collective-permute-start.12 = (bf16[112,1472]{1,0:T(8,128)(2,1)S(1)}, bf16[112,1472]{1,0:T(8,128)(2,1)S(1)}, u32[]{:S(2)}, u32[]{:S(2)}) collective-permute-start(bf16[112,1472]{1,0:T(8,128)(2,1)S(1)} %collective-permute-done.6.refs_1_.refs_2_), channel_id=1, source_target_pairs={{0,1},{1,0},{2,3},{3,2},{4,5},{5,4},{6,7},{7,6},{8,9},{9,8},{10,11... | collective-permute-start | bytes 989192 | tf_op jit(solution)/shard_map/ppermute | solution.py:524
  94.5 30.6 %collective-permute-start.18 = (bf16[112,1472]{1,0:T(8,128)(2,1)S(1)}, bf16[112,1472]{1,0:T(8,128)(2,1)S(1)}, u32[]{:S(2)}, u32[]{:S(2)}) collective-permute-start(bf16[112,1472]{1,0:T(8,128)(2,1)S(1)} %get-tuple-element.236.refs_4_), channel_id=1, source_target_pairs={{0,1},{1,0},{2,3},{3,2},{4,5},{5,4},{6,7},{7,6},{8,9},{9,8},{10,11... | collective-permute-start | bytes 989192 | tf_op jit(solution)/shard_map/ppermute | solution.py:524
  95.2 29.9 %collective-permute-start.17 = (bf16[112,1472]{1,0:T(8,128)(2,1)S(1)}, bf16[112,1472]{1,0:T(8,128)(2,1)S(1)}, u32[]{:S(2)}, u32[]{:S(2)}) collective-permute-start(bf16[112,1472]{1,0:T(8,128)(2,1)S(1)} %get-tuple-element.236.refs_4_), channel_id=1, source_target_pairs={{0,16},{1,17},{2,18},{3,19},{4,20},{5,21},{6,22},{7,23},{8,24},{9,... | collective-permute-start | bytes 989192 | tf_op jit(solution)/shard_map/ppermute | solution.py:524
  101.9 23.2 %collective-permute-start.16 = (bf16[112,1472]{1,0:T(8,128)(2,1)S(1)}, bf16[112,1472]{1,0:T(8,128)(2,1)S(1)}, u32[]{:S(2)}, u32[]{:S(2)}) collective-permute-start(bf16[112,1472]{1,0:T(8,128)(2,1)S(1)} %collective-permute-done.10.refs_1_), channel_id=1, source_target_pairs={{0,1},{1,0},{2,3},{3,2},{4,5},{5,4},{6,7},{7,6},{8,9},{9,8},{10,11... | collective-permute-start | bytes 989192 | tf_op jit(solution)/shard_map/ppermute | solution.py:524
  102.6 22.2 %collective-permute-start.15 = (bf16[6,64,1472]{2,1,0:T(8,128)(2,1)S(1)}, bf16[6,64,1472]{2,1,0:T(8,128)(2,1)S(1)}, u32[]{:S(2)}, u32[]{:S(2)}) collective-permute-start(bf16[6,64,1472]{2,1,0:T(8,128)(2,1)S(1)} %bitcast.103), channel_id=1, source_target_pairs={{0,8},{1,9},{2,6},{3,7},{4,12},{5,13},{6,2},{7,3},{8,0},{9,1},{10,... | collective-permute-start | bytes 3391496 | tf_op jit(solution)/shard_map/ppermute | solution.py:524
  167.4 23.2 %collective-permute-start.26 = (bf16[12,64,1472]{2,1,0:T(8,128)(2,1)}, bf16[12,64,1472]{2,1,0:T(8,128)(2,1)S(1)}, u32[]{:S(2)}, u32[]{:S(2)}) collective-permute-start(bf16[12,64,1472]{2,1,0:T(8,128)(2,1)} %bitcast.32), channel_id=1, source_target_pairs={{0,2},{1,3},{2,0},{3,1},{4,6},{5,7},{6,4},{7,5},{8,10},{9,11},{10,... | collective-permute-start | bytes 6782984 | tf_op jit(solution)/shard_map/ppermute | solution.py:524
  168.0 22.6 %collective-permute-start.25 = (bf16[6,64,1472]{2,1,0:T(8,128)(2,1)S(1)}, bf16[6,64,1472]{2,1,0:T(8,128)(2,1)S(1)}, u32[]{:S(2)}, u32[]{:S(2)}) collective-permute-start(bf16[6,64,1472]{2,1,0:T(8,128)(2,1)S(1)} %bitcast.117), channel_id=1, source_target_pairs={{0,8},{1,9},{2,6},{3,7},{4,12},{5,13},{6,2},{7,3},{8,0},{9,1},{10,... | collective-permute-start | bytes 3391496 | tf_op jit(solution)/shard_map/ppermute | solution.py:524
  169.1 22.7 %collective-permute-start.28 = (bf16[192,1472]{1,0:T(8,128)(2,1)S(1)}, bf16[192,1472]{1,0:T(8,128)(2,1)S(1)}, u32[]{:S(2)}, u32[]{:S(2)}) collective-permute-start(bf16[192,1472]{1,0:T(8,128)(2,1)S(1)} %get-tuple-element.268.n1_ref), channel_id=1, source_target_pairs={{0,4},{1,5},{2,10},{3,11},{4,0},{5,1},{6,14},{7,15},{8,12},{9,13},... | collective-permute-start | bytes 1695752 | tf_op jit(solution)/shard_map/ppermute | solution.py:524
  192.0 18.3 %collective-permute-start.29 = (bf16[224,1472]{1,0:T(8,128)(2,1)S(1)}, bf16[224,1472]{1,0:T(8,128)(2,1)S(1)}, u32[]{:S(2)}, u32[]{:S(2)}) collective-permute-start(bf16[224,1472]{1,0:T(8,128)(2,1)S(1)} %slice.288), channel_id=1, source_target_pairs={{0,1},{1,0},{2,3},{3,2},{4,5},{5,4},{6,7},{7,6},{8,9},{9,8},{10,11... | collective-permute-start | bytes 1978376 | tf_op jit(solution)/shard_map/ppermute | solution.py:524
  200.8 19.1 %collective-permute-start.30 = (bf16[6,64,1472]{2,1,0:T(8,128)(2,1)S(1)}, bf16[6,64,1472]{2,1,0:T(8,128)(2,1)S(1)}, u32[]{:S(2)}, u32[]{:S(2)}) collective-permute-start(bf16[6,64,1472]{2,1,0:T(8,128)(2,1)S(1)} %bitcast.104), channel_id=1, source_target_pairs={{0,8},{1,9},{2,6},{3,7},{4,12},{5,13},{6,2},{7,3},{8,0},{9,1},{10,... | collective-permute-start | bytes 3391496 | tf_op jit(solution)/shard_map/ppermute | solution.py:524
  221.5 32.7 %collective-permute-start.32 = (bf16[12,64,1472]{2,1,0:T(8,128)(2,1)}, bf16[12,64,1472]{2,1,0:T(8,128)(2,1)}, u32[]{:S(2)}, u32[]{:S(2)}) collective-permute-start(bf16[12,64,1472]{2,1,0:T(8,128)(2,1)} %bitcast.37), channel_id=1, source_target_pairs={{0,2},{1,3},{2,0},{3,1},{4,6},{5,7},{6,4},{7,5},{8,10},{9,11},{10,... | collective-permute-start | bytes 6782984 | tf_op jit(solution)/shard_map/ppermute | solution.py:524
  222.7 31.5 %collective-permute-start.34 = (bf16[6,64,1472]{2,1,0:T(8,128)(2,1)}, bf16[6,64,1472]{2,1,0:T(8,128)(2,1)}, u32[]{:S(2)}, u32[]{:S(2)}) collective-permute-start(bf16[6,64,1472]{2,1,0:T(8,128)(2,1)} %bitcast.39), channel_id=1, source_target_pairs={{0,8},{1,9},{2,6},{3,7},{4,12},{5,13},{6,2},{7,3},{8,0},{9,1},{10,... | collective-permute-start | bytes 3391496 | tf_op jit(solution)/shard_map/ppermute | solution.py:524
  225.2 29.0 %collective-permute-start.33 = (bf16[224,1472]{1,0:T(8,128)(2,1)}, bf16[224,1472]{1,0:T(8,128)(2,1)}, u32[]{:S(2)}, u32[]{:S(2)}) collective-permute-start(bf16[224,1472]{1,0:T(8,128)(2,1)} %slice.290), channel_id=1, source_target_pairs={{0,1},{1,0},{2,3},{3,2},{4,5},{5,4},{6,7},{7,6},{8,9},{9,8},{10,11... | collective-permute-start | bytes 1978376 | tf_op jit(solution)/shard_map/ppermute | solution.py:524
  226.4 27.8 %all-to-all-start = ((bf16[8,160,192]{2,1,0:T(8,128)(2,1)}), bf16[8,160,192]{2,1,0:T(8,128)(2,1)}, u32[]{:S(2)}, u32[]{:S(2)}) async-start(bf16[8,160,192]{2,1,0:T(8,128)(2,1)} %bitcast.36), calls=%async_computation | async-start | bytes 1310720 | tf_op jit(solution)/shard_map/all_to_all | solution.py:547
  230.9 21.6 %collective-permute-start.31 = (f32[4,1472]{1,0:T(4,128)S(1)}, f32[4,1472]{1,0:T(4,128)S(1)}, u32[]{:S(2)}, u32[]{:S(2)}) collective-permute-start(f32[4,1472]{1,0:T(4,128)S(1)} %get-tuple-element.296), channel_id=1, source_target_pairs={{0,2},{1,3},{2,0},{3,1},{4,6},{5,7},{6,4},{7,5},{8,10},{9,11},{10,... | collective-permute-start | bytes 70664 | tf_op jit(solution)/shard_map/ppermute | solution.py:524
  231.4 22.8 %collective-permute-start.35 = (bf16[112,1472]{1,0:T(8,128)(2,1)S(1)}, bf16[112,1472]{1,0:T(8,128)(2,1)}, u32[]{:S(2)}, u32[]{:S(2)}) collective-permute-start(bf16[112,1472]{1,0:T(8,128)(2,1)S(1)} %add_convert_fusion.8), channel_id=1, source_target_pairs={{0,16},{1,17},{2,18},{3,19},{4,20},{5,21},{6,22},{7,23},{8,24},{9,... | collective-permute-start | bytes 989192 | tf_op jit(solution)/shard_map/ppermute | solution.py:524
  254.2 17.3 %collective-permute-start.36 = (bf16[16,64,1472]{2,1,0:T(8,128)(2,1)}, bf16[16,64,1472]{2,1,0:T(8,128)(2,1)S(1)}, u32[]{:S(2)}, u32[]{:S(2)}) collective-permute-start(bf16[16,64,1472]{2,1,0:T(8,128)(2,1)} %bitcast.84), channel_id=1, source_target_pairs={{0,2},{1,3},{2,0},{3,1},{4,6},{5,7},{6,4},{7,5},{8,10},{9,11},{10,... | collective-permute-start | bytes 9043976 | tf_op jit(solution)/shard_map/ppermute | solution.py:524
  267.0 19.0 %collective-permute-start.42 = (bf16[40,1472]{1,0:T(8,128)(2,1)S(1)}, bf16[40,1472]{1,0:T(8,128)(2,1)S(1)}, u32[]{:S(2)}, u32[]{:S(2)}) collective-permute-start(bf16[40,1472]{1,0:T(8,128)(2,1)S(1)} %get-tuple-element.386), channel_id=1, source_target_pairs={{0,1},{1,0},{2,3},{3,2},{4,5},{5,4},{6,7},{7,6},{8,9},{9,8},{10,11... | collective-permute-start | bytes 353288 | tf_op jit(solution)/shard_map/ppermute | solution.py:524
  268.6 32.8 %collective-permute-start.45 = (bf16[224,1472]{1,0:T(8,128)(2,1)S(1)}, bf16[224,1472]{1,0:T(8,128)(2,1)S(1)}, u32[]{:S(2)}, u32[]{:S(2)}) collective-permute-start(bf16[224,1472]{1,0:T(8,128)(2,1)S(1)} %slice.300), channel_id=1, source_target_pairs={{0,1},{1,0},{2,3},{3,2},{4,5},{5,4},{6,7},{7,6},{8,9},{9,8},{10,11... | collective-permute-start | bytes 1978376 | tf_op jit(solution)/shard_map/ppermute | solution.py:524
  272.0 35.2 %collective-permute-start.40 = (bf16[8,64,1472]{2,1,0:T(8,128)(2,1)S(1)}, bf16[8,64,1472]{2,1,0:T(8,128)(2,1)S(1)}, u32[]{:S(2)}, u32[]{:S(2)}) collective-permute-start(bf16[8,64,1472]{2,1,0:T(8,128)(2,1)S(1)} %bitcast.113), channel_id=1, source_target_pairs={{0,8},{1,9},{2,6},{3,7},{4,12},{5,13},{6,2},{7,3},{8,0},{9,1},{10,... | collective-permute-start | bytes 4521992 | tf_op jit(solution)/shard_map/ppermute | solution.py:524
  280.6 20.8 %collective-permute-start.41 = (bf16[40,1472]{1,0:T(8,128)(2,1)S(1)}, bf16[40,1472]{1,0:T(8,128)(2,1)S(1)}, u32[]{:S(2)}, u32[]{:S(2)}) collective-permute-start(bf16[40,1472]{1,0:T(8,128)(2,1)S(1)} %get-tuple-element.387), channel_id=1, source_target_pairs={{0,16},{1,17},{2,18},{3,19},{4,20},{5,21},{6,22},{7,23},{8,24},{9,... | collective-permute-start | bytes 353288 | tf_op jit(solution)/shard_map/ppermute | solution.py:524
  282.8 24.3 %collective-permute-start.46 = (bf16[112,1472]{1,0:T(8,128)(2,1)S(1)}, bf16[112,1472]{1,0:T(8,128)(2,1)S(1)}, u32[]{:S(2)}, u32[]{:S(2)}) collective-permute-start(bf16[112,1472]{1,0:T(8,128)(2,1)S(1)} %add_convert_fusion.7), channel_id=1, source_target_pairs={{0,16},{1,17},{2,18},{3,19},{4,20},{5,21},{6,22},{7,23},{8,24},{9,... | collective-permute-start | bytes 989192 | tf_op jit(solution)/shard_map/ppermute | solution.py:524
  313.4 21.9 %collective-permute-start.54 = (bf16[112,1472]{1,0:T(8,128)(2,1)S(1)}, bf16[112,1472]{1,0:T(8,128)(2,1)S(1)}, u32[]{:S(2)}, u32[]{:S(2)}) collective-permute-start(bf16[112,1472]{1,0:T(8,128)(2,1)S(1)} %add_convert_fusion.6), channel_id=1, source_target_pairs={{0,16},{1,17},{2,18},{3,19},{4,20},{5,21},{6,22},{7,23},{8,24},{9,... | collective-permute-start | bytes 989192 | tf_op jit(solution)/shard_map/ppermute | solution.py:524
  (99 other events, 1117.3 us)

commit v5 on v4

--- a/solution.py
+++ b/solution.py
@@ -668,7 +668,7 @@
 
     gh_lo = grad_hidden(cot_lo)
 
-    n_1, cot_hi, gh_lo, own_1, w_up = stage((n_1, cot_hi, gh_lo, own_1, w_up))
+    n_1, cot_hi, gh_lo, own_1 = stage((n_1, cot_hi, gh_lo, own_1))
     n_lo = grow(n_1, second_move)
     gh_hi = grad_hidden(cot_hi)
 
@@ -679,7 +679,7 @@
             value, gh, *w_gate, *w_up, scratch=[gate, up],
         )
 
-    n_lo, gh_hi, own_1 = stage((n_lo, gh_hi, own_1))
+    n_lo, gh_hi, own_1, w_up = stage((n_lo, gh_hi, own_1, w_up))
     n_hi = permute(n_lo, core_move)
     lo_f = ffn(n_lo, gh_lo)
     one_1 = grow(own_1, first_move)

time: 350 us -> 349 us (level)
  transfers between devices with their start and end apart: 56 -> 56, of which waited for: 20 -> 19; matrix products, arithmetic and copies ran while one was open for 6% -> 6% of each run, Pallas kernels for 20% -> 21%
where the time goes in v5:
time: 349 us; the launch traced here: 345 us
  waiting for transfers between devices  152 us (44%)
  Pallas kernels  78.8 us (23%)
  starting transfers between devices  73 us (21%)
  local copies, waits for them, and re-layouts  20.8 us (6%)
  other arithmetic  17.5 us (5%)
    ppermute x55, waiting for transfers between devices, permute(): return lax.ppermute(cut(value), AXES, pairs).reshape(value.shape)  152 us
    pallas_call x18, Pallas kernels, kernel_call(): pl.pallas_call(body, out_shape=out_shape, in_specs=[pl.BlockSpec(memory_s...  78.8 us
    ppermute x55, starting transfers between devices, permute(): return lax.ppermute(cut(value), AXES, pairs).reshape(value.shape)  68.6 us
    unnamed x153, local copies, waits for them, and re-layouts  14.4 us
  transfers between devices with their start and end apart: 56, of which 19 were waited for; matrix products, arithmetic and copies ran while one was open for 6% of the time, Pallas kernels for 21%

profile of v5, /device:TPU:0, one launch (start us, length us, event | category | flops | bytes accessed | tf_op | source)
XLA Modules:
  0.0 344.9 jit_solution(9696994178630411884)
XLA Ops:
  3.4 5.1 %collective-permute-start.2 = (bf16[96,1472]{1,0:T(8,128)(2,1)}, bf16[96,1472]{1,0:T(8,128)(2,1)S(1)}, u32[]{:S(2)}, u32[]{:S(2)}) collective-permute-start(bf16[96,1472]{1,0:T(8,128)(2,1)} %shard_map.336.refs_0_), channel_id=1, source_target_pairs={{0,17},{1,16},{2,19},{3,18},{4,21},{5,20},{6,23},{7,22},{8,25},{9,... | collective-permute-start | bytes 847880 | tf_op jit(solution)/shard_map/ppermute | solution.py:524
  13.2 16.0 %collective-permute-done.2.refs_3_ = bf16[96,1472]{1,0:T(8,128)(2,1)S(1)} collective-permute-done((bf16[96,1472]{1,0:T(8,128)(2,1)}, bf16[96,1472]{1,0:T(8,128)(2,1)S(1)}, u32[]{:S(2)}, u32[]{:S(2)}) %collective-permute-start.2) | collective-permute-done | bytes 282656 | tf_op jit(solution)/shard_map/ppermute | solution.py:524
  29.2 5.5 %collective-permute-done.refs_1_ = bf16[96,1472]{1,0:T(8,128)(2,1)S(1)} collective-permute-done((bf16[96,1472]{1,0:T(8,128)(2,1)}, bf16[96,1472]{1,0:T(8,128)(2,1)S(1)}, u32[]{:S(2)}, u32[]{:S(2)}) %collective-permute-start) | collective-permute-done | bytes 282656 | tf_op jit(solution)/shard_map/ppermute | solution.py:524
  42.5 11.9 %collective-permute-done.5 = bf16[6,64,1472]{2,1,0:T(8,128)(2,1)} collective-permute-done((bf16[6,64,1472]{2,1,0:T(8,128)(2,1)S(1)}, bf16[6,64,1472]{2,1,0:T(8,128)(2,1)}, u32[]{:S(2)}, u32[]{:S(2)}) %collective-permute-start.5) | collective-permute-done | bytes 1130528 | tf_op jit(solution)/shard_map/ppermute | solution.py:524
  62.8 29.6 %collective-permute-done.8 = bf16[12,64,1472]{2,1,0:T(8,128)(2,1)S(1)} collective-permute-done((bf16[12,64,1472]{2,1,0:T(8,128)(2,1)S(1)}, bf16[12,64,1472]{2,1,0:T(8,128)(2,1)S(1)}, u32[]{:S(2)}, u32[]{:S(2)}) %collective-permute-start.8) | collective-permute-done | bytes 2261024 | tf_op jit(solution)/shard_map/ppermute | solution.py:524
  98.5 3.4 collective-permute-done.13
  104.1 4.7 %shard_map.340 = (bf16[288,768]{1,0:T(8,128)(2,1)S(1)}, bf16[288,768]{1,0:T(8,128)(2,1)S(1)}) custom-call(bf16[288,1472]{1,0:T(8,128)(2,1)S(1)} %copy-done.21, bf16[288,1472]{1,0:T(8,128)(2,1)S(1)} %collective-permute-done.9.peer_ref.mem_peer_ref, bf16[768,1472]{1,0:T(8,128)(2,1)S(1)} %get-tuple-element.205.w0_ref, bf16[768,1472]{1,0:T(8,128)(2,1)S(1)} %bitcast.85, ...), custom_call_target="tpu_custom_call" | custom-call | flops 5000000000 | bytes 1 | tf_op jit(solution)/shard_map/pallas_call | solution.py:70
  108.8 5.5 %shard_map.339 = (f32[192,1472]{1,0:T(8,128)S(1)}, bf16[192,1472]{1,0:T(8,128)(2,1)S(1)}, bf16[192,1152]{1,0:T(8,128)(2,1)S(1)}, bf16[192,384]{1,0:T(8,128)(2,1)S(1)}) custom-call(bf16[192,1472]{1,0:T(8,128)(2,1)S(1)} %copy-done.26, bf16[192,1472]{1,0:T(8,128)(2,1)S(1)} %get-tuple-element.268.n1_ref, f32[3,1472]{1,0:T(4,128)S(1)} %copy-done.33, ...), custom_call_target="tpu_custom_call" | custom-call | flops 5000000000 | bytes 1 | tf_op jit(solution)/shard_map/pallas_call | solution.py:70
  114.5 6.8 %shard_map.341 = (f32[192,1472]{1,0:T(8,128)S(1)}, bf16[192,1472]{1,0:T(8,128)(2,1)S(1)}, bf16[192,384]{1,0:T(8,128)(2,1)S(1)}, bf16[192,384]{1,0:T(8,128)(2,1)S(1)}) custom-call(f32[192,1472]{1,0:T(8,128)S(1)} %get-tuple-element.203.x_ref.x2_ref, bf16[192,1472]{1,0:T(8,128)(2,1)S(1)} %get-tuple-element.204.n_ref.n2_ref, f32[3,1472]{1,0:T(4,128)S(1)} %copy-done.33, ...), custom_call_target="tpu_custom_call" | custom-call | flops 5000000000 | bytes 1 | tf_op jit(solution)/shard_map/pallas_call | solution.py:70
  121.3 3.6 %collective-permute-done.15 = bf16[6,64,1472]{2,1,0:T(8,128)(2,1)S(1)} collective-permute-done((bf16[6,64,1472]{2,1,0:T(8,128)(2,1)S(1)}, bf16[6,64,1472]{2,1,0:T(8,128)(2,1)S(1)}, u32[]{:S(2)}, u32[]{:S(2)}) %collective-permute-start.15) | collective-permute-done | bytes 1130528 | tf_op jit(solution)/shard_map/ppermute | solution.py:524
  127.9 7.2 %collective-permute-done.19 = bf16[192,1472]{1,0:T(8,128)(2,1)S(1)} collective-permute-done((bf16[192,1472]{1,0:T(8,128)(2,1)S(1)}, bf16[192,1472]{1,0:T(8,128)(2,1)S(1)}, u32[]{:S(2)}, u32[]{:S(2)}) %collective-permute-start.19) | collective-permute-done | bytes 565280 | tf_op jit(solution)/shard_map/ppermute | solution.py:524
  138.1 13.4 %collective-permute-done.21 = bf16[6,64,1472]{2,1,0:T(8,128)(2,1)S(1)} collective-permute-done((bf16[6,64,1472]{2,1,0:T(8,128)(2,1)S(1)}, bf16[6,64,1472]{2,1,0:T(8,128)(2,1)S(1)}, u32[]{:S(2)}, u32[]{:S(2)}) %collective-permute-start.21) | collective-permute-done | bytes 1130528 | tf_op jit(solution)/shard_map/ppermute | solution.py:524
  151.8 5.2 %shard_map.344 = (bf16[768,448]{1,0:T(8,128)(2,1)S(1)}, bf16[768,448]{1,0:T(8,128)(2,1)S(1)}, bf16[768,448]{1,0:T(8,128)(2,1)S(1)}, bf16[768,1472]{1,0:T(8,128)(2,1)S(1)}) custom-call(bf16[768,1472]{1,0:T(8,128)(2,1)S(1)} %pad_maximum_fusion.4.n_ref.n0_ref, f32[768,448]{1,0:T(8,128)S(1)} %shard_map.342.gh_ref, ...), custom_call_target="tpu_custom_call" | custom-call | flops 5000000000 | bytes 1 | tf_op jit(solution)/shard_map/pallas_call | solution.py:70
  157.1 5.2 %shard_map.345 = (bf16[768,448]{1,0:T(8,128)(2,1)S(1)}, bf16[768,448]{1,0:T(8,128)(2,1)S(1)}, bf16[768,448]{1,0:T(8,128)(2,1)S(1)}, bf16[768,1472]{1,0:T(8,128)(2,1)S(1)}) custom-call(bf16[768,1472]{1,0:T(8,128)(2,1)S(1)} %bitcast.93, f32[768,448]{1,0:T(8,128)S(1)} %shard_map.343.gh_ref, bf16[112,1472]{1,0:T(8,128)(2,1)S(1)} %get-tuple-element.232.refs_0_, ...), custom_call_target="tpu_custom_call" | custom-call | flops 5000000000 | bytes 1 | tf_op jit(solution)/shard_map/pallas_call | solution.py:70
  169.1 6.6 %shard_map.347 = (bf16[448,1472]{1,0:T(8,128)(2,1)S(1)}, bf16[448,1472]{1,0:T(8,128)(2,1)S(1)}, bf16[448,1472]{1,0:T(8,128)(2,1)S(1)}) custom-call(bf16[768,448]{1,0:T(8,128)(2,1)S(1)} %get-tuple-element.260.h0_ref.h_ref, bf16[768,448]{1,0:T(8,128)(2,1)S(1)} %get-tuple-element.256.h_ref.h1_ref, bf16[768,448]{1,0:T(8,128)(2,1)S(1)} %get-tuple-element.261.g0_ref, ...), custom_call_target="tpu_custom_call" | custom-call | flops 5000000000 | bytes 1 | tf_op jit(solution)/shard_map/pallas_call | solution.py:70
  175.7 14.6 %collective-permute-done.25 = bf16[6,64,1472]{2,1,0:T(8,128)(2,1)S(1)} collective-permute-done((bf16[6,64,1472]{2,1,0:T(8,128)(2,1)S(1)}, bf16[6,64,1472]{2,1,0:T(8,128)(2,1)S(1)}, u32[]{:S(2)}, u32[]{:S(2)}) %collective-permute-start.25) | collective-permute-done | bytes 1130528 | tf_op jit(solution)/shard_map/ppermute | solution.py:524
  194.5 6.0 %collective-permute-done.27.got_ref = bf16[192,1472]{1,0:T(8,128)(2,1)S(1)} collective-permute-done((bf16[192,1472]{1,0:T(8,128)(2,1)S(1)}, bf16[192,1472]{1,0:T(8,128)(2,1)S(1)}, u32[]{:S(2)}, u32[]{:S(2)}) %collective-permute-start.27) | collective-permute-done | bytes 565280 | tf_op jit(solution)/shard_map/ppermute | solution.py:524
  200.5 9.0 %shard_map.349 = (bf16[192,1472]{1,0:T(8,128)(2,1)S(1)}, f32[192,1472]{1,0:T(8,128)S(1)}, bf16[192,384]{1,0:T(8,128)(2,1)S(1)}, bf16[288,768]{1,0:T(8,128)(2,1)S...) custom-call(bf16[768,1472]{1,0:T(8,128)(2,1)S(1)} %get-tuple-element.254.lo_ref, ...), custom_call_target="tpu_custom_call" | custom-call | flops 8000000000 | bytes 1 | tf_op jit(solution)/shard_map/pallas_call | solution.py:70
  209.7 9.5 %shard_map.351 = (f32[192,1472]{1,0:T(8,128)}, bf16[1280,192]{1,0:T(8,128)(2,1)}, f32[4,1472]{1,0:T(4,128)S(1)}) custom-call(f32[192,1472]{1,0:T(8,128)S(1)} %get-tuple-element.283.g2_ref, bf16[192,1472]{1,0:T(8,128)(2,1)S(1)} %copy-done.26, f32[3,1472]{1,0:T(4,128)S(1)} %copy-done.33, bf16[768,1472]{1,0:T(8,128)(2,1)S(1)} %get-tuple-element.197.w0_ref, ...), custom_call_target="tpu_custom_call" | custom-call | flops 8000000000 | bytes 1 | tf_op jit(solution)/shard_map/pallas_call | solution.py:70
  226.1 4.5 %all-to-all-start = ((bf16[8,160,192]{2,1,0:T(8,128)(2,1)}), bf16[8,160,192]{2,1,0:T(8,128)(2,1)}, u32[]{:S(2)}, u32[]{:S(2)}) async-start(bf16[8,160,192]{2,1,0:T(8,128)(2,1)} %bitcast.36), calls=%async_computation | async-start | bytes 1310720 | tf_op jit(solution)/shard_map/all_to_all | solution.py:547
  231.1 4.2 %collective-permute-start.35 = (bf16[112,1472]{1,0:T(8,128)(2,1)S(1)}, bf16[112,1472]{1,0:T(8,128)(2,1)}, u32[]{:S(2)}, u32[]{:S(2)}) collective-permute-start(bf16[112,1472]{1,0:T(8,128)(2,1)S(1)} %add_convert_fusion.8), channel_id=1, source_target_pairs={{0,16},{1,17},{2,18},{3,19},{4,20},{5,21},{6,22},{7,23},{8,24},{9,... | collective-permute-start | bytes 989192 | tf_op jit(solution)/shard_map/ppermute | solution.py:524
  244.0 8.0 %shard_map.350 = (bf16[1024,1472]{1,0:T(8,128)(2,1)S(1)}, bf16[1024,1472]{1,0:T(8,128)(2,1)S(1)}) custom-call(bf16[192,384]{1,0:T(8,128)(2,1)S(1)} %copy-done.59, bf16[192,384]{1,0:T(8,128)(2,1)S(1)} %copy-done.55, bf16[288,768]{1,0:T(8,128)(2,1)S(1)} %copy-done.48, bf16[288,768]{1,0:T(8,128)(2,1)S(1)} %copy-done.28, bf16[192,384]{1,0:T(8,128)(2,1)S(1)} %copy-done.57, ...), custom_call_target="tpu_custom_call" | custom-call | flops 10000000000 | bytes 1 | tf_op jit(solution)/shard_map/pallas_call | solution.py:70
  253.8 4.6 %collective-permute-start.37 = (f32[4,1472]{1,0:T(4,128)S(1)}, f32[4,1472]{1,0:T(4,128)S(1)}, u32[]{:S(2)}, u32[]{:S(2)}) collective-permute-start(f32[4,1472]{1,0:T(4,128)S(1)} %add.279), channel_id=1, source_target_pairs={{0,8},{1,9},{2,6},{3,7},{4,12},{5,13},{6,2},{7,3},{8,0},{9,1},{10,... | collective-permute-start | bytes 70664 | tf_op jit(solution)/shard_map/ppermute | solution.py:524
  262.3 3.7 %shard_map.352 = bf16[160,1472]{1,0:T(8,128)(2,1)S(1)} custom-call(s32[8]{0:T(128)S(1)} %and_select_fusion.at_ref, bf16[8,160,192]{2,1,0:T(8,128)(2,1)} %all-to-all-done.held_ref, bf16[768,1472]{1,0:T(8,128)(2,1)} %pad_maximum_fusion.5.lo_ref, bf16[768,1472]{1,0:T(8,128)(2,1)} %bitcast.38.hi_ref), custom_call_target="tpu_custom_call" | custom-call | flops 2000000000 | bytes 1 | tf_op jit(solution)/shard_map/pallas_call | solution.py:70
  271.7 4.6 %collective-permute-start.40 = (bf16[8,64,1472]{2,1,0:T(8,128)(2,1)S(1)}, bf16[8,64,1472]{2,1,0:T(8,128)(2,1)S(1)}, u32[]{:S(2)}, u32[]{:S(2)}) collective-permute-start(bf16[8,64,1472]{2,1,0:T(8,128)(2,1)S(1)} %bitcast.113), channel_id=1, source_target_pairs={{0,8},{1,9},{2,6},{3,7},{4,12},{5,13},{6,2},{7,3},{8,0},{9,1},{10,... | collective-permute-start | bytes 4521992 | tf_op jit(solution)/shard_map/ppermute | solution.py:524
  285.6 15.4 %collective-permute-done.41 = bf16[40,1472]{1,0:T(8,128)(2,1)S(1)} collective-permute-done((bf16[40,1472]{1,0:T(8,128)(2,1)S(1)}, bf16[40,1472]{1,0:T(8,128)(2,1)S(1)}, u32[]{:S(2)}, u32[]{:S(2)}) %collective-permute-start.41) | collective-permute-done | bytes 117792 | tf_op jit(solution)/shard_map/ppermute | solution.py:524
  301.1 5.8 %collective-permute-done.46 = bf16[112,1472]{1,0:T(8,128)(2,1)S(1)} collective-permute-done((bf16[112,1472]{1,0:T(8,128)(2,1)S(1)}, bf16[112,1472]{1,0:T(8,128)(2,1)S(1)}, u32[]{:S(2)}, u32[]{:S(2)}) %collective-permute-start.46) | collective-permute-done | bytes 329760 | tf_op jit(solution)/shard_map/ppermute | solution.py:524
  306.8 3.4 collective-permute-start.50
  317.3 3.4 shard_map.353
  320.8 7.6 %collective-permute-done.47 = bf16[4,64,1472]{2,1,0:T(8,128)(2,1)S(1)} collective-permute-done((bf16[4,64,1472]{2,1,0:T(8,128)(2,1)S(1)}, bf16[4,64,1472]{2,1,0:T(8,128)(2,1)S(1)}, u32[]{:S(2)}, u32[]{:S(2)}) %collective-permute-start.47) | collective-permute-done | bytes 753696 | tf_op jit(solution)/shard_map/ppermute | solution.py:524
  329.6 3.9 %collective-permute-start.53 = (bf16[64,1472]{1,0:T(8,128)(2,1)S(1)}, bf16[64,1472]{1,0:T(8,128)(2,1)S(1)}, u32[]{:S(2)}, u32[]{:S(2)}) collective-permute-start(bf16[64,1472]{1,0:T(8,128)(2,1)S(1)} %pad_maximum_fusion.11), channel_id=1, source_target_pairs={{0,17},{1,16},{2,19},{3,18},{4,21},{5,20},{6,23},{7,22},{8,25},{9,... | collective-permute-start | bytes 565256 | tf_op jit(solution)/shard_map/ppermute | solution.py:524
  335.0 3.8 %collective-permute-done.51 = bf16[64,1472]{1,0:T(8,128)(2,1)S(1)} collective-permute-done((bf16[64,1472]{1,0:T(8,128)(2,1)S(1)}, bf16[64,1472]{1,0:T(8,128)(2,1)S(1)}, u32[]{:S(2)}, u32[]{:S(2)}) %collective-permute-start.51) | collective-permute-done | bytes 188448 | tf_op jit(solution)/shard_map/ppermute | solution.py:524
  (313 shorter events, 100.7 us)
Async XLA Ops:
  3.4 25.8 %collective-permute-start.2 = (bf16[96,1472]{1,0:T(8,128)(2,1)}, bf16[96,1472]{1,0:T(8,128)(2,1)S(1)}, u32[]{:S(2)}, u32[]{:S(2)}) collective-permute-start(bf16[96,1472]{1,0:T(8,128)(2,1)} %shard_map.336.refs_0_), channel_id=1, source_target_pairs={{0,17},{1,16},{2,19},{3,18},{4,21},{5,20},{6,23},{7,22},{8,25},{9,... | collective-permute-start | bytes 847880 | tf_op jit(solution)/shard_map/ppermute | solution.py:524
  8.5 20.7 %collective-permute-start.1 = (bf16[96,1472]{1,0:T(8,128)(2,1)}, bf16[96,1472]{1,0:T(8,128)(2,1)S(1)}, u32[]{:S(2)}, u32[]{:S(2)}) collective-permute-start(bf16[96,1472]{1,0:T(8,128)(2,1)} %shard_map.336.refs_0_), channel_id=1, source_target_pairs={{0,1},{1,0},{2,3},{3,2},{4,5},{5,4},{6,7},{7,6},{8,9},{9,8},{10,11... | collective-permute-start | bytes 847880 | tf_op jit(solution)/shard_map/ppermute | solution.py:524
  9.0 25.7 %collective-permute-start = (bf16[96,1472]{1,0:T(8,128)(2,1)}, bf16[96,1472]{1,0:T(8,128)(2,1)S(1)}, u32[]{:S(2)}, u32[]{:S(2)}) collective-permute-start(bf16[96,1472]{1,0:T(8,128)(2,1)} %shard_map.336.refs_0_), channel_id=1, source_target_pairs={{0,16},{1,17},{2,18},{3,19},{4,20},{5,21},{6,22},{7,23},{8,24},{9,... | collective-permute-start | bytes 847880 | tf_op jit(solution)/shard_map/ppermute | solution.py:524
  9.1 29.0 %collective-permute-start.4 = (s32[1,288]{1,0:T(1,128)S(1)}, s32[1,288]{1,0:T(1,128)S(1)}, u32[]{:S(2)}, u32[]{:S(2)}) collective-permute-start(s32[1,288]{1,0:T(1,128)S(1)} %reshape.243.keep_ref), channel_id=1, source_target_pairs={{0,1},{1,0},{2,3},{3,2},{4,5},{5,4},{6,7},{7,6},{8,9},{9,8},{10,11... | collective-permute-start | bytes 3464 | tf_op jit(solution)/shard_map/ppermute | solution.py:524
  10.8 25.0 %collective-permute-start.3 = (bf16[192,1472]{1,0:T(8,128)(2,1)S(1)}, bf16[192,1472]{1,0:T(8,128)(2,1)}, u32[]{:S(2)}, u32[]{:S(2)}) collective-permute-start(bf16[192,1472]{1,0:T(8,128)(2,1)S(1)} %copy-done.10), channel_id=1, source_target_pairs={{0,4},{1,5},{2,10},{3,11},{4,0},{5,1},{6,14},{7,15},{8,12},{9,13},... | collective-permute-start | bytes 1695752 | tf_op jit(solution)/shard_map/ppermute | solution.py:524
  56.0 36.4 %collective-permute-start.8 = (bf16[12,64,1472]{2,1,0:T(8,128)(2,1)S(1)}, bf16[12,64,1472]{2,1,0:T(8,128)(2,1)S(1)}, u32[]{:S(2)}, u32[]{:S(2)}) collective-permute-start(bf16[12,64,1472]{2,1,0:T(8,128)(2,1)S(1)} %bitcast.100), channel_id=1, source_target_pairs={{0,8},{1,9},{2,6},{3,7},{4,12},{5,13},{6,2},{7,3},{8,0},{9,1},{10,... | collective-permute-start | bytes 6782984 | tf_op jit(solution)/shard_map/ppermute | solution.py:524
  56.9 37.0 %collective-permute-start.9 = (bf16[288,1472]{1,0:T(8,128)(2,1)S(1)}, bf16[288,1472]{1,0:T(8,128)(2,1)S(1)}, u32[]{:S(2)}, u32[]{:S(2)}) collective-permute-start(bf16[288,1472]{1,0:T(8,128)(2,1)S(1)} %copy-done.21), channel_id=1, source_target_pairs={{0,1},{1,0},{2,3},{3,2},{4,5},{5,4},{6,7},{7,6},{8,9},{9,8},{10,11... | collective-permute-start | bytes 2543624 | tf_op jit(solution)/shard_map/ppermute | solution.py:524
  57.4 36.5 %collective-permute-start.11 = (bf16[112,1472]{1,0:T(8,128)(2,1)S(1)}, bf16[112,1472]{1,0:T(8,128)(2,1)S(1)}, u32[]{:S(2)}, u32[]{:S(2)}) collective-permute-start(bf16[112,1472]{1,0:T(8,128)(2,1)S(1)} %get-tuple-element.232.refs_0_), channel_id=1, source_target_pairs={{0,1},{1,0},{2,3},{3,2},{4,5},{5,4},{6,7},{7,6},{8,9},{9,8},{10,11... | collective-permute-start | bytes 989192 | tf_op jit(solution)/shard_map/ppermute | solution.py:524
  58.9 35.0 %collective-permute-start.10 = (bf16[112,1472]{1,0:T(8,128)(2,1)S(1)}, bf16[112,1472]{1,0:T(8,128)(2,1)S(1)}, u32[]{:S(2)}, u32[]{:S(2)}) collective-permute-start(bf16[112,1472]{1,0:T(8,128)(2,1)S(1)} %get-tuple-element.232.refs_0_), channel_id=1, source_target_pairs={{0,16},{1,17},{2,18},{3,19},{4,20},{5,21},{6,22},{7,23},{8,24},{9,... | collective-permute-start | bytes 989192 | tf_op jit(solution)/shard_map/ppermute | solution.py:524
  62.1 31.8 %collective-permute-start.12 = (bf16[112,1472]{1,0:T(8,128)(2,1)S(1)}, bf16[112,1472]{1,0:T(8,128)(2,1)S(1)}, u32[]{:S(2)}, u32[]{:S(2)}) collective-permute-start(bf16[112,1472]{1,0:T(8,128)(2,1)S(1)} %collective-permute-done.6.refs_1_.refs_2_), channel_id=1, source_target_pairs={{0,1},{1,0},{2,3},{3,2},{4,5},{5,4},{6,7},{7,6},{8,9},{9,8},{10,11... | collective-permute-start | bytes 989192 | tf_op jit(solution)/shard_map/ppermute | solution.py:524
  94.5 30.6 %collective-permute-start.18 = (bf16[112,1472]{1,0:T(8,128)(2,1)S(1)}, bf16[112,1472]{1,0:T(8,128)(2,1)S(1)}, u32[]{:S(2)}, u32[]{:S(2)}) collective-permute-start(bf16[112,1472]{1,0:T(8,128)(2,1)S(1)} %get-tuple-element.236.refs_4_), channel_id=1, source_target_pairs={{0,1},{1,0},{2,3},{3,2},{4,5},{5,4},{6,7},{7,6},{8,9},{9,8},{10,11... | collective-permute-start | bytes 989192 | tf_op jit(solution)/shard_map/ppermute | solution.py:524
  95.2 29.9 %collective-permute-start.17 = (bf16[112,1472]{1,0:T(8,128)(2,1)S(1)}, bf16[112,1472]{1,0:T(8,128)(2,1)S(1)}, u32[]{:S(2)}, u32[]{:S(2)}) collective-permute-start(bf16[112,1472]{1,0:T(8,128)(2,1)S(1)} %get-tuple-element.236.refs_4_), channel_id=1, source_target_pairs={{0,16},{1,17},{2,18},{3,19},{4,20},{5,21},{6,22},{7,23},{8,24},{9,... | collective-permute-start | bytes 989192 | tf_op jit(solution)/shard_map/ppermute | solution.py:524
  101.9 23.2 %collective-permute-start.16 = (bf16[112,1472]{1,0:T(8,128)(2,1)S(1)}, bf16[112,1472]{1,0:T(8,128)(2,1)S(1)}, u32[]{:S(2)}, u32[]{:S(2)}) collective-permute-start(bf16[112,1472]{1,0:T(8,128)(2,1)S(1)} %collective-permute-done.10.refs_1_), channel_id=1, source_target_pairs={{0,1},{1,0},{2,3},{3,2},{4,5},{5,4},{6,7},{7,6},{8,9},{9,8},{10,11... | collective-permute-start | bytes 989192 | tf_op jit(solution)/shard_map/ppermute | solution.py:524
  102.6 22.2 %collective-permute-start.15 = (bf16[6,64,1472]{2,1,0:T(8,128)(2,1)S(1)}, bf16[6,64,1472]{2,1,0:T(8,128)(2,1)S(1)}, u32[]{:S(2)}, u32[]{:S(2)}) collective-permute-start(bf16[6,64,1472]{2,1,0:T(8,128)(2,1)S(1)} %bitcast.103), channel_id=1, source_target_pairs={{0,8},{1,9},{2,6},{3,7},{4,12},{5,13},{6,2},{7,3},{8,0},{9,1},{10,... | collective-permute-start | bytes 3391496 | tf_op jit(solution)/shard_map/ppermute | solution.py:524
  167.0 23.2 %collective-permute-start.26 = (bf16[12,64,1472]{2,1,0:T(8,128)(2,1)}, bf16[12,64,1472]{2,1,0:T(8,128)(2,1)S(1)}, u32[]{:S(2)}, u32[]{:S(2)}) collective-permute-start(bf16[12,64,1472]{2,1,0:T(8,128)(2,1)} %bitcast.32), channel_id=1, source_target_pairs={{0,2},{1,3},{2,0},{3,1},{4,6},{5,7},{6,4},{7,5},{8,10},{9,11},{10,... | collective-permute-start | bytes 6782984 | tf_op jit(solution)/shard_map/ppermute | solution.py:524
  167.7 22.6 %collective-permute-start.25 = (bf16[6,64,1472]{2,1,0:T(8,128)(2,1)S(1)}, bf16[6,64,1472]{2,1,0:T(8,128)(2,1)S(1)}, u32[]{:S(2)}, u32[]{:S(2)}) collective-permute-start(bf16[6,64,1472]{2,1,0:T(8,128)(2,1)S(1)} %bitcast.117), channel_id=1, source_target_pairs={{0,8},{1,9},{2,6},{3,7},{4,12},{5,13},{6,2},{7,3},{8,0},{9,1},{10,... | collective-permute-start | bytes 3391496 | tf_op jit(solution)/shard_map/ppermute | solution.py:524
  167.8 23.7 %collective-permute-start.28 = (bf16[192,1472]{1,0:T(8,128)(2,1)S(1)}, bf16[192,1472]{1,0:T(8,128)(2,1)S(1)}, u32[]{:S(2)}, u32[]{:S(2)}) collective-permute-start(bf16[192,1472]{1,0:T(8,128)(2,1)S(1)} %get-tuple-element.268.n1_ref), channel_id=1, source_target_pairs={{0,4},{1,5},{2,10},{3,11},{4,0},{5,1},{6,14},{7,15},{8,12},{9,13},... | collective-permute-start | bytes 1695752 | tf_op jit(solution)/shard_map/ppermute | solution.py:524
  191.7 17.9 %collective-permute-start.29 = (bf16[224,1472]{1,0:T(8,128)(2,1)S(1)}, bf16[224,1472]{1,0:T(8,128)(2,1)S(1)}, u32[]{:S(2)}, u32[]{:S(2)}) collective-permute-start(bf16[224,1472]{1,0:T(8,128)(2,1)S(1)} %slice.288), channel_id=1, source_target_pairs={{0,1},{1,0},{2,3},{3,2},{4,5},{5,4},{6,7},{7,6},{8,9},{9,8},{10,11... | collective-permute-start | bytes 1978376 | tf_op jit(solution)/shard_map/ppermute | solution.py:524
  200.4 18.7 %collective-permute-start.30 = (bf16[6,64,1472]{2,1,0:T(8,128)(2,1)S(1)}, bf16[6,64,1472]{2,1,0:T(8,128)(2,1)S(1)}, u32[]{:S(2)}, u32[]{:S(2)}) collective-permute-start(bf16[6,64,1472]{2,1,0:T(8,128)(2,1)S(1)} %bitcast.104), channel_id=1, source_target_pairs={{0,8},{1,9},{2,6},{3,7},{4,12},{5,13},{6,2},{7,3},{8,0},{9,1},{10,... | collective-permute-start | bytes 3391496 | tf_op jit(solution)/shard_map/ppermute | solution.py:524
  220.8 32.9 %collective-permute-start.32 = (bf16[12,64,1472]{2,1,0:T(8,128)(2,1)}, bf16[12,64,1472]{2,1,0:T(8,128)(2,1)}, u32[]{:S(2)}, u32[]{:S(2)}) collective-permute-start(bf16[12,64,1472]{2,1,0:T(8,128)(2,1)} %bitcast.37), channel_id=1, source_target_pairs={{0,2},{1,3},{2,0},{3,1},{4,6},{5,7},{6,4},{7,5},{8,10},{9,11},{10,... | collective-permute-start | bytes 6782984 | tf_op jit(solution)/shard_map/ppermute | solution.py:524
  221.9 31.8 %collective-permute-start.34 = (bf16[6,64,1472]{2,1,0:T(8,128)(2,1)}, bf16[6,64,1472]{2,1,0:T(8,128)(2,1)}, u32[]{:S(2)}, u32[]{:S(2)}) collective-permute-start(bf16[6,64,1472]{2,1,0:T(8,128)(2,1)} %bitcast.39), channel_id=1, source_target_pairs={{0,8},{1,9},{2,6},{3,7},{4,12},{5,13},{6,2},{7,3},{8,0},{9,1},{10,... | collective-permute-start | bytes 3391496 | tf_op jit(solution)/shard_map/ppermute | solution.py:524
  224.8 28.9 %collective-permute-start.33 = (bf16[224,1472]{1,0:T(8,128)(2,1)}, bf16[224,1472]{1,0:T(8,128)(2,1)}, u32[]{:S(2)}, u32[]{:S(2)}) collective-permute-start(bf16[224,1472]{1,0:T(8,128)(2,1)} %slice.290), channel_id=1, source_target_pairs={{0,1},{1,0},{2,3},{3,2},{4,5},{5,4},{6,7},{7,6},{8,9},{9,8},{10,11... | collective-permute-start | bytes 1978376 | tf_op jit(solution)/shard_map/ppermute | solution.py:524
  226.1 27.6 %all-to-all-start = ((bf16[8,160,192]{2,1,0:T(8,128)(2,1)}), bf16[8,160,192]{2,1,0:T(8,128)(2,1)}, u32[]{:S(2)}, u32[]{:S(2)}) async-start(bf16[8,160,192]{2,1,0:T(8,128)(2,1)} %bitcast.36), calls=%async_computation | async-start | bytes 1310720 | tf_op jit(solution)/shard_map/all_to_all | solution.py:547
  230.6 21.4 %collective-permute-start.31 = (f32[4,1472]{1,0:T(4,128)S(1)}, f32[4,1472]{1,0:T(4,128)S(1)}, u32[]{:S(2)}, u32[]{:S(2)}) collective-permute-start(f32[4,1472]{1,0:T(4,128)S(1)} %get-tuple-element.296), channel_id=1, source_target_pairs={{0,2},{1,3},{2,0},{3,1},{4,6},{5,7},{6,4},{7,5},{8,10},{9,11},{10,... | collective-permute-start | bytes 70664 | tf_op jit(solution)/shard_map/ppermute | solution.py:524
  231.1 22.6 %collective-permute-start.35 = (bf16[112,1472]{1,0:T(8,128)(2,1)S(1)}, bf16[112,1472]{1,0:T(8,128)(2,1)}, u32[]{:S(2)}, u32[]{:S(2)}) collective-permute-start(bf16[112,1472]{1,0:T(8,128)(2,1)S(1)} %add_convert_fusion.8), channel_id=1, source_target_pairs={{0,16},{1,17},{2,18},{3,19},{4,20},{5,21},{6,22},{7,23},{8,24},{9,... | collective-permute-start | bytes 989192 | tf_op jit(solution)/shard_map/ppermute | solution.py:524
  253.7 17.5 %collective-permute-start.36 = (bf16[16,64,1472]{2,1,0:T(8,128)(2,1)}, bf16[16,64,1472]{2,1,0:T(8,128)(2,1)S(1)}, u32[]{:S(2)}, u32[]{:S(2)}) collective-permute-start(bf16[16,64,1472]{2,1,0:T(8,128)(2,1)} %bitcast.84), channel_id=1, source_target_pairs={{0,2},{1,3},{2,0},{3,1},{4,6},{5,7},{6,4},{7,5},{8,10},{9,11},{10,... | collective-permute-start | bytes 9043976 | tf_op jit(solution)/shard_map/ppermute | solution.py:524
  266.3 19.3 %collective-permute-start.42 = (bf16[40,1472]{1,0:T(8,128)(2,1)S(1)}, bf16[40,1472]{1,0:T(8,128)(2,1)S(1)}, u32[]{:S(2)}, u32[]{:S(2)}) collective-permute-start(bf16[40,1472]{1,0:T(8,128)(2,1)S(1)} %get-tuple-element.386), channel_id=1, source_target_pairs={{0,1},{1,0},{2,3},{3,2},{4,5},{5,4},{6,7},{7,6},{8,9},{9,8},{10,11... | collective-permute-start | bytes 353288 | tf_op jit(solution)/shard_map/ppermute | solution.py:524
  267.9 33.1 %collective-permute-start.45 = (bf16[224,1472]{1,0:T(8,128)(2,1)S(1)}, bf16[224,1472]{1,0:T(8,128)(2,1)S(1)}, u32[]{:S(2)}, u32[]{:S(2)}) collective-permute-start(bf16[224,1472]{1,0:T(8,128)(2,1)S(1)} %slice.300), channel_id=1, source_target_pairs={{0,1},{1,0},{2,3},{3,2},{4,5},{5,4},{6,7},{7,6},{8,9},{9,8},{10,11... | collective-permute-start | bytes 1978376 | tf_op jit(solution)/shard_map/ppermute | solution.py:524
  271.7 35.2 %collective-permute-start.40 = (bf16[8,64,1472]{2,1,0:T(8,128)(2,1)S(1)}, bf16[8,64,1472]{2,1,0:T(8,128)(2,1)S(1)}, u32[]{:S(2)}, u32[]{:S(2)}) collective-permute-start(bf16[8,64,1472]{2,1,0:T(8,128)(2,1)S(1)} %bitcast.113), channel_id=1, source_target_pairs={{0,8},{1,9},{2,6},{3,7},{4,12},{5,13},{6,2},{7,3},{8,0},{9,1},{10,... | collective-permute-start | bytes 4521992 | tf_op jit(solution)/shard_map/ppermute | solution.py:524
  280.3 20.8 %collective-permute-start.41 = (bf16[40,1472]{1,0:T(8,128)(2,1)S(1)}, bf16[40,1472]{1,0:T(8,128)(2,1)S(1)}, u32[]{:S(2)}, u32[]{:S(2)}) collective-permute-start(bf16[40,1472]{1,0:T(8,128)(2,1)S(1)} %get-tuple-element.387), channel_id=1, source_target_pairs={{0,16},{1,17},{2,18},{3,19},{4,20},{5,21},{6,22},{7,23},{8,24},{9,... | collective-permute-start | bytes 353288 | tf_op jit(solution)/shard_map/ppermute | solution.py:524
  282.5 24.3 %collective-permute-start.46 = (bf16[112,1472]{1,0:T(8,128)(2,1)S(1)}, bf16[112,1472]{1,0:T(8,128)(2,1)S(1)}, u32[]{:S(2)}, u32[]{:S(2)}) collective-permute-start(bf16[112,1472]{1,0:T(8,128)(2,1)S(1)} %add_convert_fusion.7), channel_id=1, source_target_pairs={{0,16},{1,17},{2,18},{3,19},{4,20},{5,21},{6,22},{7,23},{8,24},{9,... | collective-permute-start | bytes 989192 | tf_op jit(solution)/shard_map/ppermute | solution.py:524
  313.1 21.9 %collective-permute-start.54 = (bf16[112,1472]{1,0:T(8,128)(2,1)S(1)}, bf16[112,1472]{1,0:T(8,128)(2,1)S(1)}, u32[]{:S(2)}, u32[]{:S(2)}) collective-permute-start(bf16[112,1472]{1,0:T(8,128)(2,1)S(1)} %add_convert_fusion.6), channel_id=1, source_target_pairs={{0,16},{1,17},{2,18},{3,19},{4,20},{5,21},{6,22},{7,23},{8,24},{9,... | collective-permute-start | bytes 989192 | tf_op jit(solution)/shard_map/ppermute | solution.py:524
  (99 other events, 1117.6 us)
